TPU v7x, 32 devices: a whole 2x2x4 slice. The times are simulated.
32 devices in a mesh: grp: 4 (over x, core), blk: 8 (over z, y).
Axes of the slice: x: 2, y: 2, z: 4, core: 2. Of those that a mesh axis runs over, the one named last changes fastest.
Arguments:
- held: float32 [4, 3, 90, 4096], P('grp', None, None, 'blk'), may hold values from -6 to 6
- neighbours: int32 [6, 4096], P(None, 'blk'), may hold values from 0 to 767
- send_rows: int32 [2, 1024], P(None, 'blk'), may hold values from 0 to 511
- diffusion: float32 [6, 4096], P(None, 'blk'), may hold values from 0.02 to 0.12
- transport: float32 [6, 4096], P(None, 'blk'), may hold values from -0.06 to 0.06
- w_in: bfloat16 [512, 270], replicated, may hold values from -0.375 to 0.375
- b_in: float32 [512], replicated, may hold values from -3 to 3
- w_mid: bfloat16 [512, 512], replicated, may hold values from -0.25 to 0.25
- b_mid: float32 [512], replicated, may hold values from -3 to 3
- w_out: bfloat16 [90, 512], replicated, may hold values from -0.25 to 0.25
- b_out: float32 [90], replicated, may hold values from -3 to 3
Outputs:
- held_new: float32 [4, 3, 90, 4096], P('grp', None, None, 'blk')
All inputs are finite; a program needn't handle non-finite values.
Results may differ from a plain program's by a relative error of at most 0.0017.
Values may be sent and summed in bfloat16 or wider, within the bound.
No kernel may reach another device: no remote copies, remote signals or barrier semaphores. Data moves between devices by JAX's collectives and lax.ppermute only.
A program may use at most 64 MiB of HBM per device.

v0:
```python
import jax
import jax.numpy as jnp
from jax import lax
from jax.sharding import PartitionSpec as P

heat_gain = 0.5


def extended(array, sides, width):
    for axis, dim in sides:
        peers, length = (lax.axis_size(axis), array.shape[dim])
        up = [(i, (i + 1) % peers) for i in range(peers)]
        down = [(j, i) for i, j in up]
        last = lax.slice_in_dim(array, length - width, length, axis=dim)
        first = lax.slice_in_dim(array, 0, width, axis=dim)
        before = lax.ppermute(last, axis, up)
        after = lax.ppermute(first, axis, down)
        array = jnp.concatenate([before, array, after], axis=dim)
    return array


def passed_along(array, axis, by):
    peers = lax.axis_size(axis)
    pairs = [(i, i + by) for i in range(peers) if 0 <= i + by < peers]
    return lax.ppermute(array, axis, pairs)


def network(feats, w_in, b_in, w_mid, b_mid, w_out, b_out):
    first = (
        jnp.einsum("hf,...fn->...hn", w_in, feats, preferred_element_type=jnp.float32)
        + b_in[:, None]
    )
    first = jax.nn.silu(first).astype(jnp.bfloat16)
    second = (
        jnp.einsum("gh,...hn->...gn", w_mid, first, preferred_element_type=jnp.float32)
        + b_mid[:, None]
    )
    second = jax.nn.silu(second).astype(jnp.bfloat16)
    return (
        jnp.einsum("lh,...hn->...ln", w_out, second, preferred_element_type=jnp.float32)
        + b_out[:, None]
    )


def advance(field, heat, neighbours, send_rows, diffusion, transport, is_radiation):
    halo_cells = send_rows.shape[1]
    sent = field[:, :, send_rows.reshape(-1)]
    padded = extended(sent, (("blk", 2),), halo_cells)
    ext = jnp.concatenate(
        (field, padded[:, :, :halo_cells], padded[:, :, 3 * halo_cells :]), axis=2
    )

    def sweep(values):
        total = jnp.zeros_like(values)
        for edge in range(6):
            near = ext[:, :, neighbours[edge]]
            total = (
                total + diffusion[edge] * (near - values) - 0.5 * transport[edge] * (near + values)
            )
        moved = values + total
        return moved.at[0].add(heat_gain * heat)

    return lax.cond(is_radiation, lambda values: values, sweep, field)


def gather_back(slots, quarter, group_slot):
    result = jnp.zeros(slots.shape[1:], jnp.float32)
    for index in range(3):
        piece = passed_along(slots[index], "grp", (index + 1) * quarter)
        result = jnp.where(group_slot == index + 1, piece, result)
    return result


def body(held, neighbours, send_rows, diffusion, transport, w_in, b_in, w_mid, b_mid, w_out, b_out):
    quarter = lax.axis_size("grp") // 4
    group_slot = lax.axis_index("grp") // quarter
    is_radiation = group_slot == 0
    weights = (w_in, b_in, w_mid, b_mid, w_out, b_out)
    local = held[0]
    fields, levels, cells = local.shape

    def near_heat(feats):
        return lax.cond(
            is_radiation,
            lambda x: jnp.zeros((levels, x.shape[1]), jnp.float32),
            lambda x: network(x, *weights),
            feats,
        )

    feats0 = local.reshape(fields * levels, cells).astype(jnp.bfloat16)
    heat0 = gather_back(local, quarter, group_slot)
    heat1 = near_heat(feats0)
    state1 = advance(local, heat0, neighbours, send_rows, diffusion, transport, is_radiation)
    state2 = advance(state1, heat1, neighbours, send_rows, diffusion, transport, is_radiation)
    feats1 = state1.reshape(fields * levels, cells).astype(jnp.bfloat16)
    heat2 = near_heat(feats1)
    given = []
    for index in range(3):
        given.append(passed_along(heat2, "grp", -(index + 1) * quarter))
    radiat_out = jnp.stack(given)
    return jnp.where(is_radiation, radiat_out, state2)[None]


def solution(mesh):
    placed = (
        P("grp", None, None, "blk"),
        P(None, "blk"),
        P(None, "blk"),
        P(None, "blk"),
        P(None, "blk"),
        P(),
        P(),
        P(),
        P(),
        P(),
        P(),
    )
    return jax.shard_map(
        body, mesh=mesh, in_specs=placed, out_specs=P("grp", None, None, "blk"), check_vma=False
    )
```

profile of v0, /device:TPU:3, one launch (start us, length us, event | category | flops | bytes accessed | tf_op | source)
XLA Modules:
  0.0 106.6 jit_solution(16450834777608772617)
XLA Ops:
  0.0 2.4 %copy.46 = f32[1,3,90,512]{2,1,3,0:T(4,128)S(1)} copy(f32[1,3,90,512]{3,0,2,1:T(1,128)} %param.23) | data formatting | bytes 1105920 | tf_op args[0]
  2.4 1.0 gather_fusion.12
  3.4 0.1 fusion.65
  3.5 1.3 %collective-permute-start = (f32[3,90,128]{1,0,2:T(4,128)S(1)}, f32[3,90,128]{1,0,2:T(4,128)S(1)}, u32[]{:S(2)}, u32[]{:S(2)}) collective-permute-start(f32[3,90,128]{1,0,2:T(4,128)S(1)} %get-tuple-element.278), channel_id=1, source_target_pairs={{0,1},{1,2},{2,3},{3,4},{4,5},{5,6},{6,7},{7,0},{8,9},{9,10},{10,1... | collective-permute-start | bytes 414728 | tf_op jit(solution)/shard_map/ppermute | solution.py:16
  4.8 3.1 %collective-permute-start.1 = (f32[3,90,128]{1,0,2:T(4,128)S(1)}, f32[3,90,128]{1,0,2:T(4,128)}, u32[]{:S(2)}, u32[]{:S(2)}) collective-permute-start(f32[3,90,128]{1,0,2:T(4,128)S(1)} %get-tuple-element.279), channel_id=1, source_target_pairs={{1,0},{2,1},{3,2},{4,3},{5,4},{6,5},{7,6},{0,7},{9,8},{10,9},{11,1... | collective-permute-start | bytes 414728 | tf_op jit(solution)/shard_map/ppermute | solution.py:17
  8.0 1.3 %collective-permute-start.2 = (f32[90,512]{1,0:T(8,128)S(1)}, f32[90,512]{1,0:T(8,128)}, u32[]{:S(2)}, u32[]{:S(2)}) collective-permute-start(f32[90,512]{1,0:T(8,128)S(1)} %get-tuple-element.275), channel_id=1, source_target_pairs={{0,24},{1,25},{2,26},{3,27},{4,28},{5,29},{6,30},{7,31}} | collective-permute-start | bytes 552968 | tf_op jit(solution)/shard_map/ppermute | solution.py:25
  9.3 1.3 %collective-permute-start.3 = (f32[90,512]{1,0:T(8,128)S(1)}, f32[90,512]{1,0:T(8,128)}, u32[]{:S(2)}, u32[]{:S(2)}) collective-permute-start(f32[90,512]{1,0:T(8,128)S(1)} %get-tuple-element.274), channel_id=1, source_target_pairs={{0,16},{8,24},{1,17},{9,25},{2,18},{10,26},{3,19},{11,27},{4,20},{... | collective-permute-start | bytes 552968 | tf_op jit(solution)/shard_map/ppermute | solution.py:25
  10.6 1.3 %collective-permute-start.4 = (f32[90,512]{1,0:T(8,128)S(1)}, f32[90,512]{1,0:T(8,128)}, u32[]{:S(2)}, u32[]{:S(2)}) collective-permute-start(f32[90,512]{1,0:T(8,128)S(1)} %get-tuple-element.273), channel_id=1, source_target_pairs={{0,8},{8,16},{16,24},{1,9},{9,17},{17,25},{2,10},{10,18},{18,26},{... | collective-permute-start | bytes 552968 | tf_op jit(solution)/shard_map/ppermute | solution.py:25
  11.9 0.0 copy-start.9
  12.0 3.4 %collective-permute-done = f32[3,90,128]{1,0,2:T(4,128)S(1)} collective-permute-done((f32[3,90,128]{1,0,2:T(4,128)S(1)}, f32[3,90,128]{1,0,2:T(4,128)S(1)}, u32[]{:S(2)}, u32[]{:S(2)}) %collective-permute-start) | collective-permute-done | bytes 138272 | tf_op jit(solution)/shard_map/ppermute | solution.py:16
  15.4 2.0 %collective-permute-done.1 = f32[3,90,128]{1,0,2:T(4,128)} collective-permute-done((f32[3,90,128]{1,0,2:T(4,128)S(1)}, f32[3,90,128]{1,0,2:T(4,128)}, u32[]{:S(2)}, u32[]{:S(2)}) %collective-permute-start.1) | collective-permute-done | bytes 138272 | tf_op jit(solution)/shard_map/ppermute | solution.py:17
  17.4 1.4 %pad_maximum_fusion = f32[3,90,768]{1,0,2:T(4,128)S(1)} fusion(f32[3,90,128]{1,0,2:T(4,128)} %collective-permute-done.1, f32[3,90,128]{1,0,2:T(4,128)S(1)} %collective-permute-done, f32[3,90,512]{1,0,2:T(4,128)S(1)} %bitcast.281), kind=kLoop, calls=%fused_computation.149 | loop fusion | flops 414720 | bytes 1658880 | tf_op jit(solution)/shard_map/concatenate | solution.py:49
  18.8 34.6 %conditional.4 = (f32[3,90,512]{2,1,0:T(8,128)S(1)}) conditional(s32[]{:T(128)} %convert_element_type.30, (f32[6,512]{1,0:T(8,128)S(1)}, s32[6,512]{1,0:T(8,128)S(1)}, f32[3,90,768]{1,0,2:T(4,128)S(1)}, f32[3,90,512]{1,0,2:T(4,128)S(1)}, f32[6,512]{1,0:T(8,128)S(1)}, /*index=5*/s32[]{:T(128)}, f32[90,512]{1,0:T(8,128)}, s32[]{:T(128)}, ...), branch_computations={%region_0.1_spmd.clone, %region_1.2_spmd} | conditional | flops 5225475 | bytes 26529912 | solution.py:63
  18.9 2.7 %gather_fusion.6 = f32[512,3,90]{2,1,0:T(4,128)} fusion(f32[3,90,768]{1,0,2:T(4,128)S(1)} %get-tuple-element.144, s32[1024]{0:T(1024)S(1)} %pad_clamp_fusion.11), kind=kCustom, calls=%fused_computation.6 | custom fusion | bytes 1107968 | tf_op jit(solution)/shard_map/cond/branch_0_fun/gather | solution.py:56
  21.6 2.3 %copy.40 = f32[512,3,90]{0,2,1:T(8,128)} copy(f32[512,3,90]{2,1,0:T(4,128)} %gather_fusion.6) | data formatting | bytes 1105920 | tf_op jit(solution)/shard_map/cond/branch_0_fun/gather | solution.py:56
  23.9 2.6 %gather_fusion.7 = f32[512,3,90]{2,1,0:T(4,128)} fusion(f32[3,90,768]{1,0,2:T(4,128)S(1)} %get-tuple-element.144, s32[1024]{0:T(1024)S(1)} %pad_clamp_fusion.10), kind=kCustom, calls=%fused_computation.7 | custom fusion | bytes 1107968 | tf_op jit(solution)/shard_map/cond/branch_0_fun/gather | solution.py:56
  26.6 2.3 %copy.41 = f32[512,3,90]{0,2,1:T(8,128)} copy(f32[512,3,90]{2,1,0:T(4,128)} %gather_fusion.7) | data formatting | bytes 1105920 | tf_op jit(solution)/shard_map/cond/branch_0_fun/gather | solution.py:56
  28.9 2.6 %gather_fusion.8 = f32[512,3,90]{2,1,0:T(4,128)} fusion(f32[3,90,768]{1,0,2:T(4,128)S(1)} %get-tuple-element.144, s32[1024]{0:T(1024)S(1)} %pad_clamp_fusion.9), kind=kCustom, calls=%fused_computation.8 | custom fusion | bytes 1107968 | tf_op jit(solution)/shard_map/cond/branch_0_fun/gather | solution.py:56
  31.6 2.3 %copy.42 = f32[512,3,90]{0,2,1:T(8,128)} copy(f32[512,3,90]{2,1,0:T(4,128)} %gather_fusion.8) | data formatting | bytes 1105920 | tf_op jit(solution)/shard_map/cond/branch_0_fun/gather | solution.py:56
  33.9 2.6 %gather_fusion.9 = f32[512,3,90]{2,1,0:T(4,128)} fusion(f32[3,90,768]{1,0,2:T(4,128)S(1)} %get-tuple-element.144, s32[1024]{0:T(1024)S(1)} %pad_clamp_fusion.8), kind=kCustom, calls=%fused_computation.9 | custom fusion | bytes 1107968 | tf_op jit(solution)/shard_map/cond/branch_0_fun/gather | solution.py:56
  36.5 2.3 %copy.43 = f32[512,3,90]{0,2,1:T(8,128)} copy(f32[512,3,90]{2,1,0:T(4,128)} %gather_fusion.9) | data formatting | bytes 1105920 | tf_op jit(solution)/shard_map/cond/branch_0_fun/gather | solution.py:56
  38.9 2.6 %gather_fusion.10 = f32[512,3,90]{2,1,0:T(4,128)} fusion(f32[3,90,768]{1,0,2:T(4,128)S(1)} %get-tuple-element.144, s32[1024]{0:T(1024)S(1)} %pad_clamp_fusion.7), kind=kCustom, calls=%fused_computation.10 | custom fusion | bytes 1107968 | tf_op jit(solution)/shard_map/cond/branch_0_fun/gather | solution.py:56
  41.5 2.3 %copy.44 = f32[512,3,90]{0,2,1:T(8,128)} copy(f32[512,3,90]{2,1,0:T(4,128)} %gather_fusion.10) | data formatting | bytes 1105920 | tf_op jit(solution)/shard_map/cond/branch_0_fun/gather | solution.py:56
  43.9 2.6 %gather_fusion.11 = f32[512,3,90]{2,1,0:T(4,128)} fusion(f32[3,90,768]{1,0,2:T(4,128)S(1)} %get-tuple-element.144, s32[1024]{0:T(1024)S(1)} %pad_clamp_fusion.6), kind=kCustom, calls=%fused_computation.11 | custom fusion | bytes 1107968 | tf_op jit(solution)/shard_map/cond/branch_0_fun/gather | solution.py:56
  46.5 2.5 %copy.45 = f32[512,3,90]{0,2,1:T(8,128)} copy(f32[512,3,90]{2,1,0:T(4,128)} %gather_fusion.11) | data formatting | bytes 1105920 | tf_op jit(solution)/shard_map/cond/branch_0_fun/gather | solution.py:56
  49.0 1.1 %copy.50 = f32[3,90,512]{2,1,0:T(8,128)} copy(f32[3,90,512]{1,0,2:T(4,128)S(1)} %get-tuple-element.201) | data formatting | bytes 1105920 | tf_op jit(solution)/shard_map
  50.1 2.3 %fusion.37 = f32[3,90,512]{2,1,0:T(8,128)S(1)} fusion(f32[3,90,512]{2,1,0:T(8,128)} %copy.50, f32[512,3,90]{0,2,1:T(8,128)} %copy.45, f32[512,3,90]{0,2,1:T(8,128)} %copy.44, f32[512,3,90]{0,2,1:T(8,128)} %copy.43, f32[512,3,90]{0,2,1:T(8,128)S(1)} %copy-done.6, f32[512,3,90]{0,2,1:T(8,128)S(1)} %copy-done.4, f32[512,3,90]{0,2,1:T(8,128)S(1)} %copy-done.2, ...), kind=kLoop, calls=%fused_computation.94 | loop fusion | flops 4976640 | bytes 4448256 | tf_op jit(solution)/shard_map/cond/branch_0_fun/add | solution.py:60
  52.4 1.0 fusion.59
  53.5 0.4 copy.54
  54.0 1.0 gather_fusion.13
  55.0 0.8 fusion.64
  55.7 0.3 collective-permute-start.8
  56.1 3.8 %collective-permute-start.9 = (f32[3,90,128]{1,0,2:T(4,128)S(1)}, f32[3,90,128]{1,0,2:T(4,128)}, u32[]{:S(2)}, u32[]{:S(2)}) collective-permute-start(f32[3,90,128]{1,0,2:T(4,128)S(1)} %get-tuple-element.277), channel_id=1, source_target_pairs={{1,0},{2,1},{3,2},{4,3},{5,4},{6,5},{7,6},{0,7},{9,8},{10,9},{11,1... | collective-permute-start | bytes 414728 | tf_op jit(solution)/shard_map/ppermute | solution.py:17
  60.0 5.2 %conditional.5 = (f32[90,512]{1,0:T(8,128)}) conditional(s32[]{:T(128)} %convert_element_type.30, (bf16[512,270]{0,1:T(8,128)(2,1)}, bf16[3,90,512]{2,1,0:T(8,128)(2,1)S(1)}, f32[512]{0:T(512)S(1)}, bf16[512,512]{1,0:T(8,128)(2,1)}, f32[512]{0:T(512)S(1)}, /*index=5*/bf16[90,512]{1,0:T(8,128)(2,1)S(1)}, f32[90]{0:T(128)S(1)}) %tuple.137, () %tuple.39), branch_computations={%region_2.3_spmd, %region_3.4_spmd} | conditional | flops 460370944 | bytes 2959728 | solution.py:83
  60.0 0.1 convert_element_type.35
  60.1 2.4 %multiply_convert_fusion.1 = bf16[512,512]{1,0:T(8,128)(2,1)} fusion(bf16[512,270]{0,1:T(8,128)(2,1)} %get-tuple-element.209, bf16[270,512]{1,0:T(8,128)(2,1)S(1)} %convert_element_type.35, f32[512]{0:T(512)S(1)} %get-tuple-element.103), kind=kOutput, calls=%fused_computation.20 | convolution fusion | flops 143130624 | bytes 1079296 | tf_op jit(solution)/shard_map/cond/branch_0_fun/hf,...fn->...hn/dot_general | solution.py:30
  62.5 2.6 %fusion.1 = f32[90,512]{1,0:T(8,128)} fusion(bf16[90,512]{1,0:T(8,128)(2,1)S(1)} %get-tuple-element.106, bf16[512,512]{1,0:T(8,128)(2,1)} %get-tuple-element.104, bf16[512,512]{1,0:T(8,128)(2,1)} %multiply_convert_fusion.1, f32[512]{0:T(512)S(1)} %get-tuple-element.105, f32[90]{0:T(128)S(1)} %get-tuple-element.107), kind=kOutput, calls=%fused_computation.18 | convolution fusion | flops 317240320 | bytes 1327464 | tf_op jit(solution)/shard_map/cond/branch_0_fun/lh,...hn->...ln/dot_general | solution.py:40
  65.2 6.5 %collective-permute-start.5 = (f32[90,512]{1,0:T(8,128)}, f32[90,512]{1,0:T(8,128)}, u32[]{:S(2)}, u32[]{:S(2)}) collective-permute-start(f32[90,512]{1,0:T(8,128)} %get-tuple-element.281), channel_id=1, source_target_pairs={{8,0},{16,8},{24,16},{9,1},{17,9},{25,17},{10,2},{18,10},{26,18},{... | collective-permute-start | bytes 552968 | tf_op jit(solution)/shard_map/ppermute | solution.py:25
  71.6 2.0 %collective-permute-start.6 = (f32[90,512]{1,0:T(8,128)}, f32[90,512]{1,0:T(8,128)}, u32[]{:S(2)}, u32[]{:S(2)}) collective-permute-start(f32[90,512]{1,0:T(8,128)} %get-tuple-element.281), channel_id=1, source_target_pairs={{16,0},{24,8},{17,1},{25,9},{18,2},{26,10},{19,3},{27,11},{20,4},{... | collective-permute-start | bytes 552968 | tf_op jit(solution)/shard_map/ppermute | solution.py:25
  73.6 2.0 %collective-permute-start.7 = (f32[90,512]{1,0:T(8,128)}, f32[90,512]{1,0:T(8,128)}, u32[]{:S(2)}, u32[]{:S(2)}) collective-permute-start(f32[90,512]{1,0:T(8,128)} %get-tuple-element.281), channel_id=1, source_target_pairs={{24,0},{25,1},{26,2},{27,3},{28,4},{29,5},{30,6},{31,7}} | collective-permute-start | bytes 552968 | tf_op jit(solution)/shard_map/ppermute | solution.py:25
  75.6 4.5 %conditional.6 = (f32[90,512]{1,0:T(8,128)S(1)}) conditional(s32[]{:T(128)} %convert_element_type.30, (bf16[512,270]{0,1:T(8,128)(2,1)}, bf16[1,3,90,512]{3,2,1,0:T(8,128)(2,1)S(1)}, f32[512]{0:T(512)S(1)}, bf16[512,512]{1,0:T(8,128)(2,1)}, f32[512]{0:T(512)S(1)}, /*index=5*/bf16[90,512]{1,0:T(8,128)(2,1)S(1)}, f32[90]{0:T(128)S(1)}) %tuple.138, () %tuple.41), branch_computations={%region_4.5_spmd, %region_5.6_spmd} | conditional | flops 460370944 | bytes 5056908 | solution.py:83
  75.8 0.1 convert_element_type.36
  75.9 2.4 %multiply_convert_fusion.3 = bf16[512,512]{1,0:T(8,128)(2,1)} fusion(bf16[512,270]{0,1:T(8,128)(2,1)} %get-tuple-element.216, bf16[270,512]{1,0:T(8,128)(2,1)S(1)} %convert_element_type.36, f32[512]{0:T(512)S(1)} %get-tuple-element.110), kind=kOutput, calls=%fused_computation.30 | convolution fusion | flops 143130624 | bytes 1079296 | tf_op jit(solution)/shard_map/cond/branch_0_fun/hf,...fn->...hn/dot_general | solution.py:30
  78.3 1.8 %fusion.6 = f32[90,512]{1,0:T(8,128)S(1)} fusion(bf16[90,512]{1,0:T(8,128)(2,1)S(1)} %get-tuple-element.113, bf16[512,512]{1,0:T(8,128)(2,1)S(1)} %copy-done.13, bf16[512,512]{1,0:T(8,128)(2,1)} %multiply_convert_fusion.3, f32[512]{0:T(512)S(1)} %get-tuple-element.112, f32[90]{0:T(128)S(1)} %get-tuple-element.114), kind=kOutput, calls=%fused_computation.28 | convolution fusion | flops 317240320 | bytes 1327464 | tf_op jit(solution)/shard_map/cond/branch_0_fun/lh,...hn->...ln/dot_general | solution.py:40
  80.2 0.7 copy-done.7
  80.8 1.4 %pad_maximum_fusion.1 = f32[3,90,768]{1,0,2:T(4,128)S(1)} fusion(f32[3,90,128]{1,0,2:T(4,128)} %collective-permute-done.9, f32[3,90,128]{1,0,2:T(4,128)S(1)} %collective-permute-done.8, f32[3,90,512]{1,0,2:T(4,128)S(1)} %copy.54), kind=kLoop, calls=%fused_computation.150 | loop fusion | flops 414720 | bytes 1658880 | tf_op jit(solution)/shard_map/concatenate | solution.py:49
  82.2 22.0 %conditional.7 = (f32[3,90,512]{2,1,0:T(8,128)S(1)}) conditional(s32[]{:T(128)} %convert_element_type.30, (f32[6,512]{1,0:T(8,128)S(1)}, s32[6,512]{1,0:T(8,128)S(1)}, f32[3,90,768]{1,0,2:T(4,128)S(1)}, f32[3,90,512]{2,1,0:T(8,128)S(1)}, f32[6,512]{1,0:T(8,128)S(1)}, /*index=5*/f32[90,512]{1,0:T(8,128)}) %tuple.130, ...), branch_computations={%region_6.7_spmd, %region_7.8_spmd} | conditional | flops 5087232 | bytes 23593052 | solution.py:63
  82.3 2.1 %gather_fusion = f32[512,3,90]{2,1,0:T(4,128)S(1)} fusion(f32[3,90,768]{1,0,2:T(4,128)S(1)} %get-tuple-element.117, s32[1024]{0:T(1024)S(1)} %pad_clamp_fusion.5), kind=kCustom, calls=%fused_computation | custom fusion | bytes 1107968 | tf_op jit(solution)/shard_map/cond/branch_0_fun/gather | solution.py:56
  84.3 1.1 %copy.34 = f32[512,3,90]{0,2,1:T(8,128)} copy(f32[512,3,90]{2,1,0:T(4,128)S(1)} %gather_fusion) | data formatting | bytes 1105920 | tf_op jit(solution)/shard_map/cond/branch_0_fun/gather | solution.py:56
  85.5 2.1 %gather_fusion.1 = f32[512,3,90]{2,1,0:T(4,128)S(1)} fusion(f32[3,90,768]{1,0,2:T(4,128)S(1)} %get-tuple-element.117, s32[1024]{0:T(1024)S(1)} %pad_clamp_fusion.4), kind=kCustom, calls=%fused_computation.1 | custom fusion | bytes 1107968 | tf_op jit(solution)/shard_map/cond/branch_0_fun/gather | solution.py:56
  87.6 1.1 %copy.35 = f32[512,3,90]{0,2,1:T(8,128)} copy(f32[512,3,90]{2,1,0:T(4,128)S(1)} %gather_fusion.1) | data formatting | bytes 1105920 | tf_op jit(solution)/shard_map/cond/branch_0_fun/gather | solution.py:56
  88.7 2.1 %gather_fusion.2 = f32[512,3,90]{2,1,0:T(4,128)S(1)} fusion(f32[3,90,768]{1,0,2:T(4,128)S(1)} %get-tuple-element.117, s32[1024]{0:T(1024)S(1)} %pad_clamp_fusion.3), kind=kCustom, calls=%fused_computation.2 | custom fusion | bytes 1107968 | tf_op jit(solution)/shard_map/cond/branch_0_fun/gather | solution.py:56
  90.8 1.1 %copy.36 = f32[512,3,90]{0,2,1:T(8,128)} copy(f32[512,3,90]{2,1,0:T(4,128)S(1)} %gather_fusion.2) | data formatting | bytes 1105920 | tf_op jit(solution)/shard_map/cond/branch_0_fun/gather | solution.py:56
  91.9 2.1 %gather_fusion.3 = f32[512,3,90]{2,1,0:T(4,128)S(1)} fusion(f32[3,90,768]{1,0,2:T(4,128)S(1)} %get-tuple-element.117, s32[1024]{0:T(1024)S(1)} %pad_clamp_fusion.2), kind=kCustom, calls=%fused_computation.3 | custom fusion | bytes 1107968 | tf_op jit(solution)/shard_map/cond/branch_0_fun/gather | solution.py:56
  94.0 1.1 %copy.37 = f32[512,3,90]{0,2,1:T(8,128)} copy(f32[512,3,90]{2,1,0:T(4,128)S(1)} %gather_fusion.3) | data formatting | bytes 1105920 | tf_op jit(solution)/shard_map/cond/branch_0_fun/gather | solution.py:56
  95.2 2.1 %gather_fusion.4 = f32[512,3,90]{2,1,0:T(4,128)S(1)} fusion(f32[3,90,768]{1,0,2:T(4,128)S(1)} %get-tuple-element.117, s32[1024]{0:T(1024)S(1)} %pad_clamp_fusion.1), kind=kCustom, calls=%fused_computation.4 | custom fusion | bytes 1107968 | tf_op jit(solution)/shard_map/cond/branch_0_fun/gather | solution.py:56
  97.2 1.2 %copy.38 = f32[512,3,90]{0,2,1:T(8,128)} copy(f32[512,3,90]{2,1,0:T(4,128)S(1)} %gather_fusion.4) | data formatting | bytes 1105920 | tf_op jit(solution)/shard_map/cond/branch_0_fun/gather | solution.py:56
  98.4 2.1 %gather_fusion.5 = f32[512,3,90]{2,1,0:T(4,128)S(1)} fusion(f32[3,90,768]{1,0,2:T(4,128)S(1)} %get-tuple-element.117, s32[1024]{0:T(1024)S(1)} %pad_clamp_fusion), kind=kCustom, calls=%fused_computation.5 | custom fusion | bytes 1107968 | tf_op jit(solution)/shard_map/cond/branch_0_fun/gather | solution.py:56
  100.5 1.1 %copy.39 = f32[512,3,90]{0,2,1:T(8,128)} copy(f32[512,3,90]{2,1,0:T(4,128)S(1)} %gather_fusion.5) | data formatting | bytes 1105920 | tf_op jit(solution)/shard_map/cond/branch_0_fun/gather | solution.py:56
  101.6 0.1 copy-done.5
  101.7 2.3 %fusion.12 = f32[3,90,512]{2,1,0:T(8,128)S(1)} fusion(f32[3,90,512]{2,1,0:T(8,128)S(1)} %get-tuple-element.115, f32[512,3,90]{0,2,1:T(8,128)} %copy.39, f32[512,3,90]{0,2,1:T(8,128)} %copy.38, f32[512,3,90]{0,2,1:T(8,128)} %copy.37, f32[512,3,90]{0,2,1:T(8,128)} %copy.36, f32[512,3,90]{0,2,1:T(8,128)S(1)} %copy-done.5, f32[512,3,90]{0,2,1:T(8,128)S(1)} %copy-done.3, ...), kind=kLoop, calls=%fused_computation.38 | loop fusion | flops 4976640 | bytes 4448256 | tf_op jit(solution)/shard_map/cond/branch_0_fun/add | solution.py:60
  104.1 0.1 fusion.34
  104.2 1.2 %maximum_select_fusion = f32[3,90,512]{2,1,0:T(8,128)S(1)} fusion(f32[3,90,512]{2,1,0:T(8,128)S(1)} %get-tuple-element.283, f32[1,90,512]{2,1,0:T(8,128)} %bitcast.44, f32[1,90,512]{2,1,0:T(8,128)} %bitcast.43, f32[1,90,512]{2,1,0:T(8,128)} %bitcast.42, pred[]{:T(512)S(6)} %eq.12), kind=kLoop, calls=%fused_computation.151 | loop fusion | flops 414720 | bytes 1658881 | tf_op jit(solution)/shard_map/jit(_where)/select_n | solution.py:101
  105.4 1.2 %broadcast_in_dim.2 = f32[1,3,90,512]{3,0,2,1:T(1,128)} reshape(f32[3,90,512]{2,1,0:T(8,128)S(1)} %maximum_select_fusion) | data formatting | bytes 1105920 | tf_op jit(solution)/shard_map/broadcast_in_dim | solution.py:101
  (63 shorter events, 0.4 us)
Async XLA Ops:
  0.0 7.9 %copy-start = (f32[1,3,90,512]{3,0,2,1:T(1,128)S(1)}, f32[1,3,90,512]{3,0,2,1:T(1,128)}, u32[]{:S(2)}) copy-start(f32[1,3,90,512]{3,0,2,1:T(1,128)} %param.23) | copy-start | bytes 1658884
  0.0 2.4 %copy-start.12 = (s32[2,128]{1,0:T(2,128)S(1)}, s32[2,128]{1,0:T(2,128)}, u32[]{:S(2)}) copy-start(s32[2,128]{1,0:T(2,128)} %param.25) | copy-start | bytes 3076
  3.5 11.9 %collective-permute-start = (f32[3,90,128]{1,0,2:T(4,128)S(1)}, f32[3,90,128]{1,0,2:T(4,128)S(1)}, u32[]{:S(2)}, u32[]{:S(2)}) collective-permute-start(f32[3,90,128]{1,0,2:T(4,128)S(1)} %get-tuple-element.278), channel_id=1, source_target_pairs={{0,1},{1,2},{2,3},{3,4},{4,5},{5,6},{6,7},{7,0},{8,9},{9,10},{10,1... | collective-permute-start | bytes 414728 | tf_op jit(solution)/shard_map/ppermute | solution.py:16
  4.8 12.6 %collective-permute-start.1 = (f32[3,90,128]{1,0,2:T(4,128)S(1)}, f32[3,90,128]{1,0,2:T(4,128)}, u32[]{:S(2)}, u32[]{:S(2)}) collective-permute-start(f32[3,90,128]{1,0,2:T(4,128)S(1)} %get-tuple-element.279), channel_id=1, source_target_pairs={{1,0},{2,1},{3,2},{4,3},{5,4},{6,5},{7,6},{0,7},{9,8},{10,9},{11,1... | collective-permute-start | bytes 414728 | tf_op jit(solution)/shard_map/ppermute | solution.py:17
  8.0 10.7 %collective-permute-start.2 = (f32[90,512]{1,0:T(8,128)S(1)}, f32[90,512]{1,0:T(8,128)}, u32[]{:S(2)}, u32[]{:S(2)}) collective-permute-start(f32[90,512]{1,0:T(8,128)S(1)} %get-tuple-element.275), channel_id=1, source_target_pairs={{0,24},{1,25},{2,26},{3,27},{4,28},{5,29},{6,30},{7,31}} | collective-permute-start | bytes 552968 | tf_op jit(solution)/shard_map/ppermute | solution.py:25
  9.3 9.4 %collective-permute-start.3 = (f32[90,512]{1,0:T(8,128)S(1)}, f32[90,512]{1,0:T(8,128)}, u32[]{:S(2)}, u32[]{:S(2)}) collective-permute-start(f32[90,512]{1,0:T(8,128)S(1)} %get-tuple-element.274), channel_id=1, source_target_pairs={{0,16},{8,24},{1,17},{9,25},{2,18},{10,26},{3,19},{11,27},{4,20},{... | collective-permute-start | bytes 552968 | tf_op jit(solution)/shard_map/ppermute | solution.py:25
  10.6 8.2 %collective-permute-start.4 = (f32[90,512]{1,0:T(8,128)S(1)}, f32[90,512]{1,0:T(8,128)}, u32[]{:S(2)}, u32[]{:S(2)}) collective-permute-start(f32[90,512]{1,0:T(8,128)S(1)} %get-tuple-element.273), channel_id=1, source_target_pairs={{0,8},{8,16},{16,24},{1,9},{9,17},{17,25},{2,10},{10,18},{18,26},{... | collective-permute-start | bytes 552968 | tf_op jit(solution)/shard_map/ppermute | solution.py:25
  11.9 6.9 %copy-start.9 = (s32[6,512]{1,0:T(8,128)S(1)}, s32[6,512]{1,0:T(8,128)}, u32[]{:S(2)}) copy-start(s32[6,512]{1,0:T(8,128)} %param.24) | copy-start | bytes 36868
  12.0 6.9 %copy-start.10 = (f32[6,512]{1,0:T(8,128)S(1)}, f32[6,512]{1,0:T(8,128)}, u32[]{:S(2)}) copy-start(f32[6,512]{1,0:T(8,128)} %param.26) | copy-start | bytes 36868
  12.0 6.9 %copy-start.11 = (f32[6,512]{1,0:T(8,128)S(1)}, f32[6,512]{1,0:T(8,128)}, u32[]{:S(2)}) copy-start(f32[6,512]{1,0:T(8,128)} %param.27) | copy-start | bytes 36868
  46.5 3.6 %copy-start.2 = (f32[512,3,90]{0,2,1:T(8,128)S(1)}, f32[512,3,90]{0,2,1:T(8,128)}, u32[]{:S(2)}) copy-start(f32[512,3,90]{0,2,1:T(8,128)} %copy.40) | copy-start | bytes 1658884 | tf_op jit(solution)/shard_map/cond
  46.5 3.6 %copy-start.4 = (f32[512,3,90]{0,2,1:T(8,128)S(1)}, f32[512,3,90]{0,2,1:T(8,128)}, u32[]{:S(2)}) copy-start(f32[512,3,90]{0,2,1:T(8,128)} %copy.41) | copy-start | bytes 1658884 | tf_op jit(solution)/shard_map/cond
  46.5 3.6 %copy-start.6 = (f32[512,3,90]{0,2,1:T(8,128)S(1)}, f32[512,3,90]{0,2,1:T(8,128)}, u32[]{:S(2)}) copy-start(f32[512,3,90]{0,2,1:T(8,128)} %copy.42) | copy-start | bytes 1658884 | tf_op jit(solution)/shard_map/cond
  53.9 6.0 %copy-start.14 = (bf16[90,512]{1,0:T(8,128)(2,1)S(1)}, bf16[90,512]{1,0:T(8,128)(2,1)}, u32[]{:S(2)}) copy-start(bf16[90,512]{1,0:T(8,128)(2,1)} %param.32) | copy-start | bytes 276484
  53.9 6.0 %copy-start.15 = (f32[512]{0:T(512)S(1)}, f32[512]{0:T(512)}, u32[]{:S(2)}) copy-start(f32[512]{0:T(512)} %param.29) | copy-start | bytes 6148
  53.9 6.0 %copy-start.16 = (f32[512]{0:T(512)S(1)}, f32[512]{0:T(512)}, u32[]{:S(2)}) copy-start(f32[512]{0:T(512)} %param.31) | copy-start | bytes 6148
  53.9 6.0 %copy-start.17 = (f32[90]{0:T(128)S(1)}, f32[90]{0:T(128)}, u32[]{:S(2)}) copy-start(f32[90]{0:T(128)} %param.33) | copy-start | bytes 1084
  55.7 24.4 %collective-permute-start.8 = (f32[3,90,128]{1,0,2:T(4,128)}, f32[3,90,128]{1,0,2:T(4,128)S(1)}, u32[]{:S(2)}, u32[]{:S(2)}) collective-permute-start(f32[3,90,128]{1,0,2:T(4,128)} %get-tuple-element.276), channel_id=1, source_target_pairs={{0,1},{1,2},{2,3},{3,4},{4,5},{5,6},{6,7},{7,0},{8,9},{9,10},{10,1... | collective-permute-start | bytes 414728 | tf_op jit(solution)/shard_map/ppermute | solution.py:16
  56.1 24.7 %collective-permute-start.9 = (f32[3,90,128]{1,0,2:T(4,128)S(1)}, f32[3,90,128]{1,0,2:T(4,128)}, u32[]{:S(2)}, u32[]{:S(2)}) collective-permute-start(f32[3,90,128]{1,0,2:T(4,128)S(1)} %get-tuple-element.277), channel_id=1, source_target_pairs={{1,0},{2,1},{3,2},{4,3},{5,4},{6,5},{7,6},{0,7},{9,8},{10,9},{11,1... | collective-permute-start | bytes 414728 | tf_op jit(solution)/shard_map/ppermute | solution.py:17
  60.0 15.6 %copy-start.1 = (f32[1,3,90,512]{3,0,2,1:T(1,128)S(1)}, f32[1,3,90,512]{3,0,2,1:T(1,128)}, u32[]{:S(2)}) copy-start(f32[1,3,90,512]{3,0,2,1:T(1,128)} %param.23) | copy-start | bytes 1658884
  65.2 39.0 %collective-permute-start.5 = (f32[90,512]{1,0:T(8,128)}, f32[90,512]{1,0:T(8,128)}, u32[]{:S(2)}, u32[]{:S(2)}) collective-permute-start(f32[90,512]{1,0:T(8,128)} %get-tuple-element.281), channel_id=1, source_target_pairs={{8,0},{16,8},{24,16},{9,1},{17,9},{25,17},{10,2},{18,10},{26,18},{... | collective-permute-start | bytes 552968 | tf_op jit(solution)/shard_map/ppermute | solution.py:25
  71.6 32.5 %collective-permute-start.6 = (f32[90,512]{1,0:T(8,128)}, f32[90,512]{1,0:T(8,128)}, u32[]{:S(2)}, u32[]{:S(2)}) collective-permute-start(f32[90,512]{1,0:T(8,128)} %get-tuple-element.281), channel_id=1, source_target_pairs={{16,0},{24,8},{17,1},{25,9},{18,2},{26,10},{19,3},{27,11},{20,4},{... | collective-permute-start | bytes 552968 | tf_op jit(solution)/shard_map/ppermute | solution.py:25
  73.6 30.6 %collective-permute-start.7 = (f32[90,512]{1,0:T(8,128)}, f32[90,512]{1,0:T(8,128)}, u32[]{:S(2)}, u32[]{:S(2)}) collective-permute-start(f32[90,512]{1,0:T(8,128)} %get-tuple-element.281), channel_id=1, source_target_pairs={{24,0},{25,1},{26,2},{27,3},{28,4},{29,5},{30,6},{31,7}} | collective-permute-start | bytes 552968 | tf_op jit(solution)/shard_map/ppermute | solution.py:25
  75.9 2.4 %copy-start.13 = (bf16[512,512]{1,0:T(8,128)(2,1)S(1)}, bf16[512,512]{1,0:T(8,128)(2,1)}, u32[]{:S(2)}) copy-start(bf16[512,512]{1,0:T(8,128)(2,1)} %get-tuple-element.111) | copy-start | bytes 1572868 | tf_op jit(solution)/shard_map/cond
  80.1 0.7 copy-start.7
  100.5 1.2 %copy-start.3 = (f32[512,3,90]{0,2,1:T(8,128)S(1)}, f32[512,3,90]{0,2,1:T(8,128)}, u32[]{:S(2)}) copy-start(f32[512,3,90]{0,2,1:T(8,128)} %copy.34) | copy-start | bytes 1658884 | tf_op jit(solution)/shard_map/cond
  100.5 1.2 %copy-start.5 = (f32[512,3,90]{0,2,1:T(8,128)S(1)}, f32[512,3,90]{0,2,1:T(8,128)}, u32[]{:S(2)}) copy-start(f32[512,3,90]{0,2,1:T(8,128)} %copy.35) | copy-start | bytes 1658884 | tf_op jit(solution)/shard_map/cond
  101.7 2.3 %copy-start.8 = (f32[90,512]{1,0:T(8,128)S(1)}, f32[90,512]{1,0:T(8,128)}, u32[]{:S(2)}) copy-start(f32[90,512]{1,0:T(8,128)} %get-tuple-element.120) | copy-start | bytes 552964 | tf_op jit(solution)/shard_map/cond
where the time goes:
time: 107 us
  local copies, waits for them, and re-layouts  58.4 us (55%)
  starting transfers between devices  22.8 us (21%)
  other arithmetic  9.87 us (9%)
  matrix products  9.29 us (9%)
  waiting for transfers between devices  5.45 us (5%)
    gather x24, local copies, waits for them, and re-layouts, sweep(): near = ext[:, :, neighbours[edge]]  49.3 us
    ppermute x6, starting transfers between devices, passed_along(): return lax.ppermute(array, axis, pairs)  14.3 us
    ppermute x2, starting transfers between devices, extended(): after = lax.ppermute(first, axis, down)  6.94 us
    dot_general x2, matrix products, network(): jnp.einsum('hf,...fn->...hn', w_in, feats, preferred_element_type=jnp.flo...  4.87 us
    add x2, other arithmetic, sweep(): moved = values + total  4.65 us
    dot_general x2, matrix products, network(): jnp.einsum('lh,...hn->...ln', w_out, second, preferred_element_type=jnp.f...  4.42 us
    ppermute x2, waiting for transfers between devices, extended(): before = lax.ppermute(last, axis, up)  3.45 us
    unnamed x25, local copies, waits for them, and re-layouts  3.2 us
  transfers between devices with their start and end apart: 10, of which 2 were waited for; matrix products, arithmetic and copies ran while one was open for 32% of the time, Pallas kernels for 0%

commit v1 on v0

v1 whole, which is shorter than its diff:
```python
import functools

import jax
import jax.numpy as jnp
from jax import lax
from jax.experimental import pallas as pl
from jax.experimental.pallas import tpu as pltpu
from jax.sharding import PartitionSpec as P

heat_gain = 0.5
bf16, f32 = jnp.bfloat16, jnp.float32


def dot(a, b):
    return jnp.dot(a, b, preferred_element_type=f32)


def pick_matrix(rows_ref, cells):
    halo = rows_ref.shape[1]
    cell = lax.broadcasted_iota(jnp.int32, (cells, halo), 0)
    return jnp.concatenate(
        [(cell == rows_ref[side : side + 1, :]).astype(bf16) for side in range(2)], axis=1
    )


def load_rows(ref, first, rows, cells):
    tiles = cells // 128
    return jnp.concatenate(
        [ref[pl.ds(first * tiles + tile, rows, stride=tiles), :] for tile in range(tiles)], axis=1
    )


def pack_kernel(held_ref, rows_ref, *out_refs):
    *slot_refs, state_ref, lower_ref, upper_ref = out_refs
    features, cells = state_ref.shape
    state = load_rows(held_ref, 0, features, cells).astype(bf16)
    state_ref[...] = state
    halo = rows_ref.shape[1]
    sent = dot(state, pick_matrix(rows_ref, cells)).astype(bf16)
    lower_ref[...] = sent[:, :halo]
    upper_ref[...] = sent[:, halo:]
    size = slot_refs[0].shape[0]
    for index, ref in enumerate(slot_refs):
        ref[...] = held_ref[index * size : (index + 1) * size, :]


def silu(v):
    half = 0.5 * v
    return half + half * jnp.tanh(half)


def network(state, w_in_ref, b_in_ref, w_mid_ref, b_mid_ref, w_out_ref, b_out_ref):
    def bias(ref):
        return jnp.concatenate([ref[...]] * (state.shape[1] // ref.shape[1]), axis=1)

    first = silu(dot(w_in_ref[...], state) + bias(b_in_ref)).astype(bf16)
    second = silu(dot(w_mid_ref[...], first) + bias(b_mid_ref)).astype(bf16)
    return dot(w_out_ref[...], second) + bias(b_out_ref)


def first_kernel(
    held_ref, state_ref, near_ref, diff_ref, tran_ref,
    w_in_t_ref, b_in_ref, w_mid_ref, b_mid_ref, w_out_ref, b_out_ref,
    heat_ref, matrix_ref, matrix_low_ref, keep_ref, part_ref, w_in_ref, c_in_ref, c_mid_ref, c_out_ref,
):
    features, cells = state_ref.shape
    w_in_ref[...] = w_in_t_ref[...].T
    for row_ref, column_ref in ((b_in_ref, c_in_ref), (b_mid_ref, c_mid_ref), (b_out_ref, c_out_ref)):
        column_ref[...] = jnp.broadcast_to(row_ref[...], (128, row_ref.shape[1])).T
    heat_ref[...] = network(
        state_ref[...], w_in_ref, c_in_ref, w_mid_ref, c_mid_ref, w_out_ref, c_out_ref
    )
    half_tran = 0.5 * tran_ref[...]
    weight = diff_ref[...] - half_tran
    keep = 1.0 - jnp.sum(diff_ref[...] + half_tran, axis=0, keepdims=True)
    keep_ref[...] = keep
    piece = 128
    for start in range(0, matrix_ref.shape[0], piece):
        cell = lax.broadcasted_iota(jnp.int32, (piece, cells), 0) + start
        total = jnp.zeros((piece, cells), f32)
        for edge in range(near_ref.shape[0]):
            total = total + jnp.where(
                cell == near_ref[edge : edge + 1, :], weight[edge : edge + 1, :], 0.0
            )
        high = total.astype(bf16)
        matrix_ref[start : start + piece, :] = high
        matrix_low_ref[start : start + piece, :] = (total - high.astype(f32)).astype(bf16)
    state = load_rows(held_ref, 0, features, cells)
    low = (state - state_ref[...].astype(f32)).astype(bf16)
    part_ref[...] = (
        dot(state_ref[...], matrix_ref[:cells, :])
        + dot(state_ref[...], matrix_low_ref[:cells, :])
        + dot(low, matrix_ref[:cells, :])
        + state * keep
    )


def halo_sum(matrix_ref, from_lower, from_upper):
    cells, halo = matrix_ref.shape[1], from_lower.shape[1]
    return dot(from_lower, matrix_ref[cells : cells + halo, :]) + dot(
        from_upper, matrix_ref[cells + halo :, :]
    )


def middle_kernel(
    slot_ref, rows_ref, part_ref, matrix_ref, matrix_low_ref, from_lower_ref, from_upper_ref, *refs
):
    *heat_refs, state_ref, state_bf_ref, lower_ref, upper_ref = refs
    cells, halo = matrix_ref.shape[1], rows_ref.shape[1]
    levels = heat_refs[0].shape[0] * 128 // cells
    slot = slot_ref[0]
    from_lower, from_upper = from_lower_ref[...], from_upper_ref[...]
    state_ref[...] = (
        part_ref[...]
        + halo_sum(matrix_ref, from_lower, from_upper)
        + halo_sum(matrix_low_ref, from_lower, from_upper)
    )
    for index, ref in enumerate(heat_refs):

        @pl.when(slot == index + 1)
        def _():
            state_ref[:levels, :] = state_ref[:levels, :] + heat_gain * load_rows(ref, 0, levels, cells)

    state = state_ref[...].astype(bf16)
    state_bf_ref[...] = state
    sent = dot(state, pick_matrix(rows_ref, cells)).astype(bf16)
    lower_ref[...] = sent[:, :halo]
    upper_ref[...] = sent[:, halo:]


def second_kernel(
    state_ref, w_in_ref, b_in_ref, w_mid_ref, b_mid_ref, w_out_ref, b_out_ref, heat_ref
):
    heat_ref[...] = network(
        state_ref[...], w_in_ref, b_in_ref, w_mid_ref, b_mid_ref, w_out_ref, b_out_ref
    ).astype(bf16)


def own_kernel(state_ref, state_bf_ref, matrix_ref, keep_ref, heat_ref, part_ref):
    cells, levels = matrix_ref.shape[1], heat_ref.shape[0]
    part_ref[...] = dot(state_bf_ref[...], matrix_ref[:cells, :]) + state_ref[...] * keep_ref[...]
    part_ref[:levels, :] = part_ref[:levels, :] + heat_gain * heat_ref[...]


def last_kernel(slot_ref, part_ref, matrix_ref, from_lower_ref, from_upper_ref, *refs):
    *heat_refs, out_ref = refs
    cells = matrix_ref.shape[1]
    tiles = cells // 128
    levels = heat_refs[0].shape[0]

    def store_rows(first, values):
        for tile in range(tiles):
            out_ref[pl.ds(first * tiles + tile, values.shape[0], stride=tiles), :] = values[
                :, tile * 128 : (tile + 1) * 128
            ]

    @pl.when(slot_ref[0] == 0)
    def _():
        for index, ref in enumerate(heat_refs):
            store_rows(index * levels, ref[...].astype(f32))

    @pl.when(slot_ref[0] != 0)
    def _():
        store_rows(
            0, part_ref[...] + halo_sum(matrix_ref, from_lower_ref[...], from_upper_ref[...])
        )


VMEM = pl.BlockSpec(memory_space=pltpu.VMEM)
SMEM = pl.BlockSpec(memory_space=pltpu.SMEM)


def call(kernel, name, out_shape, scalars, *args, flops=0, limit=16 << 20):
    size = sum(a.size * a.dtype.itemsize for a in args)
    return pl.pallas_call(
        kernel,
        out_shape=out_shape,
        in_specs=[SMEM] * scalars + [VMEM] * (len(args) - scalars),
        out_specs=jax.tree.map(lambda _: VMEM, out_shape),
        compiler_params=pltpu.CompilerParams(vmem_limit_bytes=limit),
        cost_estimate=pl.CostEstimate(flops=flops, bytes_accessed=size, transcendentals=0),
        name=name,
    )(*args)


def body(held, neighbours, send_rows, diffusion, transport, w_in, b_in, w_mid, b_mid, w_out, b_out):
    groups, blocks = lax.axis_size("grp"), lax.axis_size("blk")
    quarter = groups // 4
    slot = (lax.axis_index("grp") // quarter).astype(jnp.int32).reshape(1)
    _, fields, levels, cells = held.shape
    halo = send_rows.shape[1]
    hidden = w_mid.shape[0]
    features = fields * levels
    up = [(i, (i + 1) % blocks) for i in range(blocks)]
    down = [(j, i) for i, j in up]

    def swap(array, slot):
        to = {0: slot, slot: 0}
        pairs = [
            (g, to.get(g // quarter, g // quarter) * quarter + g % quarter) for g in range(groups)
        ]
        return lax.ppermute(array, "grp", pairs)

    def shape(*dims, dtype=f32):
        return jax.ShapeDtypeStruct(dims, dtype)

    halo_shape = shape(features, halo, dtype=bf16)
    state_shape = shape(features, cells, dtype=bf16)
    matrix_shape = shape(cells + 2 * halo, cells, dtype=bf16)
    flat = held.reshape(features * cells // 128, 128)
    *slots, state0, lower0, upper0 = call(
        pack_kernel, "pack",
        [shape(levels * cells // 128, 128)] * 3 + [state_shape, halo_shape, halo_shape],
        0, flat, send_rows, flops=2 * features * cells * 2 * halo,
    )
    from_lower0 = lax.ppermute(upper0, "blk", up)
    from_upper0 = lax.ppermute(lower0, "blk", down)
    heats0 = [swap(array, index + 1) for index, array in enumerate(slots)]
    heat1, matrix, matrix_low, keep, part1, *weights = call(
        first_kernel, "first",
        [
            shape(levels, cells), matrix_shape, matrix_shape, shape(1, cells), shape(features, cells),
            shape(hidden, features, dtype=bf16), shape(hidden, 128), shape(hidden, 128), shape(levels, 128),
        ],
        0, flat, state0, neighbours, diffusion, transport,
        w_in.T, b_in[None], w_mid, b_mid[None], w_out, b_out[None],
        flops=2 * cells * hidden * (hidden + features),
    )
    w_in_n, c_in, c_mid, c_out = weights
    state1, state1_bf, lower1, upper1 = call(
        middle_kernel, "middle",
        [shape(features, cells), state_shape, halo_shape, halo_shape],
        1, slot, send_rows, part1, matrix, matrix_low, from_lower0, from_upper0, *heats0,
        flops=2 * features * cells * 2 * halo,
    )
    from_lower1 = lax.ppermute(upper1, "blk", up)
    from_upper1 = lax.ppermute(lower1, "blk", down)
    heat2 = call(
        second_kernel, "second", shape(levels, cells, dtype=bf16),
        0, state1_bf, w_in_n, c_in, w_mid, c_mid, w_out, c_out,
        flops=2 * cells * hidden * (hidden + features),
    )
    heats2 = [swap(heat2, index + 1) for index in range(3)]
    part2 = call(
        own_kernel, "own", shape(features, cells),
        0, state1, state1_bf, matrix, keep, heat1, flops=2 * features * cells * cells,
    )
    out = call(
        last_kernel, "last", shape(*flat.shape),
        1, slot, part2, matrix, from_lower1, from_upper1, *heats2, flops=2 * features * cells * 2 * halo,
    )
    return out.reshape(held.shape)


def solution(mesh):
    placed = (
        P("grp", None, None, "blk"),
        P(None, "blk"),
        P(None, "blk"),
        P(None, "blk"),
        P(None, "blk"),
        P(),
        P(),
        P(),
        P(),
        P(),
        P(),
    )
    return jax.shard_map(
        body, mesh=mesh, in_specs=placed, out_specs=P("grp", None, None, "blk"), check_vma=False
    )
```

time: 107 us -> 40.2 us (0.38)
  the two profiles are of different devices: /device:TPU:3 before, /device:TPU:0 now
where the time goes in v1:
time: 40.2 us; the launch traced here: 39.5 us
  starting transfers between devices  24.1 us (60%)
  local copies, waits for them, and re-layouts  6.96 us (17%)
  Pallas kernels  6.05 us (15%)
  waiting for transfers between devices  2.27 us (6%)
    ppermute x6, starting transfers between devices, swap(): return lax.ppermute(array, 'grp', pairs)  14.5 us
    unnamed x26, local copies, waits for them, and re-layouts  6.96 us
    pallas_call x6, Pallas kernels, call(): pl.pallas_call(kernel, out_shape=out_shape, in_specs=[SMEM] * scalars + [...  6.05 us
    ppermute x1, starting transfers between devices, body(): from_upper1 = lax.ppermute(lower1, 'blk', down)  4.71 us
    ppermute x1, starting transfers between devices, body(): from_upper0 = lax.ppermute(lower0, 'blk', down)  3.2 us
    ppermute x1, waiting for transfers between devices, body(): from_lower1 = lax.ppermute(upper1, 'blk', up)  2.24 us
    ppermute x1, starting transfers between devices, body(): from_lower0 = lax.ppermute(upper0, 'blk', up)  1.57 us
  transfers between devices with their start and end apart: 10, of which 1 were waited for; matrix products, arithmetic and copies ran while one was open for 0% of the time, Pallas kernels for 8%

profile of v1, /device:TPU:0, one launch (start us, length us, event | category | flops | bytes accessed | tf_op | source)
XLA Modules:
  0.0 39.5 jit_solution(11156661204632804834)
XLA Ops:
  0.0 0.0 copy-start.9
  0.0 0.7 %copy-done.9 = s32[2,128]{1,0:T(2,128)S(1)} copy-done((s32[2,128]{1,0:T(2,128)S(1)}, s32[2,128]{1,0:T(2,128)}, u32[]{:S(2)}) %copy-start.9) | copy-done | bytes 1048
  0.7 0.0 copy-start
  0.7 1.0 %copy-done = f32[1,3,90,512]{3,0,2,1:T(1,128)S(1)} copy-done((f32[1,3,90,512]{3,0,2,1:T(1,128)S(1)}, f32[1,3,90,512]{3,0,2,1:T(1,128)}, u32[]{:S(2)}) %copy-start) | copy-done | bytes 552984
  1.7 0.0 copy-start.1
  1.7 0.2 pack.1
  2.0 0.0 copy-start.6
  2.0 2.4 %collective-permute-start.2 = (f32[360,128]{1,0:T(8,128)S(1)}, f32[360,128]{1,0:T(8,128)S(1)}, u32[]{:S(2)}, u32[]{:S(2)}) collective-permute-start(f32[360,128]{1,0:T(8,128)S(1)} %get-tuple-element.30), channel_id=1, source_target_pairs={{0,8},{8,0},{16,16},{24,24},{1,9},{9,1},{17,17},{25,25},{2,10},{10... | collective-permute-start | bytes 552968 | tf_op jit(solution)/shard_map/ppermute | solution.py:202
  4.4 3.2 %collective-permute-start.3 = (f32[360,128]{1,0:T(8,128)S(1)}, f32[360,128]{1,0:T(8,128)S(1)}, u32[]{:S(2)}, u32[]{:S(2)}) collective-permute-start(f32[360,128]{1,0:T(8,128)S(1)} %get-tuple-element.31), channel_id=1, source_target_pairs={{0,16},{8,8},{16,0},{24,24},{1,17},{9,9},{17,1},{25,25},{2,18},{10... | collective-permute-start | bytes 552968 | tf_op jit(solution)/shard_map/ppermute | solution.py:202
  7.5 1.9 %collective-permute-start.4 = (f32[360,128]{1,0:T(8,128)S(1)}, f32[360,128]{1,0:T(8,128)S(1)}, u32[]{:S(2)}, u32[]{:S(2)}) collective-permute-start(f32[360,128]{1,0:T(8,128)S(1)} %get-tuple-element.32), channel_id=1, source_target_pairs={{0,24},{8,8},{16,16},{24,0},{1,25},{9,9},{17,17},{25,1},{2,26},{10... | collective-permute-start | bytes 552968 | tf_op jit(solution)/shard_map/ppermute | solution.py:202
  9.5 1.6 %collective-permute-start = (bf16[270,128]{1,0:T(8,128)(2,1)S(1)}, bf16[270,128]{1,0:T(8,128)(2,1)S(1)}, u32[]{:S(2)}, u32[]{:S(2)}) collective-permute-start(bf16[270,128]{1,0:T(8,128)(2,1)S(1)} %get-tuple-element.28), channel_id=1, source_target_pairs={{0,1},{1,2},{2,3},{3,4},{4,5},{5,6},{6,7},{7,0},{8,9},{9,10},{10,1... | collective-permute-start | bytes 207368 | tf_op jit(solution)/shard_map/ppermute | solution.py:216
  11.0 3.2 %collective-permute-start.1 = (bf16[270,128]{1,0:T(8,128)(2,1)S(1)}, bf16[270,128]{1,0:T(8,128)(2,1)S(1)}, u32[]{:S(2)}, u32[]{:S(2)}) collective-permute-start(bf16[270,128]{1,0:T(8,128)(2,1)S(1)} %get-tuple-element.29), channel_id=1, source_target_pairs={{1,0},{2,1},{3,2},{4,3},{5,4},{6,5},{7,6},{0,7},{9,8},{10,9},{11,1... | collective-permute-start | bytes 207368 | tf_op jit(solution)/shard_map/ppermute | solution.py:217
  14.2 0.0 copy-start.11
  14.2 0.0 copy-start.10
  14.2 0.0 copy-start.12
  14.2 0.0 copy-done.1
  14.3 0.0 copy-done.6
  14.3 0.7 %copy-done.11 = f32[512]{0:T(512)S(1)} copy-done((f32[512]{0:T(512)S(1)}, f32[512]{0:T(512)}, u32[]{:S(2)}) %copy-start.11) | copy-done | bytes 2072
  14.9 0.0 copy-done.10
  14.9 0.0 copy-done.12
  14.9 0.0 copy-start.2
  14.9 1.0 %copy-done.2 = bf16[512,512]{1,0:T(8,128)(2,1)S(1)} copy-done((bf16[512,512]{1,0:T(8,128)(2,1)S(1)}, bf16[512,512]{1,0:T(8,128)(2,1)}, u32[]{:S(2)}) %copy-start.2) | copy-done | bytes 524312
  16.0 0.0 copy-start.4
  16.0 0.9 %copy-done.4 = bf16[90,512]{1,0:T(8,128)(2,1)S(1)} copy-done((bf16[90,512]{1,0:T(8,128)(2,1)S(1)}, bf16[90,512]{1,0:T(8,128)(2,1)}, u32[]{:S(2)}) %copy-start.4) | copy-done | bytes 92184
  16.9 0.0 copy-start.5
  16.9 1.0 %copy-done.5 = bf16[512,270]{0,1:T(8,128)(2,1)S(1)} copy-done((bf16[512,270]{0,1:T(8,128)(2,1)S(1)}, bf16[512,270]{0,1:T(8,128)(2,1)}, u32[]{:S(2)}) %copy-start.5) | copy-done | bytes 276504
  17.8 0.0 copy-start.7
  17.8 0.7 %copy-done.7 = f32[6,512]{1,0:T(8,128)S(1)} copy-done((f32[6,512]{1,0:T(8,128)S(1)}, f32[6,512]{1,0:T(8,128)}, u32[]{:S(2)}) %copy-start.7) | copy-done | bytes 12312
  18.6 0.0 copy-start.8
  18.6 0.7 %copy-done.8 = f32[6,512]{1,0:T(8,128)S(1)} copy-done((f32[6,512]{1,0:T(8,128)S(1)}, f32[6,512]{1,0:T(8,128)}, u32[]{:S(2)}) %copy-start.8) | copy-done | bytes 12312
  19.3 2.7 %first.1 = (f32[90,512]{1,0:T(8,128)S(1)}, bf16[768,512]{1,0:T(8,128)(2,1)S(1)}, bf16[768,512]{1,0:T(8,128)(2,1)S(1)}, f32[1,512]{1,0:T(1,128)S(1)}, f32[270,512...) custom-call(f32[1080,128]{1,0:T(8,128)S(1)} %bitcast.8, ...), custom_call_target="tpu_custom_call" | custom-call | flops 409993216 | bytes 1763688 | tf_op jit(solution)/shard_map/first/pallas_call | solution.py:175
  22.0 0.0 collective-permute-done.from_lower_ref
  22.0 0.0 collective-permute-done.1.from_upper_ref
  22.0 0.0 collective-permute-done.2.refs_0_
  22.0 0.0 collective-permute-done.3.refs_1_
  22.0 0.0 collective-permute-done.4.refs_2_
  22.0 0.0 copy-start.3
  22.0 0.8 %middle.1 = (f32[270,512]{1,0:T(8,128)S(1)}, bf16[270,512]{1,0:T(8,128)(2,1)S(1)}, bf16[270,128]{1,0:T(8,128)(2,1)S(1)}, bf16[270,128]{1,0:T(8,128)(2,1)S(1)}) custom-call(s32[1]{0:T(128)} %bitcast.slot_ref, s32[2,128]{1,0:T(2,128)S(1)} %copy-done.9, f32[270,512]{1,0:T(8,128)S(1)} %get-tuple-element.25.part_ref, ...), custom_call_target="tpu_custom_call" | custom-call | flops 70778880 | bytes 2818052 | tf_op jit(solution)/shard_map/middle/pallas_call | solution.py:175
  22.8 0.2 copy-done.3
  23.1 1.1 %second.1 = bf16[90,512]{1,0:T(8,128)(2,1)S(1)} custom-call(bf16[270,512]{1,0:T(8,128)(2,1)S(1)} %get-tuple-element.34.state_bf_ref.state_ref, bf16[512,270]{1,0:T(8,128)(2,1)S(1)} %get-tuple-element.39.w_in_ref, f32[512,128]{1,0:T(8,128)S(1)} %get-tuple-element.40.b_in_ref, bf16[512,512]{1,0:T(8,128)(2,1)S(1)} %copy-done.3, ...), custom_call_target="tpu_custom_call" | custom-call | flops 409993216 | bytes 1739776 | tf_op jit(solution)/shard_map/second/pallas_call | solution.py:175
  24.2 3.3 %collective-permute-start.9 = (bf16[90,512]{1,0:T(8,128)(2,1)S(1)}, bf16[90,512]{1,0:T(8,128)(2,1)S(1)}, u32[]{:S(2)}, u32[]{:S(2)}) collective-permute-start(bf16[90,512]{1,0:T(8,128)(2,1)S(1)} %second.1), channel_id=1, source_target_pairs={{0,24},{8,8},{16,16},{24,0},{1,25},{9,9},{17,17},{25,1},{2,26},{10... | collective-permute-start | bytes 276488 | tf_op jit(solution)/shard_map/ppermute | solution.py:202
  27.5 1.9 %collective-permute-start.8 = (bf16[90,512]{1,0:T(8,128)(2,1)S(1)}, bf16[90,512]{1,0:T(8,128)(2,1)S(1)}, u32[]{:S(2)}, u32[]{:S(2)}) collective-permute-start(bf16[90,512]{1,0:T(8,128)(2,1)S(1)} %second.1), channel_id=1, source_target_pairs={{0,16},{8,8},{16,0},{24,24},{1,17},{9,9},{17,1},{25,25},{2,18},{10... | collective-permute-start | bytes 276488 | tf_op jit(solution)/shard_map/ppermute | solution.py:202
  29.4 1.9 %collective-permute-start.7 = (bf16[90,512]{1,0:T(8,128)(2,1)S(1)}, bf16[90,512]{1,0:T(8,128)(2,1)S(1)}, u32[]{:S(2)}, u32[]{:S(2)}) collective-permute-start(bf16[90,512]{1,0:T(8,128)(2,1)S(1)} %second.1), channel_id=1, source_target_pairs={{0,8},{8,0},{16,16},{24,24},{1,9},{9,1},{17,17},{25,25},{2,10},{10... | collective-permute-start | bytes 276488 | tf_op jit(solution)/shard_map/ppermute | solution.py:202
  31.3 0.1 collective-permute-start.5
  31.4 4.7 %collective-permute-start.6 = (bf16[270,128]{1,0:T(8,128)(2,1)S(1)}, bf16[270,128]{1,0:T(8,128)(2,1)S(1)}, u32[]{:S(2)}, u32[]{:S(2)}) collective-permute-start(bf16[270,128]{1,0:T(8,128)(2,1)S(1)} %get-tuple-element.38), channel_id=1, source_target_pairs={{1,0},{2,1},{3,2},{4,3},{5,4},{6,5},{7,6},{0,7},{9,8},{10,9},{11,1... | collective-permute-start | bytes 207368 | tf_op jit(solution)/shard_map/ppermute | solution.py:237
  36.1 0.3 own.1.part_ref
  36.4 2.2 %collective-permute-done.5.from_lower_ref = bf16[270,128]{1,0:T(8,128)(2,1)S(1)} collective-permute-done((bf16[270,128]{1,0:T(8,128)(2,1)S(1)}, bf16[270,128]{1,0:T(8,128)(2,1)S(1)}, u32[]{:S(2)}, u32[]{:S(2)}) %collective-permute-start.5) | collective-permute-done | bytes 69152 | tf_op jit(solution)/shard_map/ppermute | solution.py:236
  38.6 0.0 collective-permute-done.6.from_upper_ref
  38.6 0.0 collective-permute-done.9.refs_2_
  38.7 0.0 collective-permute-done.8.refs_1_
  38.7 0.0 collective-permute-done.7.refs_0_
  38.7 0.9 %last.1 = f32[1080,128]{1,0:T(8,128)} custom-call(s32[1]{0:T(128)} %bitcast.slot_ref, f32[270,512]{1,0:T(8,128)S(1)} %own.1.part_ref, bf16[768,512]{1,0:T(8,128)(2,1)S(1)} %get-tuple-element.26.matrix_ref, bf16[270,128]{1,0:T(8,128)(2,1)S(1)} %collective-permute-done.5.from_lower_ref, bf16[270,128]{1,0:T(8,128)(2,1)S(1)} %collective-permute-done.6.from_upper_ref, ...), custom_call_target="tpu_custom_call" | custom-call | flops 70778880 | bytes 1754116 | tf_op jit(solution)/shard_map/last/pallas_call | solution.py:175
Async XLA Ops:
  0.0 0.7 %copy-start.9 = (s32[2,128]{1,0:T(2,128)S(1)}, s32[2,128]{1,0:T(2,128)}, u32[]{:S(2)}) copy-start(s32[2,128]{1,0:T(2,128)} %rows_ref.3) | copy-start | bytes 3076
  0.7 1.1 %copy-start = (f32[1,3,90,512]{3,0,2,1:T(1,128)S(1)}, f32[1,3,90,512]{3,0,2,1:T(1,128)}, u32[]{:S(2)}) copy-start(f32[1,3,90,512]{3,0,2,1:T(1,128)} %param.11) | copy-start | bytes 1658884
  1.7 12.5 %copy-start.1 = (f32[1,3,90,512]{3,0,2,1:T(1,128)S(1)}, f32[1,3,90,512]{3,0,2,1:T(1,128)}, u32[]{:S(2)}) copy-start(f32[1,3,90,512]{3,0,2,1:T(1,128)} %param.11) | copy-start | bytes 1658884
  2.0 12.3 %copy-start.6 = (s32[6,512]{1,0:T(8,128)S(1)}, s32[6,512]{1,0:T(8,128)}, u32[]{:S(2)}) copy-start(s32[6,512]{1,0:T(8,128)} %near_ref.1) | copy-start | bytes 36868
  2.0 20.0 %collective-permute-start.2 = (f32[360,128]{1,0:T(8,128)S(1)}, f32[360,128]{1,0:T(8,128)S(1)}, u32[]{:S(2)}, u32[]{:S(2)}) collective-permute-start(f32[360,128]{1,0:T(8,128)S(1)} %get-tuple-element.30), channel_id=1, source_target_pairs={{0,8},{8,0},{16,16},{24,24},{1,9},{9,1},{17,17},{25,25},{2,10},{10... | collective-permute-start | bytes 552968 | tf_op jit(solution)/shard_map/ppermute | solution.py:202
  4.4 17.6 %collective-permute-start.3 = (f32[360,128]{1,0:T(8,128)S(1)}, f32[360,128]{1,0:T(8,128)S(1)}, u32[]{:S(2)}, u32[]{:S(2)}) collective-permute-start(f32[360,128]{1,0:T(8,128)S(1)} %get-tuple-element.31), channel_id=1, source_target_pairs={{0,16},{8,8},{16,0},{24,24},{1,17},{9,9},{17,1},{25,25},{2,18},{10... | collective-permute-start | bytes 552968 | tf_op jit(solution)/shard_map/ppermute | solution.py:202
  7.5 14.5 %collective-permute-start.4 = (f32[360,128]{1,0:T(8,128)S(1)}, f32[360,128]{1,0:T(8,128)S(1)}, u32[]{:S(2)}, u32[]{:S(2)}) collective-permute-start(f32[360,128]{1,0:T(8,128)S(1)} %get-tuple-element.32), channel_id=1, source_target_pairs={{0,24},{8,8},{16,16},{24,0},{1,25},{9,9},{17,17},{25,1},{2,26},{10... | collective-permute-start | bytes 552968 | tf_op jit(solution)/shard_map/ppermute | solution.py:202
  9.5 12.5 %collective-permute-start = (bf16[270,128]{1,0:T(8,128)(2,1)S(1)}, bf16[270,128]{1,0:T(8,128)(2,1)S(1)}, u32[]{:S(2)}, u32[]{:S(2)}) collective-permute-start(bf16[270,128]{1,0:T(8,128)(2,1)S(1)} %get-tuple-element.28), channel_id=1, source_target_pairs={{0,1},{1,2},{2,3},{3,4},{4,5},{5,6},{6,7},{7,0},{8,9},{9,10},{10,1... | collective-permute-start | bytes 207368 | tf_op jit(solution)/shard_map/ppermute | solution.py:216
  11.0 10.9 %collective-permute-start.1 = (bf16[270,128]{1,0:T(8,128)(2,1)S(1)}, bf16[270,128]{1,0:T(8,128)(2,1)S(1)}, u32[]{:S(2)}, u32[]{:S(2)}) collective-permute-start(bf16[270,128]{1,0:T(8,128)(2,1)S(1)} %get-tuple-element.29), channel_id=1, source_target_pairs={{1,0},{2,1},{3,2},{4,3},{5,4},{6,5},{7,6},{0,7},{9,8},{10,9},{11,1... | collective-permute-start | bytes 207368 | tf_op jit(solution)/shard_map/ppermute | solution.py:217
  14.2 0.7 %copy-start.11 = (f32[512]{0:T(512)S(1)}, f32[512]{0:T(512)}, u32[]{:S(2)}) copy-start(f32[512]{0:T(512)} %param.19) | copy-start | bytes 6148
  14.2 0.7 %copy-start.10 = (f32[512]{0:T(512)S(1)}, f32[512]{0:T(512)}, u32[]{:S(2)}) copy-start(f32[512]{0:T(512)} %param.17) | copy-start | bytes 6148
  14.2 0.7 %copy-start.12 = (f32[90]{0:T(128)S(1)}, f32[90]{0:T(128)}, u32[]{:S(2)}) copy-start(f32[90]{0:T(128)} %param.21) | copy-start | bytes 1084
  14.9 1.0 %copy-start.2 = (bf16[512,512]{1,0:T(8,128)(2,1)S(1)}, bf16[512,512]{1,0:T(8,128)(2,1)}, u32[]{:S(2)}) copy-start(bf16[512,512]{1,0:T(8,128)(2,1)} %w_mid_ref.3) | copy-start | bytes 1572868
  16.0 0.9 %copy-start.4 = (bf16[90,512]{1,0:T(8,128)(2,1)S(1)}, bf16[90,512]{1,0:T(8,128)(2,1)}, u32[]{:S(2)}) copy-start(bf16[90,512]{1,0:T(8,128)(2,1)} %w_out_ref.3) | copy-start | bytes 276484
  16.9 1.0 %copy-start.5 = (bf16[512,270]{0,1:T(8,128)(2,1)S(1)}, bf16[512,270]{0,1:T(8,128)(2,1)}, u32[]{:S(2)}) copy-start(bf16[512,270]{0,1:T(8,128)(2,1)} %param.16) | copy-start | bytes 829444
  17.8 0.7 %copy-start.7 = (f32[6,512]{1,0:T(8,128)S(1)}, f32[6,512]{1,0:T(8,128)}, u32[]{:S(2)}) copy-start(f32[6,512]{1,0:T(8,128)} %diff_ref.1) | copy-start | bytes 36868
  18.6 0.7 %copy-start.8 = (f32[6,512]{1,0:T(8,128)S(1)}, f32[6,512]{1,0:T(8,128)}, u32[]{:S(2)}) copy-start(f32[6,512]{1,0:T(8,128)} %tran_ref.1) | copy-start | bytes 36868
  22.0 1.0 %copy-start.3 = (bf16[512,512]{1,0:T(8,128)(2,1)S(1)}, bf16[512,512]{1,0:T(8,128)(2,1)}, u32[]{:S(2)}) copy-start(bf16[512,512]{1,0:T(8,128)(2,1)} %w_mid_ref.3) | copy-start | bytes 1572868
  24.2 14.5 %collective-permute-start.9 = (bf16[90,512]{1,0:T(8,128)(2,1)S(1)}, bf16[90,512]{1,0:T(8,128)(2,1)S(1)}, u32[]{:S(2)}, u32[]{:S(2)}) collective-permute-start(bf16[90,512]{1,0:T(8,128)(2,1)S(1)} %second.1), channel_id=1, source_target_pairs={{0,24},{8,8},{16,16},{24,0},{1,25},{9,9},{17,17},{25,1},{2,26},{10... | collective-permute-start | bytes 276488 | tf_op jit(solution)/shard_map/ppermute | solution.py:202
  27.5 11.2 %collective-permute-start.8 = (bf16[90,512]{1,0:T(8,128)(2,1)S(1)}, bf16[90,512]{1,0:T(8,128)(2,1)S(1)}, u32[]{:S(2)}, u32[]{:S(2)}) collective-permute-start(bf16[90,512]{1,0:T(8,128)(2,1)S(1)} %second.1), channel_id=1, source_target_pairs={{0,16},{8,8},{16,0},{24,24},{1,17},{9,9},{17,1},{25,25},{2,18},{10... | collective-permute-start | bytes 276488 | tf_op jit(solution)/shard_map/ppermute | solution.py:202
  29.4 9.3 %collective-permute-start.7 = (bf16[90,512]{1,0:T(8,128)(2,1)S(1)}, bf16[90,512]{1,0:T(8,128)(2,1)S(1)}, u32[]{:S(2)}, u32[]{:S(2)}) collective-permute-start(bf16[90,512]{1,0:T(8,128)(2,1)S(1)} %second.1), channel_id=1, source_target_pairs={{0,8},{8,0},{16,16},{24,24},{1,9},{9,1},{17,17},{25,25},{2,10},{10... | collective-permute-start | bytes 276488 | tf_op jit(solution)/shard_map/ppermute | solution.py:202
  31.3 7.3 %collective-permute-start.5 = (bf16[270,128]{1,0:T(8,128)(2,1)S(1)}, bf16[270,128]{1,0:T(8,128)(2,1)S(1)}, u32[]{:S(2)}, u32[]{:S(2)}) collective-permute-start(bf16[270,128]{1,0:T(8,128)(2,1)S(1)} %get-tuple-element.37), channel_id=1, source_target_pairs={{0,1},{1,2},{2,3},{3,4},{4,5},{5,6},{6,7},{7,0},{8,9},{9,10},{10,1... | collective-permute-start | bytes 207368 | tf_op jit(solution)/shard_map/ppermute | solution.py:236
  31.4 7.3 %collective-permute-start.6 = (bf16[270,128]{1,0:T(8,128)(2,1)S(1)}, bf16[270,128]{1,0:T(8,128)(2,1)S(1)}, u32[]{:S(2)}, u32[]{:S(2)}) collective-permute-start(bf16[270,128]{1,0:T(8,128)(2,1)S(1)} %get-tuple-element.38), channel_id=1, source_target_pairs={{1,0},{2,1},{3,2},{4,3},{5,4},{6,5},{7,6},{0,7},{9,8},{10,9},{11,1... | collective-permute-start | bytes 207368 | tf_op jit(solution)/shard_map/ppermute | solution.py:237

commit v2 on v1

v2 whole, which is shorter than its diff:
```python
import math

import jax
import jax.numpy as jnp
from jax import lax
from jax.experimental import pallas as pl
from jax.experimental.pallas import tpu as pltpu
from jax.sharding import PartitionSpec as P

heat_gain = 0.5
bf16, f32, i16 = jnp.bfloat16, jnp.float32, jnp.int16

plan0 = ("HBA", "BHA", "BAH")
plan1 = ("HBA", "BHA", "BAH")


def dot(a, b):
    return jnp.dot(a, b, preferred_element_type=f32)


def split(values):
    high = values.astype(bf16)
    return high, (values - high.astype(f32)).astype(bf16)


def position(quarter):
    return lax.axis_index("grp") // quarter, lax.axis_index("blk") % 2


def load_rows(ref, first, rows, cells):
    tiles = cells // 128
    return jnp.concatenate(
        [ref[pl.ds(first * tiles + tile, rows, stride=tiles), :] for tile in range(tiles)], axis=1
    )


def encode(values):
    largest = jnp.max(jnp.max(jnp.abs(values), axis=0, keepdims=True), axis=1, keepdims=True)
    power = jnp.ceil(jnp.log(jnp.maximum(largest, 1e-30) * (1 / 32000)) * (1 / math.log(2)))
    return jnp.round(values * jnp.exp2(-power)), jnp.broadcast_to(power, (16, 128))


def put(message_ref, codes, power, stride):
    for tile in range(codes.shape[1] // 128):
        message_ref[tile * stride : (tile + 1) * stride, :] = (
            codes[:, tile * 128 : (tile + 1) * 128].astype(jnp.int32).astype(i16)
        )
    message_ref[-16:, :] = power.astype(jnp.int32).astype(i16)


def take(message_ref, stride, tiles):
    scale = jnp.exp2(message_ref[-16:, :].astype(f32)[:1])
    return jnp.concatenate(
        [
            message_ref[tile * stride : (tile + 1) * stride, :].astype(f32) * scale
            for tile in range(tiles)
        ],
        axis=1,
    )


def put_halos(plan, slot, odd, message_refs, codes, power):
    halo = codes.shape[1] // 2
    lower, upper = codes[:, :halo], codes[:, halo:]
    pair = {"A": jnp.where(odd == 0, upper, lower), "B": jnp.where(odd == 0, lower, upper)}
    for group, kinds in enumerate(plan):

        @pl.when(slot == group + 1)
        def _():
            for kind, ref in zip(kinds, message_refs):
                if kind != "H":
                    put(ref, pair[kind], power, codes.shape[0])


def take_halos(plan, slot, odd, message_refs, halo_ref):
    rows = halo_ref.shape[1]
    for group, kinds in enumerate(plan):

        @pl.when(slot == group + 1)
        def _():
            for kind, ref in zip(kinds, message_refs):
                if kind != "H":
                    side = 1 - odd if kind == "A" else odd
                    halo_ref[side] = take(ref, rows, 1)


def pack_kernel(quarter, features, *refs):
    count = (len(refs) - 9) // 2
    held_hbm, rows_hbm, *others_hbm = refs[: count + 2]
    first_ref, second_ref, third_ref, held_ref, rows_ref = refs[count + 2 : count + 7]
    others, (pick_ref, sems) = refs[count + 7 : -2], refs[-2:]
    messages = (first_ref, second_ref, third_ref)
    copies = [
        pltpu.make_async_copy(held_hbm, held_ref.at[pl.ds(0, held_hbm.shape[0])], sems.at[0]),
        pltpu.make_async_copy(rows_hbm, rows_ref, sems.at[1]),
    ]
    for index, (source, target) in enumerate(zip(others_hbm, others)):
        copies.append(pltpu.make_async_copy(source, target, sems.at[index + 2]))
    for copy in copies:
        copy.start()
    slot, odd = position(quarter)
    cells = pick_ref.shape[0]
    rows, halo = held_ref.shape[0] * 128 // cells, rows_ref.shape[1]
    held_ref[held_hbm.shape[0] :, :] = jnp.zeros(
        (held_ref.shape[0] - held_hbm.shape[0], 128), f32
    )
    copies[1].wait()
    cell = lax.broadcasted_iota(jnp.int32, (cells, halo), 0)
    for side in range(2):
        pick_ref[:, side * halo : (side + 1) * halo] = (
            cell == rows_ref[side : side + 1, :]
        ).astype(bf16)
    copies[0].wait()
    levels = features // 3

    @pl.when(slot == 0)
    def _():
        stride = -(-levels // 16) * 16
        for group, kinds in enumerate(plan0):
            codes, power = encode(load_rows(held_ref, group * levels, levels, cells))
            codes = jnp.concatenate([codes, jnp.zeros((stride - levels, cells), f32)], axis=0)
            put(messages[kinds.index("H")], codes, power, stride)

    @pl.when(slot != 0)
    def _():
        high, low = split(load_rows(held_ref, 0, rows, cells))
        codes, power = encode(dot(high, pick_ref[...]) + dot(low, pick_ref[...]))
        put_halos(plan0, slot, odd, messages, codes, power)

    for copy in copies[2:]:
        copy.wait()


def silu(v):
    half = 0.5 * v
    return half + half * jnp.tanh(half)


def network(state, w_in_ref, b_in_ref, w_mid_ref, b_mid_ref, w_out_ref, b_out_ref):
    def bias(ref):
        return jnp.concatenate([ref[...]] * (state.shape[1] // ref.shape[1]), axis=1)

    first = silu(dot(w_in_ref[...], state) + bias(b_in_ref)).astype(bf16)
    second = silu(dot(w_mid_ref[...], first) + bias(b_mid_ref)).astype(bf16)
    return dot(w_out_ref[...], second) + bias(b_out_ref)


def first_kernel(
    held_ref, near_ref, diff_ref, tran_ref, w_in_t_ref, b_in_ref, b_mid_ref, b_out_ref,
    matrix_ref, matrix_low_ref, keep_ref, part_ref, w_in_ref, c_in_ref, c_mid_ref, c_out_ref,
):
    rows, cells = part_ref.shape
    half_tran = 0.5 * tran_ref[...]
    weight = diff_ref[...] - half_tran
    keep = 1.0 - jnp.sum(diff_ref[...] + half_tran, axis=0, keepdims=True)
    keep_ref[...] = keep
    piece = 128
    for start in range(0, matrix_ref.shape[0], piece):
        cell = lax.broadcasted_iota(jnp.int32, (piece, cells), 0) + start
        total = jnp.zeros((piece, cells), f32)
        for edge in range(near_ref.shape[0]):
            total = total + jnp.where(
                cell == near_ref[edge : edge + 1, :], weight[edge : edge + 1, :], 0.0
            )
        matrix_ref[start : start + piece, :], matrix_low_ref[start : start + piece, :] = split(total)
    state = load_rows(held_ref, 0, rows, cells)
    high, low = split(state)
    part_ref[...] = (
        dot(high, matrix_ref[:cells, :])
        + dot(high, matrix_low_ref[:cells, :])
        + dot(low, matrix_ref[:cells, :])
        + state * keep
    )
    features = w_in_t_ref.shape[0]
    w_in_ref[...] = jnp.zeros_like(w_in_ref)
    w_in_ref[:, :features] = w_in_t_ref[...].T
    for row_ref, column_ref in ((b_in_ref, c_in_ref), (b_mid_ref, c_mid_ref), (b_out_ref, c_out_ref)):
        column_ref[...] = jnp.broadcast_to(row_ref[...], (128, row_ref.shape[1])).T


def middle_kernel(
    quarter, first_in, second_in, third_in, pick_ref, part_ref, matrix_ref, matrix_low_ref,
    w_in_ref, b_in_ref, w_mid_ref, b_mid_ref, w_out_ref, b_out_ref,
    first_out, second_out, third_out, state_ref, halo_ref,
):
    slot, odd = position(quarter)
    received, messages = (first_in, second_in, third_in), (first_out, second_out, third_out)
    cells, halo = matrix_ref.shape[1], halo_ref.shape[2]
    levels = w_out_ref.shape[0]
    stride = -(-levels // 16) * 16
    take_halos(plan0, slot, odd, received, halo_ref)
    total = part_ref[...]
    for side in range(2):
        high, low = split(halo_ref[side])
        place = slice(cells + side * halo, cells + (side + 1) * halo)
        total = (
            total
            + dot(high, matrix_ref[place, :])
            + dot(high, matrix_low_ref[place, :])
            + dot(low, matrix_ref[place, :])
        )
    state_ref[...] = total
    for group, kinds in enumerate(plan0):

        @pl.when(slot == group + 1)
        def _():
            heat = take(received[kinds.index("H")], stride, cells // 128)[:levels]
            state_ref[:levels, :] = state_ref[:levels, :] + heat_gain * heat

    state = state_ref[...].astype(bf16)
    codes, power = encode(dot(state, pick_ref[...]))
    put_halos(plan1, slot, odd, messages, codes, power)
    codes, power = encode(
        network(state, w_in_ref, b_in_ref, w_mid_ref, b_mid_ref, w_out_ref, b_out_ref)
    )
    codes = jnp.concatenate([codes, jnp.zeros((stride - levels, cells), f32)], axis=0)
    for group, kinds in enumerate(plan1):

        @pl.when(slot == group + 1)
        def _():
            put(messages[kinds.index("H")], codes, power, stride)


def own_kernel(
    held_ref, state_ref, matrix_ref, keep_ref,
    w_in_ref, b_in_ref, w_mid_ref, b_mid_ref, w_out_ref, b_out_ref, part_ref,
):
    rows, cells = state_ref.shape
    levels = w_out_ref.shape[0]
    start = load_rows(held_ref, 0, rows, cells).astype(bf16)
    heat = network(start, w_in_ref, b_in_ref, w_mid_ref, b_mid_ref, w_out_ref, b_out_ref)
    state = state_ref[...]
    part_ref[...] = dot(state.astype(bf16), matrix_ref[:cells, :]) + state * keep_ref[...]
    part_ref[:levels, :] = part_ref[:levels, :] + heat_gain * heat


def last_kernel(
    quarter, first_in, second_in, third_in, part_ref, matrix_ref, out_ref, halo_ref
):
    slot, odd = position(quarter)
    received = (first_in, second_in, third_in)
    cells, halo = matrix_ref.shape[1], halo_ref.shape[2]
    tiles = cells // 128
    features = out_ref.shape[0] // tiles
    levels = features // 3
    stride = -(-levels // 16) * 16

    def store_rows(first, values):
        for tile in range(tiles):
            out_ref[pl.ds(first * tiles + tile, values.shape[0], stride=tiles), :] = values[
                :, tile * 128 : (tile + 1) * 128
            ]

    @pl.when(slot == 0)
    def _():
        for group, kinds in enumerate(plan1):
            store_rows(group * levels, take(received[kinds.index("H")], stride, tiles)[:levels])

    take_halos(plan1, slot, odd, received, halo_ref)

    @pl.when(slot != 0)
    def _():
        total = part_ref[...]
        for side in range(2):
            place = slice(cells + side * halo, cells + (side + 1) * halo)
            total = total + dot(halo_ref[side].astype(bf16), matrix_ref[place, :])
        store_rows(0, total[:features])


VMEM = pl.BlockSpec(memory_space=pltpu.VMEM)
HBM = pl.BlockSpec(memory_space=pltpu.HBM)


def call(kernel, name, out_shape, *args, place=VMEM, scratch=(), flops=0, limit=16 << 20):
    size = sum(a.size * a.dtype.itemsize for a in args)
    if place is HBM:
        args = [pltpu.with_memory_space_constraint(a, pltpu.HBM) for a in args]
    return pl.pallas_call(
        kernel,
        out_shape=out_shape,
        in_specs=[place] * len(args),
        out_specs=jax.tree.map(lambda _: VMEM, out_shape),
        scratch_shapes=scratch,
        compiler_params=pltpu.CompilerParams(vmem_limit_bytes=limit),
        cost_estimate=pl.CostEstimate(flops=flops, bytes_accessed=size, transcendentals=0),
        name=name,
    )(*args)


def exchange(plan, messages, quarter, blocks):
    def partner(group, block, step):
        slot, place = group // quarter, group % quarter
        kinds = [kinds[step] for kinds in plan]
        if slot == 0:
            return (kinds.index("H") + 1) * quarter + place, block
        kind = kinds[slot - 1]
        if kind == "H":
            return place, block
        up = (block % 2 == 0) == (kind == "A")
        return group, (block + (1 if up else -1)) % blocks

    received = []
    for step, message in enumerate(messages):
        pairs = []
        for group in range(4 * quarter):
            for block in range(blocks):
                to_group, to_block = partner(group, block, step)
                pairs.append((group * blocks + block, to_group * blocks + to_block))
        received.append(lax.ppermute(message, ("grp", "blk"), pairs))
    return received


def body(held, neighbours, send_rows, diffusion, transport, w_in, b_in, w_mid, b_mid, w_out, b_out):
    quarter, blocks = lax.axis_size("grp") // 4, lax.axis_size("blk")
    _, fields, levels, cells = held.shape
    halo, hidden = send_rows.shape[1], w_mid.shape[0]
    features, tiles = fields * levels, cells // 128
    rows = -(-features // 16) * 16
    length = max(-(-levels // 16) * 16 * tiles, rows) + 16

    def shape(*dims, dtype=f32):
        return jax.ShapeDtypeStruct(dims, dtype)

    def like(array):
        return shape(*array.shape, dtype=array.dtype)

    message = shape(length, 128, dtype=i16)
    full = shape(rows, cells)
    matrix_shape = shape(cells + 2 * halo, cells, dtype=bf16)
    halos = pltpu.VMEM((2, rows, halo), f32)
    args = (neighbours, diffusion, transport, w_in.T, b_in[None], b_mid[None], b_out[None], w_mid, w_out)
    *messages, flat, _, near, diff, tran, w_in_t, b_in, b_mid, b_out, w_mid, w_out, pick = call(
        lambda *refs: pack_kernel(quarter, features, *refs), "pack",
        [message] * 3
        + [shape(rows * tiles, 128), like(send_rows)]
        + [like(array) for array in args]
        + [shape(cells, 2 * halo, dtype=bf16)],
        held.reshape(features * tiles, 128), send_rows, *args,
        place=HBM, scratch=[pltpu.SemaphoreType.DMA((2 + len(args),))],
    )
    received = exchange(plan0, messages, quarter, blocks)
    matrix, matrix_low, keep, part1, w_in, c_in, c_mid, c_out = call(
        first_kernel, "first",
        [
            matrix_shape, matrix_shape, shape(1, cells), full,
            shape(hidden, rows, dtype=bf16), shape(hidden, 128), shape(hidden, 128), shape(levels, 128),
        ],
        flat, near, diff, tran, w_in_t, b_in, b_mid, b_out, flops=2 * cells * hidden * hidden,
    )
    weights = (w_in, c_in, w_mid, c_mid, w_out, c_out)
    *messages, state1 = call(
        lambda *refs: middle_kernel(quarter, *refs), "middle",
        [message] * 3 + [full],
        *received, pick, part1, matrix, matrix_low, *weights,
        scratch=[halos], flops=2 * cells * hidden * hidden,
    )
    received = exchange(plan1, messages, quarter, blocks)
    part2 = call(
        own_kernel, "own", full, flat, state1, matrix, keep, *weights, flops=2 * cells * hidden * hidden
    )
    out = call(
        lambda *refs: last_kernel(quarter, *refs), "last", shape(features * tiles, 128),
        *received, part2, matrix, scratch=[halos], flops=2 * rows * cells * 2 * halo,
    )
    return out.reshape(held.shape)


def solution(mesh):
    placed = (
        P("grp", None, None, "blk"),
        P(None, "blk"),
        P(None, "blk"),
        P(None, "blk"),
        P(None, "blk"),
        P(),
        P(),
        P(),
        P(),
        P(),
        P(),
    )
    return jax.shard_map(
        body, mesh=mesh, in_specs=placed, out_specs=P("grp", None, None, "blk"), check_vma=False
    )
```

time: 40.2 us -> 24.8 us (0.62)
  the two profiles are of different devices: /device:TPU:0 before, /device:TPU:2 now
where the time goes in v2:
time: 24.8 us; the launch traced here: 24.7 us
  Pallas kernels  8.82 us (36%)
  waiting for transfers between devices  8.79 us (35%)
  starting transfers between devices  7.01 us (28%)
    pallas_call x5, Pallas kernels, call(): pl.pallas_call(kernel, out_shape=out_shape, in_specs=[place] * len(args),...  8.82 us
    ppermute x6, waiting for transfers between devices, exchange(): received.append(lax.ppermute(message, ('grp', 'blk'), pairs))  8.79 us
    ppermute x6, starting transfers between devices, exchange(): received.append(lax.ppermute(message, ('grp', 'blk'), pairs))  7.01 us
  transfers between devices with their start and end apart: 6, of which 5 were waited for; matrix products, arithmetic and copies ran while one was open for 0% of the time, Pallas kernels for 12%

profile of v2, /device:TPU:2, one launch (start us, length us, event | category | flops | bytes accessed | tf_op | source)
XLA Modules:
  0.0 24.7 jit_solution(1496674563543612682)
XLA Ops:
  0.0 2.2 %pack.1 = (s16[400,128]{1,0:T(8,128)(2,1)S(1)}, s16[400,128]{1,0:T(8,128)(2,1)S(1)}, s16[400,128]{1,0:T(8,128)(2,1)S(1)}, f32[1088,128]{1,0:T(8,128)S(1)}, s32[2...) custom-call(f32[1080,128]{1,0:T(8,128)} %bitcast.6, ...), custom_call_target="tpu_custom_call" | custom-call | bytes 1488232 | tf_op jit(solution)/shard_map/pack/pallas_call | solution.py:278
  2.2 4.6 %collective-permute-start = (s16[400,128]{1,0:T(8,128)(2,1)S(1)}, s16[400,128]{1,0:T(8,128)(2,1)S(1)}, u32[]{:S(2)}, u32[]{:S(2)}) collective-permute-start(s16[400,128]{1,0:T(8,128)(2,1)S(1)} %get-tuple-element.31), channel_id=1, source_target_pairs={{0,8},{1,9},{2,10},{3,11},{4,12},{5,13},{6,14},{7,15},{8,0},{9,1},... | collective-permute-start | bytes 307208 | tf_op jit(solution)/shard_map/ppermute | solution.py:309
  6.9 0.0 collective-permute-start.1
  6.9 0.0 collective-permute-start.2
  6.9 1.7 %first.1 = (bf16[768,512]{1,0:T(8,128)(2,1)S(1)}, bf16[768,512]{1,0:T(8,128)(2,1)S(1)}, f32[1,512]{1,0:T(1,128)S(1)}, f32[272,512]{1,0:T(8,128)S(1)}, bf16[512,2...) custom-call(f32[1088,128]{1,0:T(8,128)S(1)} %get-tuple-element.35.held_ref, ...), custom_call_target="tpu_custom_call" | custom-call | flops 268435456 | bytes 874856 | tf_op jit(solution)/shard_map/first/pallas_call | solution.py:278
  8.6 1.2 %collective-permute-done.refs_0_ = s16[400,128]{1,0:T(8,128)(2,1)S(1)} collective-permute-done((s16[400,128]{1,0:T(8,128)(2,1)S(1)}, s16[400,128]{1,0:T(8,128)(2,1)S(1)}, u32[]{:S(2)}, u32[]{:S(2)}) %collective-permute-start) | collective-permute-done | bytes 102432 | tf_op jit(solution)/shard_map/ppermute | solution.py:309
  9.8 1.7 %collective-permute-done.1.refs_1_ = s16[400,128]{1,0:T(8,128)(2,1)S(1)} collective-permute-done((s16[400,128]{1,0:T(8,128)(2,1)S(1)}, s16[400,128]{1,0:T(8,128)(2,1)S(1)}, u32[]{:S(2)}, u32[]{:S(2)}) %collective-permute-start.1) | collective-permute-done | bytes 102432 | tf_op jit(solution)/shard_map/ppermute | solution.py:309
  11.5 0.4 %collective-permute-done.2.refs_2_ = s16[400,128]{1,0:T(8,128)(2,1)S(1)} collective-permute-done((s16[400,128]{1,0:T(8,128)(2,1)S(1)}, s16[400,128]{1,0:T(8,128)(2,1)S(1)}, u32[]{:S(2)}, u32[]{:S(2)}) %collective-permute-start.2) | collective-permute-done | bytes 102432 | tf_op jit(solution)/shard_map/ppermute | solution.py:309
  11.9 2.4 %middle.1 = (s16[400,128]{1,0:T(8,128)(2,1)S(1)}, s16[400,128]{1,0:T(8,128)(2,1)S(1)}, s16[400,128]{1,0:T(8,128)(2,1)S(1)}, f32[272,512]{1,0:T(8,128)S(1)}) custom-call(s16[400,128]{1,0:T(8,128)(2,1)S(1)} %collective-permute-done.refs_0_, s16[400,128]{1,0:T(8,128)(2,1)S(1)} %collective-permute-done.1.refs_1_, ...), custom_call_target="tpu_custom_call" | custom-call | flops 268435456 | bytes 4164608 | tf_op jit(solution)/shard_map/middle/pallas_call | solution.py:278
  14.4 2.4 %collective-permute-start.3 = (s16[400,128]{1,0:T(8,128)(2,1)S(1)}, s16[400,128]{1,0:T(8,128)(2,1)S(1)}, u32[]{:S(2)}, u32[]{:S(2)}) collective-permute-start(s16[400,128]{1,0:T(8,128)(2,1)S(1)} %get-tuple-element.52), channel_id=1, source_target_pairs={{0,8},{1,9},{2,10},{3,11},{4,12},{5,13},{6,14},{7,15},{8,0},{9,1},... | collective-permute-start | bytes 307208 | tf_op jit(solution)/shard_map/ppermute | solution.py:309
  16.7 0.0 collective-permute-start.4
  16.7 0.0 collective-permute-start.5
  16.8 1.3 %own.1.refs_3_ = f32[272,512]{1,0:T(8,128)S(1)} custom-call(f32[1088,128]{1,0:T(8,128)S(1)} %get-tuple-element.35.held_ref, f32[272,512]{1,0:T(8,128)S(1)} %get-tuple-element.55.state_ref, bf16[768,512]{1,0:T(8,128)(2,1)S(1)} %get-tuple-element.44.refs_5_.matrix_ref.refs_4_, f32[1,512]{1,0:T(1,128)S(1)} %get-tuple-element.56.keep_ref, ...), custom_call_target="tpu_custom_call" | custom-call | flops 268435456 | bytes 3367936 | tf_op jit(solution)/shard_map/own/pallas_call | solution.py:278
  18.1 4.5 %collective-permute-done.3.refs_0_ = s16[400,128]{1,0:T(8,128)(2,1)S(1)} collective-permute-done((s16[400,128]{1,0:T(8,128)(2,1)S(1)}, s16[400,128]{1,0:T(8,128)(2,1)S(1)}, u32[]{:S(2)}, u32[]{:S(2)}) %collective-permute-start.3) | collective-permute-done | bytes 102432 | tf_op jit(solution)/shard_map/ppermute | solution.py:309
  22.5 0.0 collective-permute-done.4.refs_1_
  22.5 1.0 %collective-permute-done.5.refs_2_ = s16[400,128]{1,0:T(8,128)(2,1)S(1)} collective-permute-done((s16[400,128]{1,0:T(8,128)(2,1)S(1)}, s16[400,128]{1,0:T(8,128)(2,1)S(1)}, u32[]{:S(2)}, u32[]{:S(2)}) %collective-permute-start.5) | collective-permute-done | bytes 102432 | tf_op jit(solution)/shard_map/ppermute | solution.py:309
  23.5 1.1 %last.1 = f32[1080,128]{1,0:T(8,128)} custom-call(s16[400,128]{1,0:T(8,128)(2,1)S(1)} %collective-permute-done.3.refs_0_, s16[400,128]{1,0:T(8,128)(2,1)S(1)} %collective-permute-done.4.refs_1_, s16[400,128]{1,0:T(8,128)(2,1)S(1)} %collective-permute-done.5.refs_2_, f32[272,512]{1,0:T(8,128)S(1)} %own.1.refs_3_, ...), custom_call_target="tpu_custom_call" | custom-call | flops 71303168 | bytes 1650688 | tf_op jit(solution)/shard_map/last/pallas_call | solution.py:278
Async XLA Ops:
  2.2 7.6 %collective-permute-start = (s16[400,128]{1,0:T(8,128)(2,1)S(1)}, s16[400,128]{1,0:T(8,128)(2,1)S(1)}, u32[]{:S(2)}, u32[]{:S(2)}) collective-permute-start(s16[400,128]{1,0:T(8,128)(2,1)S(1)} %get-tuple-element.31), channel_id=1, source_target_pairs={{0,8},{1,9},{2,10},{3,11},{4,12},{5,13},{6,14},{7,15},{8,0},{9,1},... | collective-permute-start | bytes 307208 | tf_op jit(solution)/shard_map/ppermute | solution.py:309
  6.9 4.7 %collective-permute-start.1 = (s16[400,128]{1,0:T(8,128)(2,1)S(1)}, s16[400,128]{1,0:T(8,128)(2,1)S(1)}, u32[]{:S(2)}, u32[]{:S(2)}) collective-permute-start(s16[400,128]{1,0:T(8,128)(2,1)S(1)} %get-tuple-element.32), channel_id=1, source_target_pairs={{0,16},{1,17},{2,18},{3,19},{4,20},{5,21},{6,22},{7,23},{8,15},{9,... | collective-permute-start | bytes 307208 | tf_op jit(solution)/shard_map/ppermute | solution.py:309
  6.9 5.1 %collective-permute-start.2 = (s16[400,128]{1,0:T(8,128)(2,1)S(1)}, s16[400,128]{1,0:T(8,128)(2,1)S(1)}, u32[]{:S(2)}, u32[]{:S(2)}) collective-permute-start(s16[400,128]{1,0:T(8,128)(2,1)S(1)} %get-tuple-element.33), channel_id=1, source_target_pairs={{0,24},{1,25},{2,26},{3,27},{4,28},{5,29},{6,30},{7,31},{8,9},{9,8... | collective-permute-start | bytes 307208 | tf_op jit(solution)/shard_map/ppermute | solution.py:309
  14.4 8.2 %collective-permute-start.3 = (s16[400,128]{1,0:T(8,128)(2,1)S(1)}, s16[400,128]{1,0:T(8,128)(2,1)S(1)}, u32[]{:S(2)}, u32[]{:S(2)}) collective-permute-start(s16[400,128]{1,0:T(8,128)(2,1)S(1)} %get-tuple-element.52), channel_id=1, source_target_pairs={{0,8},{1,9},{2,10},{3,11},{4,12},{5,13},{6,14},{7,15},{8,0},{9,1},... | collective-permute-start | bytes 307208 | tf_op jit(solution)/shard_map/ppermute | solution.py:309
  16.7 5.8 %collective-permute-start.4 = (s16[400,128]{1,0:T(8,128)(2,1)S(1)}, s16[400,128]{1,0:T(8,128)(2,1)S(1)}, u32[]{:S(2)}, u32[]{:S(2)}) collective-permute-start(s16[400,128]{1,0:T(8,128)(2,1)S(1)} %get-tuple-element.53), channel_id=1, source_target_pairs={{0,16},{1,17},{2,18},{3,19},{4,20},{5,21},{6,22},{7,23},{8,15},{9,... | collective-permute-start | bytes 307208 | tf_op jit(solution)/shard_map/ppermute | solution.py:309
  16.7 6.8 %collective-permute-start.5 = (s16[400,128]{1,0:T(8,128)(2,1)S(1)}, s16[400,128]{1,0:T(8,128)(2,1)S(1)}, u32[]{:S(2)}, u32[]{:S(2)}) collective-permute-start(s16[400,128]{1,0:T(8,128)(2,1)S(1)} %get-tuple-element.54), channel_id=1, source_target_pairs={{0,24},{1,25},{2,26},{3,27},{4,28},{5,29},{6,30},{7,31},{8,9},{9,8... | collective-permute-start | bytes 307208 | tf_op jit(solution)/shard_map/ppermute | solution.py:309

commit v3 on v2

--- a/solution.py
+++ b/solution.py
@@ -10,8 +10,8 @@
 heat_gain = 0.5
 bf16, f32, i16 = jnp.bfloat16, jnp.float32, jnp.int16
 
-plan0 = ("HBA", "BHA", "BAH")
-plan1 = ("HBA", "BHA", "BAH")
+plan0 = ("HAB", "AHB", "ABH")
+plan1 = ("HAB", "AHB", "ABH")
 
 
 def dot(a, b):
@@ -68,7 +68,7 @@
         @pl.when(slot == group + 1)
         def _():
             for kind, ref in zip(kinds, message_refs):
-                if kind != "H":
+                if kind in pair:
                     put(ref, pair[kind], power, codes.shape[0])
 
 
@@ -79,17 +79,17 @@
         @pl.when(slot == group + 1)
         def _():
             for kind, ref in zip(kinds, message_refs):
-                if kind != "H":
+                if kind in ("A", "B"):
                     side = 1 - odd if kind == "A" else odd
                     halo_ref[side] = take(ref, rows, 1)
 
 
 def pack_kernel(quarter, features, *refs):
-    count = (len(refs) - 9) // 2
+    steps = len(plan0[0])
+    count = (len(refs) - steps - 6) // 2
     held_hbm, rows_hbm, *others_hbm = refs[: count + 2]
-    first_ref, second_ref, third_ref, held_ref, rows_ref = refs[count + 2 : count + 7]
-    others, (pick_ref, sems) = refs[count + 7 : -2], refs[-2:]
-    messages = (first_ref, second_ref, third_ref)
+    *messages, held_ref, rows_ref = refs[count + 2 : count + steps + 4]
+    others, (pick_ref, sems) = refs[count + steps + 4 : -2], refs[-2:]
     copies = [
         pltpu.make_async_copy(held_hbm, held_ref.at[pl.ds(0, held_hbm.shape[0])], sems.at[0]),
         pltpu.make_async_copy(rows_hbm, rows_ref, sems.at[1]),
@@ -179,12 +179,11 @@
 
 
 def middle_kernel(
-    quarter, first_in, second_in, third_in, pick_ref, part_ref, matrix_ref, matrix_low_ref,
+    quarter, received, pick_ref, part_ref, matrix_ref, matrix_low_ref,
     w_in_ref, b_in_ref, w_mid_ref, b_mid_ref, w_out_ref, b_out_ref,
-    first_out, second_out, third_out, state_ref, halo_ref,
+    messages, state_ref, halo_ref,
 ):
     slot, odd = position(quarter)
-    received, messages = (first_in, second_in, third_in), (first_out, second_out, third_out)
     cells, halo = matrix_ref.shape[1], halo_ref.shape[2]
     levels = w_out_ref.shape[0]
     stride = -(-levels // 16) * 16
@@ -234,11 +233,8 @@
     part_ref[:levels, :] = part_ref[:levels, :] + heat_gain * heat
 
 
-def last_kernel(
-    quarter, first_in, second_in, third_in, part_ref, matrix_ref, out_ref, halo_ref
-):
+def last_kernel(quarter, received, part_ref, matrix_ref, out_ref, halo_ref):
     slot, odd = position(quarter)
-    received = (first_in, second_in, third_in)
     cells, halo = matrix_ref.shape[1], halo_ref.shape[2]
     tiles = cells // 128
     features = out_ref.shape[0] // tiles
@@ -291,12 +287,12 @@
     def partner(group, block, step):
         slot, place = group // quarter, group % quarter
         kinds = [kinds[step] for kinds in plan]
-        if slot == 0:
+        if slot == 0 and "H" in kinds:
             return (kinds.index("H") + 1) * quarter + place, block
-        kind = kinds[slot - 1]
+        kind = kinds[slot - 1] if slot else "a"
         if kind == "H":
             return place, block
-        up = (block % 2 == 0) == (kind == "A")
+        up = (block % 2 == 0) == (kind != "B")
         return group, (block + (1 if up else -1)) % blocks
 
     received = []
@@ -328,10 +324,11 @@
     full = shape(rows, cells)
     matrix_shape = shape(cells + 2 * halo, cells, dtype=bf16)
     halos = pltpu.VMEM((2, rows, halo), f32)
+    count0, count1 = len(plan0[0]), len(plan1[0])
     args = (neighbours, diffusion, transport, w_in.T, b_in[None], b_mid[None], b_out[None], w_mid, w_out)
     *messages, flat, _, near, diff, tran, w_in_t, b_in, b_mid, b_out, w_mid, w_out, pick = call(
         lambda *refs: pack_kernel(quarter, features, *refs), "pack",
-        [message] * 3
+        [message] * len(plan0[0])
         + [shape(rows * tiles, 128), like(send_rows)]
         + [like(array) for array in args]
         + [shape(cells, 2 * halo, dtype=bf16)],
@@ -349,8 +346,11 @@
     )
     weights = (w_in, c_in, w_mid, c_mid, w_out, c_out)
     *messages, state1 = call(
-        lambda *refs: middle_kernel(quarter, *refs), "middle",
-        [message] * 3 + [full],
+        lambda *refs: middle_kernel(
+            quarter, refs[:count0], *refs[count0 : count0 + 10],
+            refs[count0 + 10 : count0 + 10 + count1], *refs[count0 + 10 + count1 :],
+        ),
+        "middle", [message] * count1 + [full],
         *received, pick, part1, matrix, matrix_low, *weights,
         scratch=[halos], flops=2 * cells * hidden * hidden,
     )
@@ -359,7 +359,7 @@
         own_kernel, "own", full, flat, state1, matrix, keep, *weights, flops=2 * cells * hidden * hidden
     )
     out = call(
-        lambda *refs: last_kernel(quarter, *refs), "last", shape(features * tiles, 128),
+        lambda *refs: last_kernel(quarter, refs[:count1], *refs[count1:]), "last", shape(features * tiles, 128),
         *received, part2, matrix, scratch=[halos], flops=2 * rows * cells * 2 * halo,
     )
     return out.reshape(held.shape)

time: 24.8 us -> 22.5 us (0.907)
  waiting for transfers between devices: 8.79 us -> 4.55 us
  starting transfers between devices: 7.01 us -> 8.88 us
    ppermute x6, waiting for transfers between devices: 8.79 us -> 4.55 us  [exchange(): received.append(lax.ppermute(message, ('grp', 'blk'), pairs))]
    ppermute x6, starting transfers between devices: 7.01 us -> 8.88 us  [exchange(): received.append(lax.ppermute(message, ('grp', 'blk'), pairs))]
  transfers between devices with their start and end apart: 6 -> 6, of which waited for: 5 -> 2; matrix products, arithmetic and copies ran while one was open for 0% -> 0% of each run, Pallas kernels for 12% -> 14%
where the time goes in v3:
time: 22.5 us; the launch traced here: 22.3 us
  starting transfers between devices  8.88 us (39%)
  Pallas kernels  8.83 us (39%)
  waiting for transfers between devices  4.55 us (20%)
    ppermute x6, starting transfers between devices, exchange(): received.append(lax.ppermute(message, ('grp', 'blk'), pairs))  8.88 us
    pallas_call x5, Pallas kernels, call(): pl.pallas_call(kernel, out_shape=out_shape, in_specs=[place] * len(args),...  8.83 us
    ppermute x6, waiting for transfers between devices, exchange(): received.append(lax.ppermute(message, ('grp', 'blk'), pairs))  4.55 us
  transfers between devices with their start and end apart: 6, of which 2 were waited for; matrix products, arithmetic and copies ran while one was open for 0% of the time, Pallas kernels for 14%

profile of v3, /device:TPU:2, one launch (start us, length us, event | category | flops | bytes accessed | tf_op | source)
XLA Modules:
  0.0 22.3 jit_solution(13976469041557599823)
XLA Ops:
  0.0 2.2 %pack.1 = (s16[400,128]{1,0:T(8,128)(2,1)S(1)}, s16[400,128]{1,0:T(8,128)(2,1)S(1)}, s16[400,128]{1,0:T(8,128)(2,1)S(1)}, f32[1088,128]{1,0:T(8,128)S(1)}, s32[2...) custom-call(f32[1080,128]{1,0:T(8,128)} %bitcast.6, ...), custom_call_target="tpu_custom_call" | custom-call | bytes 1488232 | tf_op jit(solution)/shard_map/pack/pallas_call | solution.py:274
  2.2 1.6 %collective-permute-start = (s16[400,128]{1,0:T(8,128)(2,1)S(1)}, s16[400,128]{1,0:T(8,128)(2,1)S(1)}, u32[]{:S(2)}, u32[]{:S(2)}) collective-permute-start(s16[400,128]{1,0:T(8,128)(2,1)S(1)} %get-tuple-element.31), channel_id=1, source_target_pairs={{0,8},{1,9},{2,10},{3,11},{4,12},{5,13},{6,14},{7,15},{8,0},{9,1},... | collective-permute-start | bytes 307208 | tf_op jit(solution)/shard_map/ppermute | solution.py:305
  3.8 0.0 collective-permute-start.1
  3.8 3.5 %collective-permute-start.2 = (s16[400,128]{1,0:T(8,128)(2,1)S(1)}, s16[400,128]{1,0:T(8,128)(2,1)S(1)}, u32[]{:S(2)}, u32[]{:S(2)}) collective-permute-start(s16[400,128]{1,0:T(8,128)(2,1)S(1)} %get-tuple-element.33), channel_id=1, source_target_pairs={{0,24},{1,25},{2,26},{3,27},{4,28},{5,29},{6,30},{7,31},{8,15},{9,... | collective-permute-start | bytes 307208 | tf_op jit(solution)/shard_map/ppermute | solution.py:305
  7.4 1.7 %first.1 = (bf16[768,512]{1,0:T(8,128)(2,1)S(1)}, bf16[768,512]{1,0:T(8,128)(2,1)S(1)}, f32[1,512]{1,0:T(1,128)S(1)}, f32[272,512]{1,0:T(8,128)S(1)}, bf16[512,2...) custom-call(f32[1088,128]{1,0:T(8,128)S(1)} %get-tuple-element.35.held_ref, ...), custom_call_target="tpu_custom_call" | custom-call | flops 268435456 | bytes 874856 | tf_op jit(solution)/shard_map/first/pallas_call | solution.py:274
  9.1 0.0 collective-permute-done.refs_0_
  9.1 0.0 collective-permute-done.1.refs_1_
  9.1 2.1 %collective-permute-done.2.refs_2_ = s16[400,128]{1,0:T(8,128)(2,1)S(1)} collective-permute-done((s16[400,128]{1,0:T(8,128)(2,1)S(1)}, s16[400,128]{1,0:T(8,128)(2,1)S(1)}, u32[]{:S(2)}, u32[]{:S(2)}) %collective-permute-start.2) | collective-permute-done | bytes 102432 | tf_op jit(solution)/shard_map/ppermute | solution.py:305
  11.2 2.4 %middle.1 = (s16[400,128]{1,0:T(8,128)(2,1)S(1)}, s16[400,128]{1,0:T(8,128)(2,1)S(1)}, s16[400,128]{1,0:T(8,128)(2,1)S(1)}, f32[272,512]{1,0:T(8,128)S(1)}) custom-call(s16[400,128]{1,0:T(8,128)(2,1)S(1)} %collective-permute-done.refs_0_, s16[400,128]{1,0:T(8,128)(2,1)S(1)} %collective-permute-done.1.refs_1_, ...), custom_call_target="tpu_custom_call" | custom-call | flops 268435456 | bytes 4164608 | tf_op jit(solution)/shard_map/middle/pallas_call | solution.py:274
  13.6 0.1 collective-permute-start.3
  13.7 0.1 collective-permute-start.4
  13.8 3.6 %collective-permute-start.5 = (s16[400,128]{1,0:T(8,128)(2,1)S(1)}, s16[400,128]{1,0:T(8,128)(2,1)S(1)}, u32[]{:S(2)}, u32[]{:S(2)}) collective-permute-start(s16[400,128]{1,0:T(8,128)(2,1)S(1)} %get-tuple-element.54), channel_id=1, source_target_pairs={{0,24},{1,25},{2,26},{3,27},{4,28},{5,29},{6,30},{7,31},{8,15},{9,... | collective-permute-start | bytes 307208 | tf_op jit(solution)/shard_map/ppermute | solution.py:305
  17.4 1.3 %own.1.refs_3_ = f32[272,512]{1,0:T(8,128)S(1)} custom-call(f32[1088,128]{1,0:T(8,128)S(1)} %get-tuple-element.35.held_ref, f32[272,512]{1,0:T(8,128)S(1)} %get-tuple-element.55.state_ref, bf16[768,512]{1,0:T(8,128)(2,1)S(1)} %get-tuple-element.44.refs_5_.matrix_ref.refs_4_, f32[1,512]{1,0:T(1,128)S(1)} %get-tuple-element.56.keep_ref, ...), custom_call_target="tpu_custom_call" | custom-call | flops 268435456 | bytes 3367936 | tf_op jit(solution)/shard_map/own/pallas_call | solution.py:274
  18.7 0.0 collective-permute-done.3.refs_0_
  18.7 0.0 collective-permute-done.4.refs_1_
  18.7 2.5 %collective-permute-done.5.refs_2_ = s16[400,128]{1,0:T(8,128)(2,1)S(1)} collective-permute-done((s16[400,128]{1,0:T(8,128)(2,1)S(1)}, s16[400,128]{1,0:T(8,128)(2,1)S(1)}, u32[]{:S(2)}, u32[]{:S(2)}) %collective-permute-start.5) | collective-permute-done | bytes 102432 | tf_op jit(solution)/shard_map/ppermute | solution.py:305
  21.2 1.1 %last.1 = f32[1080,128]{1,0:T(8,128)} custom-call(s16[400,128]{1,0:T(8,128)(2,1)S(1)} %collective-permute-done.3.refs_0_, s16[400,128]{1,0:T(8,128)(2,1)S(1)} %collective-permute-done.4.refs_1_, s16[400,128]{1,0:T(8,128)(2,1)S(1)} %collective-permute-done.5.refs_2_, f32[272,512]{1,0:T(8,128)S(1)} %own.1.refs_3_, ...), custom_call_target="tpu_custom_call" | custom-call | flops 71303168 | bytes 1650688 | tf_op jit(solution)/shard_map/last/pallas_call | solution.py:274
Async XLA Ops:
  2.2 6.9 %collective-permute-start = (s16[400,128]{1,0:T(8,128)(2,1)S(1)}, s16[400,128]{1,0:T(8,128)(2,1)S(1)}, u32[]{:S(2)}, u32[]{:S(2)}) collective-permute-start(s16[400,128]{1,0:T(8,128)(2,1)S(1)} %get-tuple-element.31), channel_id=1, source_target_pairs={{0,8},{1,9},{2,10},{3,11},{4,12},{5,13},{6,14},{7,15},{8,0},{9,1},... | collective-permute-start | bytes 307208 | tf_op jit(solution)/shard_map/ppermute | solution.py:305
  3.8 5.3 %collective-permute-start.1 = (s16[400,128]{1,0:T(8,128)(2,1)S(1)}, s16[400,128]{1,0:T(8,128)(2,1)S(1)}, u32[]{:S(2)}, u32[]{:S(2)}) collective-permute-start(s16[400,128]{1,0:T(8,128)(2,1)S(1)} %get-tuple-element.32), channel_id=1, source_target_pairs={{0,16},{1,17},{2,18},{3,19},{4,20},{5,21},{6,22},{7,23},{8,9},{9,8... | collective-permute-start | bytes 307208 | tf_op jit(solution)/shard_map/ppermute | solution.py:305
  3.8 7.4 %collective-permute-start.2 = (s16[400,128]{1,0:T(8,128)(2,1)S(1)}, s16[400,128]{1,0:T(8,128)(2,1)S(1)}, u32[]{:S(2)}, u32[]{:S(2)}) collective-permute-start(s16[400,128]{1,0:T(8,128)(2,1)S(1)} %get-tuple-element.33), channel_id=1, source_target_pairs={{0,24},{1,25},{2,26},{3,27},{4,28},{5,29},{6,30},{7,31},{8,15},{9,... | collective-permute-start | bytes 307208 | tf_op jit(solution)/shard_map/ppermute | solution.py:305
  13.6 5.1 %collective-permute-start.3 = (s16[400,128]{1,0:T(8,128)(2,1)S(1)}, s16[400,128]{1,0:T(8,128)(2,1)S(1)}, u32[]{:S(2)}, u32[]{:S(2)}) collective-permute-start(s16[400,128]{1,0:T(8,128)(2,1)S(1)} %get-tuple-element.52), channel_id=1, source_target_pairs={{0,8},{1,9},{2,10},{3,11},{4,12},{5,13},{6,14},{7,15},{8,0},{9,1},... | collective-permute-start | bytes 307208 | tf_op jit(solution)/shard_map/ppermute | solution.py:305
  13.7 5.0 %collective-permute-start.4 = (s16[400,128]{1,0:T(8,128)(2,1)S(1)}, s16[400,128]{1,0:T(8,128)(2,1)S(1)}, u32[]{:S(2)}, u32[]{:S(2)}) collective-permute-start(s16[400,128]{1,0:T(8,128)(2,1)S(1)} %get-tuple-element.53), channel_id=1, source_target_pairs={{0,16},{1,17},{2,18},{3,19},{4,20},{5,21},{6,22},{7,23},{8,9},{9,8... | collective-permute-start | bytes 307208 | tf_op jit(solution)/shard_map/ppermute | solution.py:305
  13.8 7.4 %collective-permute-start.5 = (s16[400,128]{1,0:T(8,128)(2,1)S(1)}, s16[400,128]{1,0:T(8,128)(2,1)S(1)}, u32[]{:S(2)}, u32[]{:S(2)}) collective-permute-start(s16[400,128]{1,0:T(8,128)(2,1)S(1)} %get-tuple-element.54), channel_id=1, source_target_pairs={{0,24},{1,25},{2,26},{3,27},{4,28},{5,29},{6,30},{7,31},{8,15},{9,... | collective-permute-start | bytes 307208 | tf_op jit(solution)/shard_map/ppermute | solution.py:305

commit v4 on v3

--- a/solution.py
+++ b/solution.py
@@ -34,54 +34,58 @@
     )
 
 
-def encode(values):
+def power_of(values):
     largest = jnp.max(jnp.max(jnp.abs(values), axis=0, keepdims=True), axis=1, keepdims=True)
     power = jnp.ceil(jnp.log(jnp.maximum(largest, 1e-30) * (1 / 32000)) * (1 / math.log(2)))
-    return jnp.round(values * jnp.exp2(-power)), jnp.broadcast_to(power, (16, 128))
-
-
-def put(message_ref, codes, power, stride):
-    for tile in range(codes.shape[1] // 128):
-        message_ref[tile * stride : (tile + 1) * stride, :] = (
-            codes[:, tile * 128 : (tile + 1) * 128].astype(jnp.int32).astype(i16)
-        )
-    message_ref[-16:, :] = power.astype(jnp.int32).astype(i16)
-
-
-def take(message_ref, stride, tiles):
-    scale = jnp.exp2(message_ref[-16:, :].astype(f32)[:1])
+    return jnp.broadcast_to(power, (16, 128))
+
+
+def padded(values, rows):
+    spare = rows - values.shape[0]
+    return jnp.concatenate([values, jnp.zeros((spare, values.shape[1]), f32)], axis=0) if spare else values
+
+
+def to_message(codes, power, length):
+    tiles = [codes[:, at : at + 128] for at in range(0, codes.shape[1], 128)]
+    spare = length - 16 - len(tiles) * codes.shape[0]
+    if spare:
+        tiles.append(jnp.zeros((spare, 128), f32))
+    return jnp.concatenate([*tiles, power], axis=0).astype(jnp.int32).astype(i16)
+
+
+def from_message(message, rows, tiles):
+    values = message.astype(f32)
+    values = values[:-16] * jnp.exp2(values[-16:-15])
+    return jnp.concatenate([values[at * rows : (at + 1) * rows] for at in range(tiles)], axis=1)
+
+
+def halo_messages(odd, codes, power, length):
+    halo = codes.shape[1] // 2
+    lower, upper = (to_message(part, power, length) for part in (codes[:, :halo], codes[:, halo:]))
+    return {"A": jnp.where(odd == 0, upper, lower), "B": jnp.where(odd == 0, lower, upper)}
+
+
+def send(plan, slot, message_refs, messages):
+    for step, ref in enumerate(message_refs):
+        value = messages[plan[0][step]]
+        for group in range(1, len(plan)):
+            value = jnp.where(slot == group + 1, messages[plan[group][step]], value)
+        ref[...] = value
+
+
+def receive(plan, slot, message_refs, kind):
+    value = message_refs[plan[0].index(kind)][...]
+    for group in range(1, len(plan)):
+        value = jnp.where(slot == group + 1, message_refs[plan[group].index(kind)][...], value)
+    return value
+
+
+def receive_halos(plan, slot, odd, message_refs, rows):
+    near = from_message(receive(plan, slot, message_refs, "A"), rows, 1)
+    far = from_message(receive(plan, slot, message_refs, "B"), rows, 1)
     return jnp.concatenate(
-        [
-            message_ref[tile * stride : (tile + 1) * stride, :].astype(f32) * scale
-            for tile in range(tiles)
-        ],
-        axis=1,
-    )
-
-
-def put_halos(plan, slot, odd, message_refs, codes, power):
-    halo = codes.shape[1] // 2
-    lower, upper = codes[:, :halo], codes[:, halo:]
-    pair = {"A": jnp.where(odd == 0, upper, lower), "B": jnp.where(odd == 0, lower, upper)}
-    for group, kinds in enumerate(plan):
-
-        @pl.when(slot == group + 1)
-        def _():
-            for kind, ref in zip(kinds, message_refs):
-                if kind in pair:
-                    put(ref, pair[kind], power, codes.shape[0])
-
-
-def take_halos(plan, slot, odd, message_refs, halo_ref):
-    rows = halo_ref.shape[1]
-    for group, kinds in enumerate(plan):
-
-        @pl.when(slot == group + 1)
-        def _():
-            for kind, ref in zip(kinds, message_refs):
-                if kind in ("A", "B"):
-                    side = 1 - odd if kind == "A" else odd
-                    halo_ref[side] = take(ref, rows, 1)
+        [jnp.where(odd == 0, far, near), jnp.where(odd == 0, near, far)], axis=1
+    )
 
 
 def pack_kernel(quarter, features, *refs):
@@ -100,7 +104,7 @@
         copy.start()
     slot, odd = position(quarter)
     cells = pick_ref.shape[0]
-    rows, halo = held_ref.shape[0] * 128 // cells, rows_ref.shape[1]
+    rows, halo, length = held_ref.shape[0] * 128 // cells, rows_ref.shape[1], messages[0].shape[0]
     held_ref[held_hbm.shape[0] :, :] = jnp.zeros(
         (held_ref.shape[0] - held_hbm.shape[0], 128), f32
     )
@@ -117,15 +121,20 @@
     def _():
         stride = -(-levels // 16) * 16
         for group, kinds in enumerate(plan0):
-            codes, power = encode(load_rows(held_ref, group * levels, levels, cells))
-            codes = jnp.concatenate([codes, jnp.zeros((stride - levels, cells), f32)], axis=0)
-            put(messages[kinds.index("H")], codes, power, stride)
+            heat = load_rows(held_ref, group * levels, levels, cells)
+            power = power_of(heat)
+            messages[kinds.index("H")][...] = to_message(
+                padded(jnp.round(heat * jnp.exp2(-power[:1, :1])), stride), power, length
+            )
 
     @pl.when(slot != 0)
     def _():
-        high, low = split(load_rows(held_ref, 0, rows, cells))
-        codes, power = encode(dot(high, pick_ref[...]) + dot(low, pick_ref[...]))
-        put_halos(plan0, slot, odd, messages, codes, power)
+        state = load_rows(held_ref, 0, rows, cells)
+        power = power_of(state)
+        high, low = split(state)
+        sent = dot(high, pick_ref[...]) + dot(low, pick_ref[...])
+        both = halo_messages(odd, jnp.round(sent * jnp.exp2(-power[:1, :1])), power, length)
+        send(plan0, slot, messages, {**both, "H": both["A"]})
 
     for copy in copies[2:]:
         copy.wait()
@@ -146,9 +155,18 @@
 
 
 def first_kernel(
-    held_ref, near_ref, diff_ref, tran_ref, w_in_t_ref, b_in_ref, b_mid_ref, b_out_ref,
+    w_in_t_hbm, w_mid_hbm, w_out_hbm,
+    held_ref, near_ref, diff_ref, tran_ref, b_in_ref, b_mid_ref, b_out_ref,
     matrix_ref, matrix_low_ref, keep_ref, part_ref, w_in_ref, c_in_ref, c_mid_ref, c_out_ref,
+    w_mid_ref, w_out_ref, w_in_t_ref, sems,
 ):
+    sources = (w_in_t_hbm, w_mid_hbm, w_out_hbm)
+    copies = [
+        pltpu.make_async_copy(source, target, sems.at[index])
+        for index, (source, target) in enumerate(zip(sources, (w_in_t_ref, w_mid_ref, w_out_ref)))
+    ]
+    for copy in copies:
+        copy.start()
     rows, cells = part_ref.shape
     half_tran = 0.5 * tran_ref[...]
     weight = diff_ref[...] - half_tran
@@ -171,6 +189,8 @@
         + dot(low, matrix_ref[:cells, :])
         + state * keep
     )
+    for copy in copies:
+        copy.wait()
     features = w_in_t_ref.shape[0]
     w_in_ref[...] = jnp.zeros_like(w_in_ref)
     w_in_ref[:, :features] = w_in_t_ref[...].T
@@ -181,43 +201,29 @@
 def middle_kernel(
     quarter, received, pick_ref, part_ref, matrix_ref, matrix_low_ref,
     w_in_ref, b_in_ref, w_mid_ref, b_mid_ref, w_out_ref, b_out_ref,
-    messages, state_ref, halo_ref,
+    messages, state_ref,
 ):
     slot, odd = position(quarter)
-    cells, halo = matrix_ref.shape[1], halo_ref.shape[2]
-    levels = w_out_ref.shape[0]
+    rows, cells = state_ref.shape
+    levels, length = w_out_ref.shape[0], messages[0].shape[0]
     stride = -(-levels // 16) * 16
-    take_halos(plan0, slot, odd, received, halo_ref)
-    total = part_ref[...]
-    for side in range(2):
-        high, low = split(halo_ref[side])
-        place = slice(cells + side * halo, cells + (side + 1) * halo)
-        total = (
-            total
-            + dot(high, matrix_ref[place, :])
-            + dot(high, matrix_low_ref[place, :])
-            + dot(low, matrix_ref[place, :])
-        )
-    state_ref[...] = total
-    for group, kinds in enumerate(plan0):
-
-        @pl.when(slot == group + 1)
-        def _():
-            heat = take(received[kinds.index("H")], stride, cells // 128)[:levels]
-            state_ref[:levels, :] = state_ref[:levels, :] + heat_gain * heat
-
+    heat = from_message(receive(plan0, slot, received, "H"), stride, cells // 128)[:levels]
+    high, low = split(receive_halos(plan0, slot, odd, received, rows))
+    state_ref[...] = (
+        part_ref[...]
+        + dot(high, matrix_ref[cells:, :])
+        + dot(high, matrix_low_ref[cells:, :])
+        + dot(low, matrix_ref[cells:, :])
+    )
+    state_ref[:levels, :] = state_ref[:levels, :] + heat_gain * heat
     state = state_ref[...].astype(bf16)
-    codes, power = encode(dot(state, pick_ref[...]))
-    put_halos(plan1, slot, odd, messages, codes, power)
-    codes, power = encode(
-        network(state, w_in_ref, b_in_ref, w_mid_ref, b_mid_ref, w_out_ref, b_out_ref)
-    )
-    codes = jnp.concatenate([codes, jnp.zeros((stride - levels, cells), f32)], axis=0)
-    for group, kinds in enumerate(plan1):
-
-        @pl.when(slot == group + 1)
-        def _():
-            put(messages[kinds.index("H")], codes, power, stride)
+    sent = dot(state, pick_ref[...])
+    power = power_of(sent)
+    out = halo_messages(odd, jnp.round(sent * jnp.exp2(-power[:1, :1])), power, length)
+    heat = network(state, w_in_ref, b_in_ref, w_mid_ref, b_mid_ref, w_out_ref, b_out_ref)
+    power = power_of(heat)
+    out["H"] = to_message(padded(jnp.round(heat * jnp.exp2(-power[:1, :1])), stride), power, length)
+    send(plan1, slot, messages, out)
 
 
 def own_kernel(
@@ -233,9 +239,9 @@
     part_ref[:levels, :] = part_ref[:levels, :] + heat_gain * heat
 
 
-def last_kernel(quarter, received, part_ref, matrix_ref, out_ref, halo_ref):
+def last_kernel(quarter, received, part_ref, matrix_ref, out_ref):
     slot, odd = position(quarter)
-    cells, halo = matrix_ref.shape[1], halo_ref.shape[2]
+    rows, cells = part_ref.shape
     tiles = cells // 128
     features = out_ref.shape[0] // tiles
     levels = features // 3
@@ -250,31 +256,29 @@
     @pl.when(slot == 0)
     def _():
         for group, kinds in enumerate(plan1):
-            store_rows(group * levels, take(received[kinds.index("H")], stride, tiles)[:levels])
-
-    take_halos(plan1, slot, odd, received, halo_ref)
+            heat = from_message(received[kinds.index("H")][...], stride, tiles)
+            store_rows(group * levels, heat[:levels])
 
     @pl.when(slot != 0)
     def _():
-        total = part_ref[...]
-        for side in range(2):
-            place = slice(cells + side * halo, cells + (side + 1) * halo)
-            total = total + dot(halo_ref[side].astype(bf16), matrix_ref[place, :])
-        store_rows(0, total[:features])
+        halos = receive_halos(plan1, slot, odd, received, rows).astype(bf16)
+        store_rows(0, (part_ref[...] + dot(halos, matrix_ref[cells:, :]))[:features])
 
 
 VMEM = pl.BlockSpec(memory_space=pltpu.VMEM)
 HBM = pl.BlockSpec(memory_space=pltpu.HBM)
 
 
-def call(kernel, name, out_shape, *args, place=VMEM, scratch=(), flops=0, limit=16 << 20):
+def call(kernel, name, out_shape, *args, hbm=0, scratch=(), flops=0, limit=16 << 20):
     size = sum(a.size * a.dtype.itemsize for a in args)
-    if place is HBM:
-        args = [pltpu.with_memory_space_constraint(a, pltpu.HBM) for a in args]
+    args = [
+        pltpu.with_memory_space_constraint(a, pltpu.HBM) if index < hbm else a
+        for index, a in enumerate(args)
+    ]
     return pl.pallas_call(
         kernel,
         out_shape=out_shape,
-        in_specs=[place] * len(args),
+        in_specs=[HBM] * hbm + [VMEM] * (len(args) - hbm),
         out_specs=jax.tree.map(lambda _: VMEM, out_shape),
         scratch_shapes=scratch,
         compiler_params=pltpu.CompilerParams(vmem_limit_bytes=limit),
@@ -323,44 +327,44 @@
     message = shape(length, 128, dtype=i16)
     full = shape(rows, cells)
     matrix_shape = shape(cells + 2 * halo, cells, dtype=bf16)
-    halos = pltpu.VMEM((2, rows, halo), f32)
     count0, count1 = len(plan0[0]), len(plan1[0])
-    args = (neighbours, diffusion, transport, w_in.T, b_in[None], b_mid[None], b_out[None], w_mid, w_out)
-    *messages, flat, _, near, diff, tran, w_in_t, b_in, b_mid, b_out, w_mid, w_out, pick = call(
+    args = (neighbours, diffusion, transport, b_in[None], b_mid[None], b_out[None])
+    *messages, flat, _, near, diff, tran, b_in, b_mid, b_out, pick = call(
         lambda *refs: pack_kernel(quarter, features, *refs), "pack",
         [message] * len(plan0[0])
         + [shape(rows * tiles, 128), like(send_rows)]
         + [like(array) for array in args]
         + [shape(cells, 2 * halo, dtype=bf16)],
         held.reshape(features * tiles, 128), send_rows, *args,
-        place=HBM, scratch=[pltpu.SemaphoreType.DMA((2 + len(args),))],
+        hbm=2 + len(args), scratch=[pltpu.SemaphoreType.DMA((2 + len(args),))],
     )
     received = exchange(plan0, messages, quarter, blocks)
-    matrix, matrix_low, keep, part1, w_in, c_in, c_mid, c_out = call(
+    matrix, matrix_low, keep, part1, w_in, c_in, c_mid, c_out, w_mid, w_out = call(
         first_kernel, "first",
         [
             matrix_shape, matrix_shape, shape(1, cells), full,
             shape(hidden, rows, dtype=bf16), shape(hidden, 128), shape(hidden, 128), shape(levels, 128),
+            like(w_mid), like(w_out),
         ],
-        flat, near, diff, tran, w_in_t, b_in, b_mid, b_out, flops=2 * cells * hidden * hidden,
+        w_in.T, w_mid, w_out, flat, near, diff, tran, b_in, b_mid, b_out,
+        hbm=3, scratch=[pltpu.VMEM((features, hidden), bf16), pltpu.SemaphoreType.DMA((3,))],
+        flops=2 * cells * hidden * hidden,
     )
     weights = (w_in, c_in, w_mid, c_mid, w_out, c_out)
     *messages, state1 = call(
         lambda *refs: middle_kernel(
-            quarter, refs[:count0], *refs[count0 : count0 + 10],
-            refs[count0 + 10 : count0 + 10 + count1], *refs[count0 + 10 + count1 :],
+            quarter, refs[:count0], *refs[count0 : count0 + 10], refs[count0 + 10 : -1], refs[-1]
         ),
         "middle", [message] * count1 + [full],
-        *received, pick, part1, matrix, matrix_low, *weights,
-        scratch=[halos], flops=2 * cells * hidden * hidden,
+        *received, pick, part1, matrix, matrix_low, *weights, flops=2 * cells * hidden * hidden,
     )
     received = exchange(plan1, messages, quarter, blocks)
     part2 = call(
         own_kernel, "own", full, flat, state1, matrix, keep, *weights, flops=2 * cells * hidden * hidden
     )
     out = call(
-        lambda *refs: last_kernel(quarter, refs[:count1], *refs[count1:]), "last", shape(features * tiles, 128),
-        *received, part2, matrix, scratch=[halos], flops=2 * rows * cells * 2 * halo,
+        lambda *refs: last_kernel(quarter, refs[:count1], *refs[count1:]), "last",
+        shape(features * tiles, 128), *received, part2, matrix, flops=2 * rows * cells * 2 * halo,
     )
     return out.reshape(held.shape)
 

time: 22.5 us -> 21.4 us (0.951)
  waiting for transfers between devices: 4.55 us -> 3.71 us
  Pallas kernels: 8.83 us -> 8.56 us
    ppermute x6, waiting for transfers between devices: 4.55 us -> 3.71 us  [exchange(): received.append(lax.ppermute(message, ('grp', 'blk'), pairs))]
    pallas_call x5, Pallas kernels: 8.83 us -> 8.56 us  [call(): pl.pallas_call(kernel, out_shape=out_shape, in_specs=[HBM] * hbm + [VMEM]...]
  transfers between devices with their start and end apart: 6 -> 6, of which waited for: 2 -> 2; matrix products, arithmetic and copies ran while one was open for 0% -> 0% of each run, Pallas kernels for 14% -> 18%
where the time goes in v4:
time: 21.4 us; the launch traced here: 21.2 us
  starting transfers between devices  8.88 us (41%)
  Pallas kernels  8.56 us (40%)
  waiting for transfers between devices  3.71 us (17%)
    ppermute x6, starting transfers between devices, exchange(): received.append(lax.ppermute(message, ('grp', 'blk'), pairs))  8.88 us
    pallas_call x5, Pallas kernels, call(): pl.pallas_call(kernel, out_shape=out_shape, in_specs=[HBM] * hbm + [VMEM]...  8.56 us
    ppermute x6, waiting for transfers between devices, exchange(): received.append(lax.ppermute(message, ('grp', 'blk'), pairs))  3.71 us
  transfers between devices with their start and end apart: 6, of which 2 were waited for; matrix products, arithmetic and copies ran while one was open for 0% of the time, Pallas kernels for 18%

profile of v4, /device:TPU:2, one launch (start us, length us, event | category | flops | bytes accessed | tf_op | source)
XLA Modules:
  0.0 21.2 jit_solution(15975639292358941264)
XLA Ops:
  0.0 2.0 %pack.1 = (s16[400,128]{1,0:T(8,128)(2,1)S(1)}, s16[400,128]{1,0:T(8,128)(2,1)S(1)}, s16[400,128]{1,0:T(8,128)(2,1)S(1)}, f32[1088,128]{1,0:T(8,128)S(1)}, s32[2...) custom-call(f32[1080,128]{1,0:T(8,128)} %bitcast.6, ...), custom_call_target="tpu_custom_call" | custom-call | bytes 595304 | tf_op jit(solution)/shard_map/pack/pallas_call | solution.py:278
  2.0 1.6 %collective-permute-start = (s16[400,128]{1,0:T(8,128)(2,1)S(1)}, s16[400,128]{1,0:T(8,128)(2,1)S(1)}, u32[]{:S(2)}, u32[]{:S(2)}) collective-permute-start(s16[400,128]{1,0:T(8,128)(2,1)S(1)} %get-tuple-element.30), channel_id=1, source_target_pairs={{0,8},{1,9},{2,10},{3,11},{4,12},{5,13},{6,14},{7,15},{8,0},{9,1},... | collective-permute-start | bytes 307208 | tf_op jit(solution)/shard_map/ppermute | solution.py:309
  3.6 0.0 collective-permute-start.1
  3.6 3.5 %collective-permute-start.2 = (s16[400,128]{1,0:T(8,128)(2,1)S(1)}, s16[400,128]{1,0:T(8,128)(2,1)S(1)}, u32[]{:S(2)}, u32[]{:S(2)}) collective-permute-start(s16[400,128]{1,0:T(8,128)(2,1)S(1)} %get-tuple-element.32), channel_id=1, source_target_pairs={{0,24},{1,25},{2,26},{3,27},{4,28},{5,29},{6,30},{7,31},{8,15},{9,... | collective-permute-start | bytes 307208 | tf_op jit(solution)/shard_map/ppermute | solution.py:309
  7.2 2.6 %first.1 = (bf16[768,512]{1,0:T(8,128)(2,1)S(1)}, bf16[768,512]{1,0:T(8,128)(2,1)S(1)}, f32[1,512]{1,0:T(1,128)S(1)}, f32[272,512]{1,0:T(8,128)S(1)}, bf16[512,2...) custom-call(bf16[270,512]{1,0:T(8,128)(2,1)} %bitcast.7, ...), custom_call_target="tpu_custom_call" | custom-call | flops 268435456 | bytes 1491304 | tf_op jit(solution)/shard_map/first/pallas_call | solution.py:278
  9.8 0.0 collective-permute-done.refs_0_
  9.8 0.0 collective-permute-done.1.refs_1_
  9.8 1.2 %collective-permute-done.2.refs_2_ = s16[400,128]{1,0:T(8,128)(2,1)S(1)} collective-permute-done((s16[400,128]{1,0:T(8,128)(2,1)S(1)}, s16[400,128]{1,0:T(8,128)(2,1)S(1)}, u32[]{:S(2)}, u32[]{:S(2)}) %collective-permute-start.2) | collective-permute-done | bytes 102432 | tf_op jit(solution)/shard_map/ppermute | solution.py:309
  11.0 1.6 %middle.1 = (s16[400,128]{1,0:T(8,128)(2,1)S(1)}, s16[400,128]{1,0:T(8,128)(2,1)S(1)}, s16[400,128]{1,0:T(8,128)(2,1)S(1)}, f32[272,512]{1,0:T(8,128)S(1)}) custom-call(s16[400,128]{1,0:T(8,128)(2,1)S(1)} %collective-permute-done.refs_0_, s16[400,128]{1,0:T(8,128)(2,1)S(1)} %collective-permute-done.1.refs_1_, ...), custom_call_target="tpu_custom_call" | custom-call | flops 268435456 | bytes 4164608 | tf_op jit(solution)/shard_map/middle/pallas_call | solution.py:278
  12.6 0.1 collective-permute-start.3
  12.7 0.1 collective-permute-start.4
  12.8 3.6 %collective-permute-start.5 = (s16[400,128]{1,0:T(8,128)(2,1)S(1)}, s16[400,128]{1,0:T(8,128)(2,1)S(1)}, u32[]{:S(2)}, u32[]{:S(2)}) collective-permute-start(s16[400,128]{1,0:T(8,128)(2,1)S(1)} %get-tuple-element.52), channel_id=1, source_target_pairs={{0,24},{1,25},{2,26},{3,27},{4,28},{5,29},{6,30},{7,31},{8,15},{9,... | collective-permute-start | bytes 307208 | tf_op jit(solution)/shard_map/ppermute | solution.py:309
  16.4 1.3 %own.1.refs_3_ = f32[272,512]{1,0:T(8,128)S(1)} custom-call(f32[1088,128]{1,0:T(8,128)S(1)} %get-tuple-element.34.held_ref, f32[272,512]{1,0:T(8,128)S(1)} %get-tuple-element.53.state_ref, bf16[768,512]{1,0:T(8,128)(2,1)S(1)} %get-tuple-element.42.refs_5_.matrix_ref.refs_4_, f32[1,512]{1,0:T(1,128)S(1)} %get-tuple-element.54.keep_ref, ...), custom_call_target="tpu_custom_call" | custom-call | flops 268435456 | bytes 3367936 | tf_op jit(solution)/shard_map/own/pallas_call | solution.py:278
  17.7 0.0 collective-permute-done.3.refs_0_
  17.7 0.0 collective-permute-done.4.refs_1_
  17.7 2.5 %collective-permute-done.5.refs_2_ = s16[400,128]{1,0:T(8,128)(2,1)S(1)} collective-permute-done((s16[400,128]{1,0:T(8,128)(2,1)S(1)}, s16[400,128]{1,0:T(8,128)(2,1)S(1)}, u32[]{:S(2)}, u32[]{:S(2)}) %collective-permute-start.5) | collective-permute-done | bytes 102432 | tf_op jit(solution)/shard_map/ppermute | solution.py:309
  20.2 1.0 %last.1 = f32[1080,128]{1,0:T(8,128)} custom-call(s16[400,128]{1,0:T(8,128)(2,1)S(1)} %collective-permute-done.3.refs_0_, s16[400,128]{1,0:T(8,128)(2,1)S(1)} %collective-permute-done.4.refs_1_, s16[400,128]{1,0:T(8,128)(2,1)S(1)} %collective-permute-done.5.refs_2_, f32[272,512]{1,0:T(8,128)S(1)} %own.1.refs_3_, ...), custom_call_target="tpu_custom_call" | custom-call | flops 71303168 | bytes 1650688 | tf_op jit(solution)/shard_map/last/pallas_call | solution.py:278
Async XLA Ops:
  2.0 7.7 %collective-permute-start = (s16[400,128]{1,0:T(8,128)(2,1)S(1)}, s16[400,128]{1,0:T(8,128)(2,1)S(1)}, u32[]{:S(2)}, u32[]{:S(2)}) collective-permute-start(s16[400,128]{1,0:T(8,128)(2,1)S(1)} %get-tuple-element.30), channel_id=1, source_target_pairs={{0,8},{1,9},{2,10},{3,11},{4,12},{5,13},{6,14},{7,15},{8,0},{9,1},... | collective-permute-start | bytes 307208 | tf_op jit(solution)/shard_map/ppermute | solution.py:309
  3.6 6.1 %collective-permute-start.1 = (s16[400,128]{1,0:T(8,128)(2,1)S(1)}, s16[400,128]{1,0:T(8,128)(2,1)S(1)}, u32[]{:S(2)}, u32[]{:S(2)}) collective-permute-start(s16[400,128]{1,0:T(8,128)(2,1)S(1)} %get-tuple-element.31), channel_id=1, source_target_pairs={{0,16},{1,17},{2,18},{3,19},{4,20},{5,21},{6,22},{7,23},{8,9},{9,8... | collective-permute-start | bytes 307208 | tf_op jit(solution)/shard_map/ppermute | solution.py:309
  3.6 7.4 %collective-permute-start.2 = (s16[400,128]{1,0:T(8,128)(2,1)S(1)}, s16[400,128]{1,0:T(8,128)(2,1)S(1)}, u32[]{:S(2)}, u32[]{:S(2)}) collective-permute-start(s16[400,128]{1,0:T(8,128)(2,1)S(1)} %get-tuple-element.32), channel_id=1, source_target_pairs={{0,24},{1,25},{2,26},{3,27},{4,28},{5,29},{6,30},{7,31},{8,15},{9,... | collective-permute-start | bytes 307208 | tf_op jit(solution)/shard_map/ppermute | solution.py:309
  12.6 5.1 %collective-permute-start.3 = (s16[400,128]{1,0:T(8,128)(2,1)S(1)}, s16[400,128]{1,0:T(8,128)(2,1)S(1)}, u32[]{:S(2)}, u32[]{:S(2)}) collective-permute-start(s16[400,128]{1,0:T(8,128)(2,1)S(1)} %get-tuple-element.50), channel_id=1, source_target_pairs={{0,8},{1,9},{2,10},{3,11},{4,12},{5,13},{6,14},{7,15},{8,0},{9,1},... | collective-permute-start | bytes 307208 | tf_op jit(solution)/shard_map/ppermute | solution.py:309
  12.7 5.0 %collective-permute-start.4 = (s16[400,128]{1,0:T(8,128)(2,1)S(1)}, s16[400,128]{1,0:T(8,128)(2,1)S(1)}, u32[]{:S(2)}, u32[]{:S(2)}) collective-permute-start(s16[400,128]{1,0:T(8,128)(2,1)S(1)} %get-tuple-element.51), channel_id=1, source_target_pairs={{0,16},{1,17},{2,18},{3,19},{4,20},{5,21},{6,22},{7,23},{8,9},{9,8... | collective-permute-start | bytes 307208 | tf_op jit(solution)/shard_map/ppermute | solution.py:309
  12.8 7.4 %collective-permute-start.5 = (s16[400,128]{1,0:T(8,128)(2,1)S(1)}, s16[400,128]{1,0:T(8,128)(2,1)S(1)}, u32[]{:S(2)}, u32[]{:S(2)}) collective-permute-start(s16[400,128]{1,0:T(8,128)(2,1)S(1)} %get-tuple-element.52), channel_id=1, source_target_pairs={{0,24},{1,25},{2,26},{3,27},{4,28},{5,29},{6,30},{7,31},{8,15},{9,... | collective-permute-start | bytes 307208 | tf_op jit(solution)/shard_map/ppermute | solution.py:309

commit v5 on v4

v5 whole, which is shorter than its diff:
```python
import functools
import math

import jax
import jax.numpy as jnp
from jax import lax
from jax.experimental import pallas as pl
from jax.experimental.pallas import tpu as pltpu
from jax.sharding import PartitionSpec as P

heat_gain = 0.5
bf16, f32, i16 = jnp.bfloat16, jnp.float32, jnp.int16

plan0 = ("UDH", "UHD", "HUD")
plan1 = ("UDH", "UHD", "HUD")


def dot(a, b):
    return jnp.dot(a, b, preferred_element_type=f32)


def split(values):
    high = values.astype(bf16)
    return high, (values - high.astype(f32)).astype(bf16)


def slot_of(quarter):
    return lax.axis_index("grp") // quarter


def load_rows(ref, first, rows, cells):
    tiles = cells // 128
    return jnp.concatenate(
        [ref[pl.ds(first * tiles + tile, rows, stride=tiles), :] for tile in range(tiles)], axis=1
    )


def power_of(values):
    largest = jnp.max(jnp.abs(values), axis=0, keepdims=True)
    largest = functools.reduce(
        jnp.maximum, [largest[:, at : at + 128] for at in range(0, values.shape[1], 128)]
    )
    power = jnp.ceil(jnp.log(jnp.maximum(largest, 1e-30) * (1 / 32000)) * (1 / math.log(2)))
    return jnp.broadcast_to(power, (8, 128))


def coded(values, power):
    factor = jnp.exp2(-power[:1])
    return jnp.round(values * jnp.concatenate([factor] * (values.shape[1] // 128), axis=1))


def to_message(codes, power, length):
    tiles = [codes[:, at : at + 128] for at in range(0, codes.shape[1], 128)]
    spare = length - power.shape[0] - len(tiles) * codes.shape[0]
    if spare:
        tiles.append(jnp.zeros((spare, 128), f32))
    return jnp.concatenate([*tiles, power], axis=0).astype(jnp.int32).astype(i16)


def from_message(message, rows, tiles):
    values = message.astype(f32)
    values = values[: rows * tiles] * jnp.exp2(values[-1:])
    return jnp.concatenate([values[at * rows : (at + 1) * rows] for at in range(tiles)], axis=1)


def halo_messages(codes, power, length):
    halo = codes.shape[1] // 2
    return {
        "D": to_message(codes[:, :halo], power, length),
        "U": to_message(codes[:, halo:], power, length),
    }


def send(plan, slot, message_refs, messages):
    for step, ref in enumerate(message_refs):
        value = messages[plan[0][step]]
        for group in range(1, len(plan)):
            value = jnp.where(slot == group + 1, messages[plan[group][step]], value)
        ref[...] = value


def receive(plan, slot, message_refs, kind):
    value = message_refs[plan[0].index(kind)][...]
    for group in range(1, len(plan)):
        value = jnp.where(slot == group + 1, message_refs[plan[group].index(kind)][...], value)
    return value


def receive_halos(plan, slot, message_refs, rows):
    return jnp.concatenate(
        [from_message(receive(plan, slot, message_refs, kind), rows, 1) for kind in "UD"], axis=1
    )


def pack_kernel(quarter, features, *refs):
    steps = len(plan0[0])
    count = (len(refs) - steps - 6) // 2
    held_hbm, rows_hbm, *others_hbm = refs[: count + 2]
    *messages, held_ref, rows_ref = refs[count + 2 : count + steps + 4]
    others, (pick_ref, sems) = refs[count + steps + 4 : -2], refs[-2:]
    copies = [
        pltpu.make_async_copy(held_hbm, held_ref.at[pl.ds(0, held_hbm.shape[0])], sems.at[0]),
        pltpu.make_async_copy(rows_hbm, rows_ref, sems.at[1]),
    ]
    for index, (source, target) in enumerate(zip(others_hbm, others)):
        copies.append(pltpu.make_async_copy(source, target, sems.at[index + 2]))
    for copy in copies:
        copy.start()
    slot = slot_of(quarter)
    cells = pick_ref.shape[0]
    rows, halo, length = held_ref.shape[0] * 128 // cells, rows_ref.shape[1], messages[0].shape[0]
    held_ref[held_hbm.shape[0] :, :] = jnp.zeros(
        (held_ref.shape[0] - held_hbm.shape[0], 128), f32
    )
    copies[1].wait()
    cell = lax.broadcasted_iota(jnp.int32, (cells, halo), 0)
    for side in range(2):
        pick_ref[:, side * halo : (side + 1) * halo] = (
            cell == rows_ref[side : side + 1, :]
        ).astype(bf16)
    copies[0].wait()
    levels = features // 3

    @pl.when(slot == 0)
    def _():
        for group, kinds in enumerate(plan0):
            heat = load_rows(held_ref, group * levels, levels, cells)
            power = power_of(heat)
            messages[kinds.index("H")][...] = to_message(
                coded(heat, power), power, length
            )

    @pl.when(slot != 0)
    def _():
        state = load_rows(held_ref, 0, rows, cells)
        high, low = split(state)
        sent = dot(high, pick_ref[...]) + dot(low, pick_ref[...])
        power = power_of(sent)
        both = halo_messages(coded(sent, power), power, length)
        send(plan0, slot, messages, {**both, "H": both["U"]})

    for copy in copies[2:]:
        copy.wait()


def silu(v):
    half = 0.5 * v
    return half + half * jnp.tanh(half)


def network(state, w_in_ref, b_in_ref, w_mid_ref, b_mid_ref, w_out_ref, b_out_ref):
    def bias(ref):
        return jnp.concatenate([ref[...]] * (state.shape[1] // ref.shape[1]), axis=1)

    first = silu(dot(w_in_ref[...], state) + bias(b_in_ref)).astype(bf16)
    second = silu(dot(w_mid_ref[...], first) + bias(b_mid_ref)).astype(bf16)
    return dot(w_out_ref[...], second) + bias(b_out_ref)


def first_kernel(
    quarter, w_in_t_hbm, w_mid_hbm, w_out_hbm,
    held_ref, near_ref, diff_ref, tran_ref, b_in_ref, b_mid_ref, b_out_ref,
    matrix_ref, matrix_low_ref, keep_ref, part_ref, w_in_ref, c_in_ref, c_mid_ref, c_out_ref,
    w_mid_ref, w_out_ref, w_in_t_ref, sems,
):
    slot = slot_of(quarter)

    @pl.when(slot != 0)
    def _():
        sources = (w_in_t_hbm, w_mid_hbm, w_out_hbm)
        copies = [
            pltpu.make_async_copy(source, target, sems.at[index])
            for index, (source, target) in enumerate(zip(sources, (w_in_t_ref, w_mid_ref, w_out_ref)))
        ]
        for copy in copies:
            copy.start()
        rows, cells = part_ref.shape
        half_tran = 0.5 * tran_ref[...]
        weight = diff_ref[...] - half_tran
        keep = 1.0 - jnp.sum(diff_ref[...] + half_tran, axis=0, keepdims=True)
        keep_ref[...] = keep
        piece = 128
        for start in range(0, matrix_ref.shape[0], piece):
            cell = lax.broadcasted_iota(jnp.int32, (piece, cells), 0) + start
            total = jnp.zeros((piece, cells), f32)
            for edge in range(near_ref.shape[0]):
                total = total + jnp.where(
                    cell == near_ref[edge : edge + 1, :], weight[edge : edge + 1, :], 0.0
                )
            matrix_ref[start : start + piece, :], matrix_low_ref[start : start + piece, :] = split(total)
        state = load_rows(held_ref, 0, rows, cells)
        high, low = split(state)
        part_ref[...] = (
            dot(high, matrix_ref[:cells, :])
            + dot(high, matrix_low_ref[:cells, :])
            + dot(low, matrix_ref[:cells, :])
            + state * keep
        )
        for copy in copies:
            copy.wait()
        features = w_in_t_ref.shape[0]
        w_in_ref[...] = jnp.zeros_like(w_in_ref)
        w_in_ref[:, :features] = w_in_t_ref[...].T
        for row_ref, column_ref in ((b_in_ref, c_in_ref), (b_mid_ref, c_mid_ref), (b_out_ref, c_out_ref)):
            column_ref[...] = jnp.broadcast_to(row_ref[...], (128, row_ref.shape[1])).T


def middle_kernel(
    quarter, received, pick_ref, part_ref, matrix_ref, matrix_low_ref,
    w_in_ref, b_in_ref, w_mid_ref, b_mid_ref, w_out_ref, b_out_ref,
    messages, state_ref,
):
    slot = slot_of(quarter)
    @pl.when(slot != 0)
    def _():
        rows, cells = state_ref.shape
        levels, length = w_out_ref.shape[0], messages[0].shape[0]
        heat = from_message(receive(plan0, slot, received, "H"), levels, cells // 128)
        high, low = split(receive_halos(plan0, slot, received, rows))
        state_ref[...] = (
            part_ref[...]
            + dot(high, matrix_ref[cells:, :])
            + dot(high, matrix_low_ref[cells:, :])
            + dot(low, matrix_ref[cells:, :])
        )
        state_ref[:levels, :] = state_ref[:levels, :] + heat_gain * heat
        state = state_ref[...].astype(bf16)
        sent = dot(state, pick_ref[...])
        power = power_of(sent)
        out = halo_messages(coded(sent, power), power, length)
        heat = network(state, w_in_ref, b_in_ref, w_mid_ref, b_mid_ref, w_out_ref, b_out_ref)
        power = power_of(heat)
        out["H"] = to_message(coded(heat, power), power, length)
        send(plan1, slot, messages, out)


def own_kernel(
    quarter, held_ref, state_ref, matrix_ref, keep_ref,
    w_in_ref, b_in_ref, w_mid_ref, b_mid_ref, w_out_ref, b_out_ref, part_ref,
):
    slot = slot_of(quarter)

    @pl.when(slot != 0)
    def _():
        rows, cells = state_ref.shape
        levels = w_out_ref.shape[0]
        start = load_rows(held_ref, 0, rows, cells).astype(bf16)
        heat = network(start, w_in_ref, b_in_ref, w_mid_ref, b_mid_ref, w_out_ref, b_out_ref)
        state = state_ref[...]
        part_ref[...] = dot(state.astype(bf16), matrix_ref[:cells, :]) + state * keep_ref[...]
        part_ref[:levels, :] = part_ref[:levels, :] + heat_gain * heat


def last_kernel(quarter, received, part_ref, matrix_ref, out_ref):
    slot = slot_of(quarter)
    rows, cells = part_ref.shape
    tiles = cells // 128
    features = out_ref.shape[0] // tiles
    levels = features // 3

    def store_rows(first, values):
        for tile in range(tiles):
            out_ref[pl.ds(first * tiles + tile, values.shape[0], stride=tiles), :] = values[
                :, tile * 128 : (tile + 1) * 128
            ]

    @pl.when(slot == 0)
    def _():
        for group, kinds in enumerate(plan1):
            heat = from_message(received[kinds.index("H")][...], levels, tiles)
            store_rows(group * levels, heat)

    @pl.when(slot != 0)
    def _():
        halos = receive_halos(plan1, slot, received, rows).astype(bf16)
        store_rows(0, (part_ref[...] + dot(halos, matrix_ref[cells:, :]))[:features])


VMEM = pl.BlockSpec(memory_space=pltpu.VMEM)
HBM = pl.BlockSpec(memory_space=pltpu.HBM)


def call(kernel, name, out_shape, *args, hbm=0, scratch=(), flops=0, limit=16 << 20):
    size = sum(a.size * a.dtype.itemsize for a in args)
    args = [
        pltpu.with_memory_space_constraint(a, pltpu.HBM) if index < hbm else a
        for index, a in enumerate(args)
    ]
    return pl.pallas_call(
        kernel,
        out_shape=out_shape,
        in_specs=[HBM] * hbm + [VMEM] * (len(args) - hbm),
        out_specs=jax.tree.map(lambda _: VMEM, out_shape),
        scratch_shapes=scratch,
        compiler_params=pltpu.CompilerParams(vmem_limit_bytes=limit),
        cost_estimate=pl.CostEstimate(flops=flops, bytes_accessed=size, transcendentals=0),
        name=name,
    )(*args)


def exchange(plan, messages, quarter, blocks):
    def partner(group, block, step):
        slot, place = group // quarter, group % quarter
        kinds = [kinds[step] for kinds in plan]
        if slot == 0:
            return (kinds.index("H") + 1) * quarter + place, block
        kind = kinds[slot - 1]
        if kind == "H":
            return place, block
        return group, (block + (1 if kind == "U" else -1)) % blocks

    received = []
    for step, message in enumerate(messages):
        pairs = []
        for group in range(4 * quarter):
            for block in range(blocks):
                to_group, to_block = partner(group, block, step)
                pairs.append((group * blocks + block, to_group * blocks + to_block))
        received.append(lax.ppermute(message, ("grp", "blk"), pairs))
    return received


def body(held, neighbours, send_rows, diffusion, transport, w_in, b_in, w_mid, b_mid, w_out, b_out):
    quarter, blocks = lax.axis_size("grp") // 4, lax.axis_size("blk")
    _, fields, levels, cells = held.shape
    halo, hidden = send_rows.shape[1], w_mid.shape[0]
    features, tiles = fields * levels, cells // 128
    rows = -(-features // 16) * 16
    length = -(-(max(levels * tiles, rows) + 8) // 16) * 16

    def shape(*dims, dtype=f32):
        return jax.ShapeDtypeStruct(dims, dtype)

    def like(array):
        return shape(*array.shape, dtype=array.dtype)

    message = shape(length, 128, dtype=i16)
    full = shape(rows, cells)
    matrix_shape = shape(cells + 2 * halo, cells, dtype=bf16)
    count0, count1 = len(plan0[0]), len(plan1[0])
    args = (neighbours, diffusion, transport, b_in[None], b_mid[None], b_out[None])
    *messages, flat, _, near, diff, tran, b_in, b_mid, b_out, pick = call(
        lambda *refs: pack_kernel(quarter, features, *refs), "pack",
        [message] * len(plan0[0])
        + [shape(rows * tiles, 128), like(send_rows)]
        + [like(array) for array in args]
        + [shape(cells, 2 * halo, dtype=bf16)],
        held.reshape(features * tiles, 128), send_rows, *args,
        hbm=2 + len(args), scratch=[pltpu.SemaphoreType.DMA((2 + len(args),))],
    )
    received = exchange(plan0, messages, quarter, blocks)
    matrix, matrix_low, keep, part1, w_in, c_in, c_mid, c_out, w_mid, w_out = call(
        lambda *refs: first_kernel(quarter, *refs), "first",
        [
            matrix_shape, matrix_shape, shape(1, cells), full,
            shape(hidden, rows, dtype=bf16), shape(hidden, 128), shape(hidden, 128), shape(levels, 128),
            like(w_mid), like(w_out),
        ],
        w_in.T, w_mid, w_out, flat, near, diff, tran, b_in, b_mid, b_out,
        hbm=3, scratch=[pltpu.VMEM((features, hidden), bf16), pltpu.SemaphoreType.DMA((3,))],
        flops=2 * cells * hidden * hidden,
    )
    weights = (w_in, c_in, w_mid, c_mid, w_out, c_out)
    *messages, state1 = call(
        lambda *refs: middle_kernel(
            quarter, refs[:count0], *refs[count0 : count0 + 10], refs[count0 + 10 : -1], refs[-1]
        ),
        "middle", [message] * count1 + [full],
        *received, pick, part1, matrix, matrix_low, *weights, flops=2 * cells * hidden * hidden,
    )
    received = exchange(plan1, messages, quarter, blocks)
    part2 = call(
        lambda *refs: own_kernel(quarter, *refs), "own", full, flat, state1, matrix, keep, *weights, flops=2 * cells * hidden * hidden
    )
    out = call(
        lambda *refs: last_kernel(quarter, refs[:count1], *refs[count1:]), "last",
        shape(features * tiles, 128), *received, part2, matrix, flops=2 * rows * cells * 2 * halo,
    )
    return out.reshape(held.shape)


def solution(mesh):
    placed = (
        P("grp", None, None, "blk"),
        P(None, "blk"),
        P(None, "blk"),
        P(None, "blk"),
        P(None, "blk"),
        P(),
        P(),
        P(),
        P(),
        P(),
        P(),
    )
    return jax.shard_map(
        body, mesh=mesh, in_specs=placed, out_specs=P("grp", None, None, "blk"), check_vma=False
    )
```

time: 21.4 us -> 21.1 us (0.986); the launches traced: 21.2 us -> 20.6 us
  waiting for transfers between devices: 3.71 us -> 1.29 us
  starting transfers between devices: 8.88 us -> 11.2 us
  Pallas kernels: 8.56 us -> 8.07 us
    ppermute x6, waiting for transfers between devices: 3.71 us -> 1.29 us  [exchange(): received.append(lax.ppermute(message, ('grp', 'blk'), pairs))]
    ppermute x6, starting transfers between devices: 8.88 us -> 11.2 us  [exchange(): received.append(lax.ppermute(message, ('grp', 'blk'), pairs))]
    pallas_call x5, Pallas kernels: 8.56 us -> 8.07 us  [call(): pl.pallas_call(kernel, out_shape=out_shape, in_specs=[HBM] * hbm + [VMEM]...]
  transfers between devices with their start and end apart: 6 -> 6, of which waited for: 2 -> 2; matrix products, arithmetic and copies ran while one was open for 0% -> 0% of each run, Pallas kernels for 18% -> 16%
where the time goes in v5:
time: 21.1 us; the launch traced here: 20.6 us
  starting transfers between devices  11.2 us (53%)
  Pallas kernels  8.07 us (38%)
  waiting for transfers between devices  1.29 us (6%)
    ppermute x6, starting transfers between devices, exchange(): received.append(lax.ppermute(message, ('grp', 'blk'), pairs))  11.2 us
    pallas_call x5, Pallas kernels, call(): pl.pallas_call(kernel, out_shape=out_shape, in_specs=[HBM] * hbm + [VMEM]...  8.07 us
    ppermute x6, waiting for transfers between devices, exchange(): received.append(lax.ppermute(message, ('grp', 'blk'), pairs))  1.29 us
  transfers between devices with their start and end apart: 6, of which 2 were waited for; matrix products, arithmetic and copies ran while one was open for 0% of the time, Pallas kernels for 16%

profile of v5, /device:TPU:2, one launch (start us, length us, event | category | flops | bytes accessed | tf_op | source)
XLA Modules:
  0.0 20.6 jit_solution(5669830995119886951)
XLA Ops:
  0.0 2.1 %pack.1 = (s16[368,128]{1,0:T(8,128)(2,1)S(1)}, s16[368,128]{1,0:T(8,128)(2,1)S(1)}, s16[368,128]{1,0:T(8,128)(2,1)S(1)}, f32[1088,128]{1,0:T(8,128)S(1)}, s32[2...) custom-call(f32[1080,128]{1,0:T(8,128)} %bitcast.6, ...), custom_call_target="tpu_custom_call" | custom-call | bytes 595304 | tf_op jit(solution)/shard_map/pack/pallas_call | solution.py:289
  2.1 1.6 %collective-permute-start = (s16[368,128]{1,0:T(8,128)(2,1)S(1)}, s16[368,128]{1,0:T(8,128)(2,1)S(1)}, u32[]{:S(2)}, u32[]{:S(2)}) collective-permute-start(s16[368,128]{1,0:T(8,128)(2,1)S(1)} %get-tuple-element.30), channel_id=1, source_target_pairs={{0,24},{1,25},{2,26},{3,27},{4,28},{5,29},{6,30},{7,31},{8,9},{9,1... | collective-permute-start | bytes 282632 | tf_op jit(solution)/shard_map/ppermute | solution.py:319
  3.7 0.0 collective-permute-start.1
  3.7 4.5 %collective-permute-start.2 = (s16[368,128]{1,0:T(8,128)(2,1)S(1)}, s16[368,128]{1,0:T(8,128)(2,1)S(1)}, u32[]{:S(2)}, u32[]{:S(2)}) collective-permute-start(s16[368,128]{1,0:T(8,128)(2,1)S(1)} %get-tuple-element.32), channel_id=1, source_target_pairs={{0,8},{1,9},{2,10},{3,11},{4,12},{5,13},{6,14},{7,15},{8,0},{9,1},... | collective-permute-start | bytes 282632 | tf_op jit(solution)/shard_map/ppermute | solution.py:319
  8.2 2.1 %first.1 = (bf16[768,512]{1,0:T(8,128)(2,1)S(1)}, bf16[768,512]{1,0:T(8,128)(2,1)S(1)}, f32[1,512]{1,0:T(1,128)S(1)}, f32[272,512]{1,0:T(8,128)S(1)}, bf16[512,2...) custom-call(bf16[270,512]{1,0:T(8,128)(2,1)} %bitcast.7, ...), custom_call_target="tpu_custom_call" | custom-call | flops 268435456 | bytes 1491304 | tf_op jit(solution)/shard_map/first/pallas_call | solution.py:289
  10.3 0.0 collective-permute-done.refs_0_
  10.3 0.0 collective-permute-done.1.refs_1_
  10.3 0.2 collective-permute-done.2.refs_2_
  10.5 1.5 %middle.1 = (s16[368,128]{1,0:T(8,128)(2,1)S(1)}, s16[368,128]{1,0:T(8,128)(2,1)S(1)}, s16[368,128]{1,0:T(8,128)(2,1)S(1)}, f32[272,512]{1,0:T(8,128)S(1)}) custom-call(s16[368,128]{1,0:T(8,128)(2,1)S(1)} %collective-permute-done.refs_0_, s16[368,128]{1,0:T(8,128)(2,1)S(1)} %collective-permute-done.1.refs_1_, ...), custom_call_target="tpu_custom_call" | custom-call | flops 268435456 | bytes 4140032 | tf_op jit(solution)/shard_map/middle/pallas_call | solution.py:289
  12.0 0.5 %collective-permute-start.3 = (s16[368,128]{1,0:T(8,128)(2,1)S(1)}, s16[368,128]{1,0:T(8,128)(2,1)S(1)}, u32[]{:S(2)}, u32[]{:S(2)}) collective-permute-start(s16[368,128]{1,0:T(8,128)(2,1)S(1)} %get-tuple-element.50), channel_id=1, source_target_pairs={{0,24},{1,25},{2,26},{3,27},{4,28},{5,29},{6,30},{7,31},{8,9},{9,1... | collective-permute-start | bytes 282632 | tf_op jit(solution)/shard_map/ppermute | solution.py:319
  12.5 0.5 %collective-permute-start.4 = (s16[368,128]{1,0:T(8,128)(2,1)S(1)}, s16[368,128]{1,0:T(8,128)(2,1)S(1)}, u32[]{:S(2)}, u32[]{:S(2)}) collective-permute-start(s16[368,128]{1,0:T(8,128)(2,1)S(1)} %get-tuple-element.51), channel_id=1, source_target_pairs={{0,16},{1,17},{2,18},{3,19},{4,20},{5,21},{6,22},{7,23},{8,15},{9,... | collective-permute-start | bytes 282632 | tf_op jit(solution)/shard_map/ppermute | solution.py:319
  13.0 4.2 %collective-permute-start.5 = (s16[368,128]{1,0:T(8,128)(2,1)S(1)}, s16[368,128]{1,0:T(8,128)(2,1)S(1)}, u32[]{:S(2)}, u32[]{:S(2)}) collective-permute-start(s16[368,128]{1,0:T(8,128)(2,1)S(1)} %get-tuple-element.52), channel_id=1, source_target_pairs={{0,8},{1,9},{2,10},{3,11},{4,12},{5,13},{6,14},{7,15},{8,0},{9,1},... | collective-permute-start | bytes 282632 | tf_op jit(solution)/shard_map/ppermute | solution.py:319
  17.2 1.3 %own.1.refs_3_ = f32[272,512]{1,0:T(8,128)S(1)} custom-call(f32[1088,128]{1,0:T(8,128)S(1)} %get-tuple-element.34.refs_3_.refs_0_, f32[272,512]{1,0:T(8,128)S(1)} %get-tuple-element.53.refs_1_, bf16[768,512]{1,0:T(8,128)(2,1)S(1)} %get-tuple-element.42.refs_5_.refs_2_.refs_4_, f32[1,512]{1,0:T(1,128)S(1)} %get-tuple-element.54.refs_3_, ...), custom_call_target="tpu_custom_call" | custom-call | flops 268435456 | bytes 3367936 | tf_op jit(solution)/shard_map/own/pallas_call | solution.py:289
  18.5 1.1 %collective-permute-done.3.refs_0_ = s16[368,128]{1,0:T(8,128)(2,1)S(1)} collective-permute-done((s16[368,128]{1,0:T(8,128)(2,1)S(1)}, s16[368,128]{1,0:T(8,128)(2,1)S(1)}, u32[]{:S(2)}, u32[]{:S(2)}) %collective-permute-start.3) | collective-permute-done | bytes 94240 | tf_op jit(solution)/shard_map/ppermute | solution.py:319
  19.6 0.0 collective-permute-done.4.refs_1_
  19.6 0.0 collective-permute-done.5.refs_2_
  19.6 1.0 %last.1 = f32[1080,128]{1,0:T(8,128)} custom-call(s16[368,128]{1,0:T(8,128)(2,1)S(1)} %collective-permute-done.3.refs_0_, s16[368,128]{1,0:T(8,128)(2,1)S(1)} %collective-permute-done.4.refs_1_, s16[368,128]{1,0:T(8,128)(2,1)S(1)} %collective-permute-done.5.refs_2_, f32[272,512]{1,0:T(8,128)S(1)} %own.1.refs_3_, ...), custom_call_target="tpu_custom_call" | custom-call | flops 71303168 | bytes 1626112 | tf_op jit(solution)/shard_map/last/pallas_call | solution.py:289
Async XLA Ops:
  2.1 8.2 %collective-permute-start = (s16[368,128]{1,0:T(8,128)(2,1)S(1)}, s16[368,128]{1,0:T(8,128)(2,1)S(1)}, u32[]{:S(2)}, u32[]{:S(2)}) collective-permute-start(s16[368,128]{1,0:T(8,128)(2,1)S(1)} %get-tuple-element.30), channel_id=1, source_target_pairs={{0,24},{1,25},{2,26},{3,27},{4,28},{5,29},{6,30},{7,31},{8,9},{9,1... | collective-permute-start | bytes 282632 | tf_op jit(solution)/shard_map/ppermute | solution.py:319
  3.7 6.6 %collective-permute-start.1 = (s16[368,128]{1,0:T(8,128)(2,1)S(1)}, s16[368,128]{1,0:T(8,128)(2,1)S(1)}, u32[]{:S(2)}, u32[]{:S(2)}) collective-permute-start(s16[368,128]{1,0:T(8,128)(2,1)S(1)} %get-tuple-element.31), channel_id=1, source_target_pairs={{0,16},{1,17},{2,18},{3,19},{4,20},{5,21},{6,22},{7,23},{8,15},{9,... | collective-permute-start | bytes 282632 | tf_op jit(solution)/shard_map/ppermute | solution.py:319
  3.7 6.8 %collective-permute-start.2 = (s16[368,128]{1,0:T(8,128)(2,1)S(1)}, s16[368,128]{1,0:T(8,128)(2,1)S(1)}, u32[]{:S(2)}, u32[]{:S(2)}) collective-permute-start(s16[368,128]{1,0:T(8,128)(2,1)S(1)} %get-tuple-element.32), channel_id=1, source_target_pairs={{0,8},{1,9},{2,10},{3,11},{4,12},{5,13},{6,14},{7,15},{8,0},{9,1},... | collective-permute-start | bytes 282632 | tf_op jit(solution)/shard_map/ppermute | solution.py:319
  12.0 7.6 %collective-permute-start.3 = (s16[368,128]{1,0:T(8,128)(2,1)S(1)}, s16[368,128]{1,0:T(8,128)(2,1)S(1)}, u32[]{:S(2)}, u32[]{:S(2)}) collective-permute-start(s16[368,128]{1,0:T(8,128)(2,1)S(1)} %get-tuple-element.50), channel_id=1, source_target_pairs={{0,24},{1,25},{2,26},{3,27},{4,28},{5,29},{6,30},{7,31},{8,9},{9,1... | collective-permute-start | bytes 282632 | tf_op jit(solution)/shard_map/ppermute | solution.py:319
  12.5 7.1 %collective-permute-start.4 = (s16[368,128]{1,0:T(8,128)(2,1)S(1)}, s16[368,128]{1,0:T(8,128)(2,1)S(1)}, u32[]{:S(2)}, u32[]{:S(2)}) collective-permute-start(s16[368,128]{1,0:T(8,128)(2,1)S(1)} %get-tuple-element.51), channel_id=1, source_target_pairs={{0,16},{1,17},{2,18},{3,19},{4,20},{5,21},{6,22},{7,23},{8,15},{9,... | collective-permute-start | bytes 282632 | tf_op jit(solution)/shard_map/ppermute | solution.py:319
  13.0 6.6 %collective-permute-start.5 = (s16[368,128]{1,0:T(8,128)(2,1)S(1)}, s16[368,128]{1,0:T(8,128)(2,1)S(1)}, u32[]{:S(2)}, u32[]{:S(2)}) collective-permute-start(s16[368,128]{1,0:T(8,128)(2,1)S(1)} %get-tuple-element.52), channel_id=1, source_target_pairs={{0,8},{1,9},{2,10},{3,11},{4,12},{5,13},{6,14},{7,15},{8,0},{9,1},... | collective-permute-start | bytes 282632 | tf_op jit(solution)/shard_map/ppermute | solution.py:319

commit v6 on v5

--- a/solution.py
+++ b/solution.py
@@ -133,8 +133,7 @@
     @pl.when(slot != 0)
     def _():
         state = load_rows(held_ref, 0, rows, cells)
-        high, low = split(state)
-        sent = dot(high, pick_ref[...]) + dot(low, pick_ref[...])
+        sent = dot(state.astype(bf16), pick_ref[...])
         power = power_of(sent)
         both = halo_messages(coded(sent, power), power, length)
         send(plan0, slot, messages, {**both, "H": both["U"]})
@@ -187,12 +186,15 @@
                 total = total + jnp.where(
                     cell == near_ref[edge : edge + 1, :], weight[edge : edge + 1, :], 0.0
                 )
-            matrix_ref[start : start + piece, :], matrix_low_ref[start : start + piece, :] = split(total)
+            high, low = split(total)
+            matrix_ref[start : start + piece, :] = high
+            if start < cells:
+                matrix_low_ref[start : start + piece, :] = low
         state = load_rows(held_ref, 0, rows, cells)
         high, low = split(state)
         part_ref[...] = (
             dot(high, matrix_ref[:cells, :])
-            + dot(high, matrix_low_ref[:cells, :])
+            + dot(high, matrix_low_ref[...])
             + dot(low, matrix_ref[:cells, :])
             + state * keep
         )
@@ -206,7 +208,7 @@
 
 
 def middle_kernel(
-    quarter, received, pick_ref, part_ref, matrix_ref, matrix_low_ref,
+    quarter, received, pick_ref, part_ref, matrix_ref,
     w_in_ref, b_in_ref, w_mid_ref, b_mid_ref, w_out_ref, b_out_ref,
     messages, state_ref,
 ):
@@ -216,13 +218,8 @@
         rows, cells = state_ref.shape
         levels, length = w_out_ref.shape[0], messages[0].shape[0]
         heat = from_message(receive(plan0, slot, received, "H"), levels, cells // 128)
-        high, low = split(receive_halos(plan0, slot, received, rows))
-        state_ref[...] = (
-            part_ref[...]
-            + dot(high, matrix_ref[cells:, :])
-            + dot(high, matrix_low_ref[cells:, :])
-            + dot(low, matrix_ref[cells:, :])
-        )
+        halos = receive_halos(plan0, slot, received, rows).astype(bf16)
+        state_ref[...] = part_ref[...] + dot(halos, matrix_ref[cells:, :])
         state_ref[:levels, :] = state_ref[:levels, :] + heat_gain * heat
         state = state_ref[...].astype(bf16)
         sent = dot(state, pick_ref[...])
@@ -235,7 +232,7 @@
 
 
 def own_kernel(
-    quarter, held_ref, state_ref, matrix_ref, keep_ref,
+    quarter, held_ref, state_ref, matrix_ref, matrix_low_ref, keep_ref,
     w_in_ref, b_in_ref, w_mid_ref, b_mid_ref, w_out_ref, b_out_ref, part_ref,
 ):
     slot = slot_of(quarter)
@@ -247,7 +244,10 @@
         start = load_rows(held_ref, 0, rows, cells).astype(bf16)
         heat = network(start, w_in_ref, b_in_ref, w_mid_ref, b_mid_ref, w_out_ref, b_out_ref)
         state = state_ref[...]
-        part_ref[...] = dot(state.astype(bf16), matrix_ref[:cells, :]) + state * keep_ref[...]
+        high = state.astype(bf16)
+        part_ref[...] = (
+            dot(high, matrix_ref[:cells, :]) + dot(high, matrix_low_ref[...]) + state * keep_ref[...]
+        )
         part_ref[:levels, :] = part_ref[:levels, :] + heat_gain * heat
 
 
@@ -352,25 +352,27 @@
     matrix, matrix_low, keep, part1, w_in, c_in, c_mid, c_out, w_mid, w_out = call(
         lambda *refs: first_kernel(quarter, *refs), "first",
         [
-            matrix_shape, matrix_shape, shape(1, cells), full,
+            matrix_shape, shape(cells, cells, dtype=bf16), shape(1, cells), full,
             shape(hidden, rows, dtype=bf16), shape(hidden, 128), shape(hidden, 128), shape(levels, 128),
             like(w_mid), like(w_out),
         ],
         w_in.T, w_mid, w_out, flat, near, diff, tran, b_in, b_mid, b_out,
-        hbm=3, scratch=[pltpu.VMEM((features, hidden), bf16), pltpu.SemaphoreType.DMA((3,))],
+        hbm=3, scratch=[
+            pltpu.VMEM((features, hidden), bf16), pltpu.SemaphoreType.DMA((3,)),
+        ],
         flops=2 * cells * hidden * hidden,
     )
     weights = (w_in, c_in, w_mid, c_mid, w_out, c_out)
     *messages, state1 = call(
         lambda *refs: middle_kernel(
-            quarter, refs[:count0], *refs[count0 : count0 + 10], refs[count0 + 10 : -1], refs[-1]
+            quarter, refs[:count0], *refs[count0 : count0 + 9], refs[count0 + 9 : -1], refs[-1]
         ),
         "middle", [message] * count1 + [full],
-        *received, pick, part1, matrix, matrix_low, *weights, flops=2 * cells * hidden * hidden,
+        *received, pick, part1, matrix, *weights, flops=2 * cells * hidden * hidden,
     )
     received = exchange(plan1, messages, quarter, blocks)
     part2 = call(
-        lambda *refs: own_kernel(quarter, *refs), "own", full, flat, state1, matrix, keep, *weights, flops=2 * cells * hidden * hidden
+        lambda *refs: own_kernel(quarter, *refs), "own", full, flat, state1, matrix, matrix_low, keep, *weights, flops=2 * cells * hidden * hidden
     )
     out = call(
         lambda *refs: last_kernel(quarter, refs[:count1], *refs[count1:]), "last",

time: 21.1 us -> 20.8 us (0.986)
  transfers between devices with their start and end apart: 6 -> 6, of which waited for: 2 -> 2; matrix products, arithmetic and copies ran while one was open for 0% -> 0% of each run, Pallas kernels for 16% -> 17%
where the time goes in v6:
time: 20.8 us; the launch traced here: 20.5 us
  starting transfers between devices  11.2 us (54%)
  Pallas kernels  7.93 us (38%)
  waiting for transfers between devices  1.35 us (6%)
    ppermute x6, starting transfers between devices, exchange(): received.append(lax.ppermute(message, ('grp', 'blk'), pairs))  11.2 us
    pallas_call x5, Pallas kernels, call(): pl.pallas_call(kernel, out_shape=out_shape, in_specs=[HBM] * hbm + [VMEM]...  7.93 us
    ppermute x6, waiting for transfers between devices, exchange(): received.append(lax.ppermute(message, ('grp', 'blk'), pairs))  1.35 us
  transfers between devices with their start and end apart: 6, of which 2 were waited for; matrix products, arithmetic and copies ran while one was open for 0% of the time, Pallas kernels for 17%

profile of v6, /device:TPU:2, one launch (start us, length us, event | category | flops | bytes accessed | tf_op | source)
XLA Modules:
  0.0 20.5 jit_solution(16060577606618302655)
XLA Ops:
  0.0 2.0 %pack.1 = (s16[368,128]{1,0:T(8,128)(2,1)S(1)}, s16[368,128]{1,0:T(8,128)(2,1)S(1)}, s16[368,128]{1,0:T(8,128)(2,1)S(1)}, f32[1088,128]{1,0:T(8,128)S(1)}, s32[2...) custom-call(f32[1080,128]{1,0:T(8,128)} %bitcast.6, ...), custom_call_target="tpu_custom_call" | custom-call | bytes 595304 | tf_op jit(solution)/shard_map/pack/pallas_call | solution.py:289
  2.0 1.6 %collective-permute-start = (s16[368,128]{1,0:T(8,128)(2,1)S(1)}, s16[368,128]{1,0:T(8,128)(2,1)S(1)}, u32[]{:S(2)}, u32[]{:S(2)}) collective-permute-start(s16[368,128]{1,0:T(8,128)(2,1)S(1)} %get-tuple-element.30), channel_id=1, source_target_pairs={{0,24},{1,25},{2,26},{3,27},{4,28},{5,29},{6,30},{7,31},{8,9},{9,1... | collective-permute-start | bytes 282632 | tf_op jit(solution)/shard_map/ppermute | solution.py:319
  3.6 0.0 collective-permute-start.1
  3.6 4.5 %collective-permute-start.2 = (s16[368,128]{1,0:T(8,128)(2,1)S(1)}, s16[368,128]{1,0:T(8,128)(2,1)S(1)}, u32[]{:S(2)}, u32[]{:S(2)}) collective-permute-start(s16[368,128]{1,0:T(8,128)(2,1)S(1)} %get-tuple-element.32), channel_id=1, source_target_pairs={{0,8},{1,9},{2,10},{3,11},{4,12},{5,13},{6,14},{7,15},{8,0},{9,1},... | collective-permute-start | bytes 282632 | tf_op jit(solution)/shard_map/ppermute | solution.py:319
  8.1 2.0 %first.1 = (bf16[768,512]{1,0:T(8,128)(2,1)S(1)}, bf16[512,512]{1,0:T(8,128)(2,1)S(1)}, f32[1,512]{1,0:T(1,128)S(1)}, f32[272,512]{1,0:T(8,128)S(1)}, bf16[512,2...) custom-call(bf16[270,512]{1,0:T(8,128)(2,1)} %bitcast.7, ...), custom_call_target="tpu_custom_call" | custom-call | flops 268435456 | bytes 1491304 | tf_op jit(solution)/shard_map/first/pallas_call | solution.py:289
  10.1 0.0 collective-permute-done.refs_0_
  10.2 0.0 collective-permute-done.1.refs_1_
  10.2 0.3 %collective-permute-done.2.refs_2_ = s16[368,128]{1,0:T(8,128)(2,1)S(1)} collective-permute-done((s16[368,128]{1,0:T(8,128)(2,1)S(1)}, s16[368,128]{1,0:T(8,128)(2,1)S(1)}, u32[]{:S(2)}, u32[]{:S(2)}) %collective-permute-start.2) | collective-permute-done | bytes 94240 | tf_op jit(solution)/shard_map/ppermute | solution.py:319
  10.5 1.4 %middle.1 = (s16[368,128]{1,0:T(8,128)(2,1)S(1)}, s16[368,128]{1,0:T(8,128)(2,1)S(1)}, s16[368,128]{1,0:T(8,128)(2,1)S(1)}, f32[272,512]{1,0:T(8,128)S(1)}) custom-call(s16[368,128]{1,0:T(8,128)(2,1)S(1)} %collective-permute-done.refs_0_, s16[368,128]{1,0:T(8,128)(2,1)S(1)} %collective-permute-done.1.refs_1_, ...), custom_call_target="tpu_custom_call" | custom-call | flops 268435456 | bytes 3353600 | tf_op jit(solution)/shard_map/middle/pallas_call | solution.py:289
  11.8 0.5 %collective-permute-start.3 = (s16[368,128]{1,0:T(8,128)(2,1)S(1)}, s16[368,128]{1,0:T(8,128)(2,1)S(1)}, u32[]{:S(2)}, u32[]{:S(2)}) collective-permute-start(s16[368,128]{1,0:T(8,128)(2,1)S(1)} %get-tuple-element.49), channel_id=1, source_target_pairs={{0,24},{1,25},{2,26},{3,27},{4,28},{5,29},{6,30},{7,31},{8,9},{9,1... | collective-permute-start | bytes 282632 | tf_op jit(solution)/shard_map/ppermute | solution.py:319
  12.3 0.6 %collective-permute-start.4 = (s16[368,128]{1,0:T(8,128)(2,1)S(1)}, s16[368,128]{1,0:T(8,128)(2,1)S(1)}, u32[]{:S(2)}, u32[]{:S(2)}) collective-permute-start(s16[368,128]{1,0:T(8,128)(2,1)S(1)} %get-tuple-element.50), channel_id=1, source_target_pairs={{0,16},{1,17},{2,18},{3,19},{4,20},{5,21},{6,22},{7,23},{8,15},{9,... | collective-permute-start | bytes 282632 | tf_op jit(solution)/shard_map/ppermute | solution.py:319
  12.9 4.1 %collective-permute-start.5 = (s16[368,128]{1,0:T(8,128)(2,1)S(1)}, s16[368,128]{1,0:T(8,128)(2,1)S(1)}, u32[]{:S(2)}, u32[]{:S(2)}) collective-permute-start(s16[368,128]{1,0:T(8,128)(2,1)S(1)} %get-tuple-element.51), channel_id=1, source_target_pairs={{0,8},{1,9},{2,10},{3,11},{4,12},{5,13},{6,14},{7,15},{8,0},{9,1},... | collective-permute-start | bytes 282632 | tf_op jit(solution)/shard_map/ppermute | solution.py:319
  16.9 1.5 %own.1.refs_3_ = f32[272,512]{1,0:T(8,128)S(1)} custom-call(f32[1088,128]{1,0:T(8,128)S(1)} %get-tuple-element.34.refs_3_.refs_0_, f32[272,512]{1,0:T(8,128)S(1)} %get-tuple-element.52.refs_1_, bf16[768,512]{1,0:T(8,128)(2,1)S(1)} %get-tuple-element.42.refs_5_.refs_2_.refs_4_, bf16[512,512]{1,0:T(8,128)(2,1)S(1)} %get-tuple-element.53.refs_3_, ...), custom_call_target="tpu_custom_call" | custom-call | flops 268435456 | bytes 3892224 | tf_op jit(solution)/shard_map/own/pallas_call | solution.py:289
  18.4 1.1 %collective-permute-done.3.refs_0_ = s16[368,128]{1,0:T(8,128)(2,1)S(1)} collective-permute-done((s16[368,128]{1,0:T(8,128)(2,1)S(1)}, s16[368,128]{1,0:T(8,128)(2,1)S(1)}, u32[]{:S(2)}, u32[]{:S(2)}) %collective-permute-start.3) | collective-permute-done | bytes 94240 | tf_op jit(solution)/shard_map/ppermute | solution.py:319
  19.4 0.0 collective-permute-done.4.refs_1_
  19.4 0.0 collective-permute-done.5.refs_2_
  19.4 1.0 %last.1 = f32[1080,128]{1,0:T(8,128)} custom-call(s16[368,128]{1,0:T(8,128)(2,1)S(1)} %collective-permute-done.3.refs_0_, s16[368,128]{1,0:T(8,128)(2,1)S(1)} %collective-permute-done.4.refs_1_, s16[368,128]{1,0:T(8,128)(2,1)S(1)} %collective-permute-done.5.refs_2_, f32[272,512]{1,0:T(8,128)S(1)} %own.1.refs_3_, ...), custom_call_target="tpu_custom_call" | custom-call | flops 71303168 | bytes 1626112 | tf_op jit(solution)/shard_map/last/pallas_call | solution.py:289
Async XLA Ops:
  2.0 8.1 %collective-permute-start = (s16[368,128]{1,0:T(8,128)(2,1)S(1)}, s16[368,128]{1,0:T(8,128)(2,1)S(1)}, u32[]{:S(2)}, u32[]{:S(2)}) collective-permute-start(s16[368,128]{1,0:T(8,128)(2,1)S(1)} %get-tuple-element.30), channel_id=1, source_target_pairs={{0,24},{1,25},{2,26},{3,27},{4,28},{5,29},{6,30},{7,31},{8,9},{9,1... | collective-permute-start | bytes 282632 | tf_op jit(solution)/shard_map/ppermute | solution.py:319
  3.6 6.6 %collective-permute-start.1 = (s16[368,128]{1,0:T(8,128)(2,1)S(1)}, s16[368,128]{1,0:T(8,128)(2,1)S(1)}, u32[]{:S(2)}, u32[]{:S(2)}) collective-permute-start(s16[368,128]{1,0:T(8,128)(2,1)S(1)} %get-tuple-element.31), channel_id=1, source_target_pairs={{0,16},{1,17},{2,18},{3,19},{4,20},{5,21},{6,22},{7,23},{8,15},{9,... | collective-permute-start | bytes 282632 | tf_op jit(solution)/shard_map/ppermute | solution.py:319
  3.6 6.9 %collective-permute-start.2 = (s16[368,128]{1,0:T(8,128)(2,1)S(1)}, s16[368,128]{1,0:T(8,128)(2,1)S(1)}, u32[]{:S(2)}, u32[]{:S(2)}) collective-permute-start(s16[368,128]{1,0:T(8,128)(2,1)S(1)} %get-tuple-element.32), channel_id=1, source_target_pairs={{0,8},{1,9},{2,10},{3,11},{4,12},{5,13},{6,14},{7,15},{8,0},{9,1},... | collective-permute-start | bytes 282632 | tf_op jit(solution)/shard_map/ppermute | solution.py:319
  11.8 7.6 %collective-permute-start.3 = (s16[368,128]{1,0:T(8,128)(2,1)S(1)}, s16[368,128]{1,0:T(8,128)(2,1)S(1)}, u32[]{:S(2)}, u32[]{:S(2)}) collective-permute-start(s16[368,128]{1,0:T(8,128)(2,1)S(1)} %get-tuple-element.49), channel_id=1, source_target_pairs={{0,24},{1,25},{2,26},{3,27},{4,28},{5,29},{6,30},{7,31},{8,9},{9,1... | collective-permute-start | bytes 282632 | tf_op jit(solution)/shard_map/ppermute | solution.py:319
  12.3 7.2 %collective-permute-start.4 = (s16[368,128]{1,0:T(8,128)(2,1)S(1)}, s16[368,128]{1,0:T(8,128)(2,1)S(1)}, u32[]{:S(2)}, u32[]{:S(2)}) collective-permute-start(s16[368,128]{1,0:T(8,128)(2,1)S(1)} %get-tuple-element.50), channel_id=1, source_target_pairs={{0,16},{1,17},{2,18},{3,19},{4,20},{5,21},{6,22},{7,23},{8,15},{9,... | collective-permute-start | bytes 282632 | tf_op jit(solution)/shard_map/ppermute | solution.py:319
  12.9 6.6 %collective-permute-start.5 = (s16[368,128]{1,0:T(8,128)(2,1)S(1)}, s16[368,128]{1,0:T(8,128)(2,1)S(1)}, u32[]{:S(2)}, u32[]{:S(2)}) collective-permute-start(s16[368,128]{1,0:T(8,128)(2,1)S(1)} %get-tuple-element.51), channel_id=1, source_target_pairs={{0,8},{1,9},{2,10},{3,11},{4,12},{5,13},{6,14},{7,15},{8,0},{9,1},... | collective-permute-start | bytes 282632 | tf_op jit(solution)/shard_map/ppermute | solution.py:319

commit v7 on v5

--- a/solution.py
+++ b/solution.py
@@ -40,12 +40,12 @@
     largest = functools.reduce(
         jnp.maximum, [largest[:, at : at + 128] for at in range(0, values.shape[1], 128)]
     )
-    power = jnp.ceil(jnp.log(jnp.maximum(largest, 1e-30) * (1 / 32000)) * (1 / math.log(2)))
+    power = jnp.ceil(jnp.log(jnp.maximum(largest, 1e-30) * (1 / 32000)) * (8 / math.log(2)))
     return jnp.broadcast_to(power, (8, 128))
 
 
 def coded(values, power):
-    factor = jnp.exp2(-power[:1])
+    factor = jnp.exp2(power[:1] * (-1 / 8))
     return jnp.round(values * jnp.concatenate([factor] * (values.shape[1] // 128), axis=1))
 
 
@@ -59,7 +59,7 @@
 
 def from_message(message, rows, tiles):
     values = message.astype(f32)
-    values = values[: rows * tiles] * jnp.exp2(values[-1:])
+    values = values[: rows * tiles] * jnp.exp2(values[-1:] * (1 / 8))
     return jnp.concatenate([values[at * rows : (at + 1) * rows] for at in range(tiles)], axis=1)
 
 

time: 21.1 us -> 21.1 us (level)
  no operation moved by 1% of the time
where the time goes in v7:
time: 21.1 us; the launch traced here: 20.6 us
  starting transfers between devices  11.2 us (53%)
  Pallas kernels  8.07 us (38%)
  waiting for transfers between devices  1.29 us (6%)
    ppermute x6, starting transfers between devices, exchange(): received.append(lax.ppermute(message, ('grp', 'blk'), pairs))  11.2 us
    pallas_call x5, Pallas kernels, call(): pl.pallas_call(kernel, out_shape=out_shape, in_specs=[HBM] * hbm + [VMEM]...  8.07 us
    ppermute x6, waiting for transfers between devices, exchange(): received.append(lax.ppermute(message, ('grp', 'blk'), pairs))  1.29 us
  transfers between devices with their start and end apart: 6, of which 2 were waited for; matrix products, arithmetic and copies ran while one was open for 0% of the time, Pallas kernels for 16%

profile of v7, /device:TPU:2, one launch (start us, length us, event | category | flops | bytes accessed | tf_op | source)
XLA Modules:
  0.0 20.6 jit_solution(16760908093610944032)
XLA Ops:
  0.0 2.1 %pack.1 = (s16[368,128]{1,0:T(8,128)(2,1)S(1)}, s16[368,128]{1,0:T(8,128)(2,1)S(1)}, s16[368,128]{1,0:T(8,128)(2,1)S(1)}, f32[1088,128]{1,0:T(8,128)S(1)}, s32[2...) custom-call(f32[1080,128]{1,0:T(8,128)} %bitcast.6, ...), custom_call_target="tpu_custom_call" | custom-call | bytes 595304 | tf_op jit(solution)/shard_map/pack/pallas_call | solution.py:289
  2.1 1.6 %collective-permute-start = (s16[368,128]{1,0:T(8,128)(2,1)S(1)}, s16[368,128]{1,0:T(8,128)(2,1)S(1)}, u32[]{:S(2)}, u32[]{:S(2)}) collective-permute-start(s16[368,128]{1,0:T(8,128)(2,1)S(1)} %get-tuple-element.30), channel_id=1, source_target_pairs={{0,24},{1,25},{2,26},{3,27},{4,28},{5,29},{6,30},{7,31},{8,9},{9,1... | collective-permute-start | bytes 282632 | tf_op jit(solution)/shard_map/ppermute | solution.py:319
  3.7 0.0 collective-permute-start.1
  3.7 4.5 %collective-permute-start.2 = (s16[368,128]{1,0:T(8,128)(2,1)S(1)}, s16[368,128]{1,0:T(8,128)(2,1)S(1)}, u32[]{:S(2)}, u32[]{:S(2)}) collective-permute-start(s16[368,128]{1,0:T(8,128)(2,1)S(1)} %get-tuple-element.32), channel_id=1, source_target_pairs={{0,8},{1,9},{2,10},{3,11},{4,12},{5,13},{6,14},{7,15},{8,0},{9,1},... | collective-permute-start | bytes 282632 | tf_op jit(solution)/shard_map/ppermute | solution.py:319
  8.2 2.1 %first.1 = (bf16[768,512]{1,0:T(8,128)(2,1)S(1)}, bf16[768,512]{1,0:T(8,128)(2,1)S(1)}, f32[1,512]{1,0:T(1,128)S(1)}, f32[272,512]{1,0:T(8,128)S(1)}, bf16[512,2...) custom-call(bf16[270,512]{1,0:T(8,128)(2,1)} %bitcast.7, ...), custom_call_target="tpu_custom_call" | custom-call | flops 268435456 | bytes 1491304 | tf_op jit(solution)/shard_map/first/pallas_call | solution.py:289
  10.3 0.0 collective-permute-done.refs_0_
  10.3 0.0 collective-permute-done.1.refs_1_
  10.3 0.2 collective-permute-done.2.refs_2_
  10.5 1.5 %middle.1 = (s16[368,128]{1,0:T(8,128)(2,1)S(1)}, s16[368,128]{1,0:T(8,128)(2,1)S(1)}, s16[368,128]{1,0:T(8,128)(2,1)S(1)}, f32[272,512]{1,0:T(8,128)S(1)}) custom-call(s16[368,128]{1,0:T(8,128)(2,1)S(1)} %collective-permute-done.refs_0_, s16[368,128]{1,0:T(8,128)(2,1)S(1)} %collective-permute-done.1.refs_1_, ...), custom_call_target="tpu_custom_call" | custom-call | flops 268435456 | bytes 4140032 | tf_op jit(solution)/shard_map/middle/pallas_call | solution.py:289
  12.0 0.5 %collective-permute-start.3 = (s16[368,128]{1,0:T(8,128)(2,1)S(1)}, s16[368,128]{1,0:T(8,128)(2,1)S(1)}, u32[]{:S(2)}, u32[]{:S(2)}) collective-permute-start(s16[368,128]{1,0:T(8,128)(2,1)S(1)} %get-tuple-element.50), channel_id=1, source_target_pairs={{0,24},{1,25},{2,26},{3,27},{4,28},{5,29},{6,30},{7,31},{8,9},{9,1... | collective-permute-start | bytes 282632 | tf_op jit(solution)/shard_map/ppermute | solution.py:319
  12.5 0.5 %collective-permute-start.4 = (s16[368,128]{1,0:T(8,128)(2,1)S(1)}, s16[368,128]{1,0:T(8,128)(2,1)S(1)}, u32[]{:S(2)}, u32[]{:S(2)}) collective-permute-start(s16[368,128]{1,0:T(8,128)(2,1)S(1)} %get-tuple-element.51), channel_id=1, source_target_pairs={{0,16},{1,17},{2,18},{3,19},{4,20},{5,21},{6,22},{7,23},{8,15},{9,... | collective-permute-start | bytes 282632 | tf_op jit(solution)/shard_map/ppermute | solution.py:319
  13.0 4.2 %collective-permute-start.5 = (s16[368,128]{1,0:T(8,128)(2,1)S(1)}, s16[368,128]{1,0:T(8,128)(2,1)S(1)}, u32[]{:S(2)}, u32[]{:S(2)}) collective-permute-start(s16[368,128]{1,0:T(8,128)(2,1)S(1)} %get-tuple-element.52), channel_id=1, source_target_pairs={{0,8},{1,9},{2,10},{3,11},{4,12},{5,13},{6,14},{7,15},{8,0},{9,1},... | collective-permute-start | bytes 282632 | tf_op jit(solution)/shard_map/ppermute | solution.py:319
  17.2 1.3 %own.1.refs_3_ = f32[272,512]{1,0:T(8,128)S(1)} custom-call(f32[1088,128]{1,0:T(8,128)S(1)} %get-tuple-element.34.refs_3_.refs_0_, f32[272,512]{1,0:T(8,128)S(1)} %get-tuple-element.53.refs_1_, bf16[768,512]{1,0:T(8,128)(2,1)S(1)} %get-tuple-element.42.refs_5_.refs_2_.refs_4_, f32[1,512]{1,0:T(1,128)S(1)} %get-tuple-element.54.refs_3_, ...), custom_call_target="tpu_custom_call" | custom-call | flops 268435456 | bytes 3367936 | tf_op jit(solution)/shard_map/own/pallas_call | solution.py:289
  18.5 1.1 %collective-permute-done.3.refs_0_ = s16[368,128]{1,0:T(8,128)(2,1)S(1)} collective-permute-done((s16[368,128]{1,0:T(8,128)(2,1)S(1)}, s16[368,128]{1,0:T(8,128)(2,1)S(1)}, u32[]{:S(2)}, u32[]{:S(2)}) %collective-permute-start.3) | collective-permute-done | bytes 94240 | tf_op jit(solution)/shard_map/ppermute | solution.py:319
  19.6 0.0 collective-permute-done.4.refs_1_
  19.6 0.0 collective-permute-done.5.refs_2_
  19.6 1.0 %last.1 = f32[1080,128]{1,0:T(8,128)} custom-call(s16[368,128]{1,0:T(8,128)(2,1)S(1)} %collective-permute-done.3.refs_0_, s16[368,128]{1,0:T(8,128)(2,1)S(1)} %collective-permute-done.4.refs_1_, s16[368,128]{1,0:T(8,128)(2,1)S(1)} %collective-permute-done.5.refs_2_, f32[272,512]{1,0:T(8,128)S(1)} %own.1.refs_3_, ...), custom_call_target="tpu_custom_call" | custom-call | flops 71303168 | bytes 1626112 | tf_op jit(solution)/shard_map/last/pallas_call | solution.py:289
Async XLA Ops:
  2.1 8.2 %collective-permute-start = (s16[368,128]{1,0:T(8,128)(2,1)S(1)}, s16[368,128]{1,0:T(8,128)(2,1)S(1)}, u32[]{:S(2)}, u32[]{:S(2)}) collective-permute-start(s16[368,128]{1,0:T(8,128)(2,1)S(1)} %get-tuple-element.30), channel_id=1, source_target_pairs={{0,24},{1,25},{2,26},{3,27},{4,28},{5,29},{6,30},{7,31},{8,9},{9,1... | collective-permute-start | bytes 282632 | tf_op jit(solution)/shard_map/ppermute | solution.py:319
  3.7 6.6 %collective-permute-start.1 = (s16[368,128]{1,0:T(8,128)(2,1)S(1)}, s16[368,128]{1,0:T(8,128)(2,1)S(1)}, u32[]{:S(2)}, u32[]{:S(2)}) collective-permute-start(s16[368,128]{1,0:T(8,128)(2,1)S(1)} %get-tuple-element.31), channel_id=1, source_target_pairs={{0,16},{1,17},{2,18},{3,19},{4,20},{5,21},{6,22},{7,23},{8,15},{9,... | collective-permute-start | bytes 282632 | tf_op jit(solution)/shard_map/ppermute | solution.py:319
  3.7 6.8 %collective-permute-start.2 = (s16[368,128]{1,0:T(8,128)(2,1)S(1)}, s16[368,128]{1,0:T(8,128)(2,1)S(1)}, u32[]{:S(2)}, u32[]{:S(2)}) collective-permute-start(s16[368,128]{1,0:T(8,128)(2,1)S(1)} %get-tuple-element.32), channel_id=1, source_target_pairs={{0,8},{1,9},{2,10},{3,11},{4,12},{5,13},{6,14},{7,15},{8,0},{9,1},... | collective-permute-start | bytes 282632 | tf_op jit(solution)/shard_map/ppermute | solution.py:319
  12.0 7.6 %collective-permute-start.3 = (s16[368,128]{1,0:T(8,128)(2,1)S(1)}, s16[368,128]{1,0:T(8,128)(2,1)S(1)}, u32[]{:S(2)}, u32[]{:S(2)}) collective-permute-start(s16[368,128]{1,0:T(8,128)(2,1)S(1)} %get-tuple-element.50), channel_id=1, source_target_pairs={{0,24},{1,25},{2,26},{3,27},{4,28},{5,29},{6,30},{7,31},{8,9},{9,1... | collective-permute-start | bytes 282632 | tf_op jit(solution)/shard_map/ppermute | solution.py:319
  12.5 7.1 %collective-permute-start.4 = (s16[368,128]{1,0:T(8,128)(2,1)S(1)}, s16[368,128]{1,0:T(8,128)(2,1)S(1)}, u32[]{:S(2)}, u32[]{:S(2)}) collective-permute-start(s16[368,128]{1,0:T(8,128)(2,1)S(1)} %get-tuple-element.51), channel_id=1, source_target_pairs={{0,16},{1,17},{2,18},{3,19},{4,20},{5,21},{6,22},{7,23},{8,15},{9,... | collective-permute-start | bytes 282632 | tf_op jit(solution)/shard_map/ppermute | solution.py:319
  13.0 6.6 %collective-permute-start.5 = (s16[368,128]{1,0:T(8,128)(2,1)S(1)}, s16[368,128]{1,0:T(8,128)(2,1)S(1)}, u32[]{:S(2)}, u32[]{:S(2)}) collective-permute-start(s16[368,128]{1,0:T(8,128)(2,1)S(1)} %get-tuple-element.52), channel_id=1, source_target_pairs={{0,8},{1,9},{2,10},{3,11},{4,12},{5,13},{6,14},{7,15},{8,0},{9,1},... | collective-permute-start | bytes 282632 | tf_op jit(solution)/shard_map/ppermute | solution.py:319

commit v8 on v7

--- a/solution.py
+++ b/solution.py
@@ -133,9 +133,10 @@
     @pl.when(slot != 0)
     def _():
         state = load_rows(held_ref, 0, rows, cells)
+        power = power_of(state)
+        power = jnp.broadcast_to(jnp.max(power[:1], axis=1, keepdims=True), power.shape)
         high, low = split(state)
         sent = dot(high, pick_ref[...]) + dot(low, pick_ref[...])
-        power = power_of(sent)
         both = halo_messages(coded(sent, power), power, length)
         send(plan0, slot, messages, {**both, "H": both["U"]})
 

time: 21.1 us -> 21 us (level)
    ppermute x6, waiting for transfers between devices: 1.29 us -> 1.5 us  [exchange(): received.append(lax.ppermute(message, ('grp', 'blk'), pairs))]
where the time goes in v8:
time: 21 us; the launch traced here: 20.7 us
  starting transfers between devices  11.2 us (53%)
  Pallas kernels  7.99 us (38%)
  waiting for transfers between devices  1.5 us (7%)
    ppermute x6, starting transfers between devices, exchange(): received.append(lax.ppermute(message, ('grp', 'blk'), pairs))  11.2 us
    pallas_call x5, Pallas kernels, call(): pl.pallas_call(kernel, out_shape=out_shape, in_specs=[HBM] * hbm + [VMEM]...  7.99 us
    ppermute x6, waiting for transfers between devices, exchange(): received.append(lax.ppermute(message, ('grp', 'blk'), pairs))  1.5 us
  transfers between devices with their start and end apart: 6, of which 2 were waited for; matrix products, arithmetic and copies ran while one was open for 0% of the time, Pallas kernels for 16%

profile of v8, /device:TPU:2, one launch (start us, length us, event | category | flops | bytes accessed | tf_op | source)
XLA Modules:
  0.0 20.7 jit_solution(3603581211489221650)
XLA Ops:
  0.0 2.0 %pack.1 = (s16[368,128]{1,0:T(8,128)(2,1)S(1)}, s16[368,128]{1,0:T(8,128)(2,1)S(1)}, s16[368,128]{1,0:T(8,128)(2,1)S(1)}, f32[1088,128]{1,0:T(8,128)S(1)}, s32[2...) custom-call(f32[1080,128]{1,0:T(8,128)} %bitcast.6, ...), custom_call_target="tpu_custom_call" | custom-call | bytes 595304 | tf_op jit(solution)/shard_map/pack/pallas_call | solution.py:290
  2.0 1.6 %collective-permute-start = (s16[368,128]{1,0:T(8,128)(2,1)S(1)}, s16[368,128]{1,0:T(8,128)(2,1)S(1)}, u32[]{:S(2)}, u32[]{:S(2)}) collective-permute-start(s16[368,128]{1,0:T(8,128)(2,1)S(1)} %get-tuple-element.30), channel_id=1, source_target_pairs={{0,24},{1,25},{2,26},{3,27},{4,28},{5,29},{6,30},{7,31},{8,9},{9,1... | collective-permute-start | bytes 282632 | tf_op jit(solution)/shard_map/ppermute | solution.py:320
  3.6 0.0 collective-permute-start.1
  3.6 4.5 %collective-permute-start.2 = (s16[368,128]{1,0:T(8,128)(2,1)S(1)}, s16[368,128]{1,0:T(8,128)(2,1)S(1)}, u32[]{:S(2)}, u32[]{:S(2)}) collective-permute-start(s16[368,128]{1,0:T(8,128)(2,1)S(1)} %get-tuple-element.32), channel_id=1, source_target_pairs={{0,8},{1,9},{2,10},{3,11},{4,12},{5,13},{6,14},{7,15},{8,0},{9,1},... | collective-permute-start | bytes 282632 | tf_op jit(solution)/shard_map/ppermute | solution.py:320
  8.1 2.1 %first.1 = (bf16[768,512]{1,0:T(8,128)(2,1)S(1)}, bf16[768,512]{1,0:T(8,128)(2,1)S(1)}, f32[1,512]{1,0:T(1,128)S(1)}, f32[272,512]{1,0:T(8,128)S(1)}, bf16[512,2...) custom-call(bf16[270,512]{1,0:T(8,128)(2,1)} %bitcast.7, ...), custom_call_target="tpu_custom_call" | custom-call | flops 268435456 | bytes 1491304 | tf_op jit(solution)/shard_map/first/pallas_call | solution.py:290
  10.2 0.0 collective-permute-done.refs_0_
  10.2 0.0 collective-permute-done.1.refs_1_
  10.2 0.2 %collective-permute-done.2.refs_2_ = s16[368,128]{1,0:T(8,128)(2,1)S(1)} collective-permute-done((s16[368,128]{1,0:T(8,128)(2,1)S(1)}, s16[368,128]{1,0:T(8,128)(2,1)S(1)}, u32[]{:S(2)}, u32[]{:S(2)}) %collective-permute-start.2) | collective-permute-done | bytes 94240 | tf_op jit(solution)/shard_map/ppermute | solution.py:320
  10.5 1.5 %middle.1 = (s16[368,128]{1,0:T(8,128)(2,1)S(1)}, s16[368,128]{1,0:T(8,128)(2,1)S(1)}, s16[368,128]{1,0:T(8,128)(2,1)S(1)}, f32[272,512]{1,0:T(8,128)S(1)}) custom-call(s16[368,128]{1,0:T(8,128)(2,1)S(1)} %collective-permute-done.refs_0_, s16[368,128]{1,0:T(8,128)(2,1)S(1)} %collective-permute-done.1.refs_1_, ...), custom_call_target="tpu_custom_call" | custom-call | flops 268435456 | bytes 4140032 | tf_op jit(solution)/shard_map/middle/pallas_call | solution.py:290
  12.0 0.5 %collective-permute-start.3 = (s16[368,128]{1,0:T(8,128)(2,1)S(1)}, s16[368,128]{1,0:T(8,128)(2,1)S(1)}, u32[]{:S(2)}, u32[]{:S(2)}) collective-permute-start(s16[368,128]{1,0:T(8,128)(2,1)S(1)} %get-tuple-element.50), channel_id=1, source_target_pairs={{0,24},{1,25},{2,26},{3,27},{4,28},{5,29},{6,30},{7,31},{8,9},{9,1... | collective-permute-start | bytes 282632 | tf_op jit(solution)/shard_map/ppermute | solution.py:320
  12.4 0.6 %collective-permute-start.4 = (s16[368,128]{1,0:T(8,128)(2,1)S(1)}, s16[368,128]{1,0:T(8,128)(2,1)S(1)}, u32[]{:S(2)}, u32[]{:S(2)}) collective-permute-start(s16[368,128]{1,0:T(8,128)(2,1)S(1)} %get-tuple-element.51), channel_id=1, source_target_pairs={{0,16},{1,17},{2,18},{3,19},{4,20},{5,21},{6,22},{7,23},{8,15},{9,... | collective-permute-start | bytes 282632 | tf_op jit(solution)/shard_map/ppermute | solution.py:320
  13.1 4.0 %collective-permute-start.5 = (s16[368,128]{1,0:T(8,128)(2,1)S(1)}, s16[368,128]{1,0:T(8,128)(2,1)S(1)}, u32[]{:S(2)}, u32[]{:S(2)}) collective-permute-start(s16[368,128]{1,0:T(8,128)(2,1)S(1)} %get-tuple-element.52), channel_id=1, source_target_pairs={{0,8},{1,9},{2,10},{3,11},{4,12},{5,13},{6,14},{7,15},{8,0},{9,1},... | collective-permute-start | bytes 282632 | tf_op jit(solution)/shard_map/ppermute | solution.py:320
  17.1 1.3 %own.1.refs_3_ = f32[272,512]{1,0:T(8,128)S(1)} custom-call(f32[1088,128]{1,0:T(8,128)S(1)} %get-tuple-element.34.refs_3_.refs_0_, f32[272,512]{1,0:T(8,128)S(1)} %get-tuple-element.53.refs_1_, bf16[768,512]{1,0:T(8,128)(2,1)S(1)} %get-tuple-element.42.refs_5_.refs_2_.refs_4_, f32[1,512]{1,0:T(1,128)S(1)} %get-tuple-element.54.refs_3_, ...), custom_call_target="tpu_custom_call" | custom-call | flops 268435456 | bytes 3367936 | tf_op jit(solution)/shard_map/own/pallas_call | solution.py:290
  18.4 1.2 %collective-permute-done.3.refs_0_ = s16[368,128]{1,0:T(8,128)(2,1)S(1)} collective-permute-done((s16[368,128]{1,0:T(8,128)(2,1)S(1)}, s16[368,128]{1,0:T(8,128)(2,1)S(1)}, u32[]{:S(2)}, u32[]{:S(2)}) %collective-permute-start.3) | collective-permute-done | bytes 94240 | tf_op jit(solution)/shard_map/ppermute | solution.py:320
  19.6 0.0 collective-permute-done.4.refs_1_
  19.6 0.0 collective-permute-done.5.refs_2_
  19.7 1.0 %last.1 = f32[1080,128]{1,0:T(8,128)} custom-call(s16[368,128]{1,0:T(8,128)(2,1)S(1)} %collective-permute-done.3.refs_0_, s16[368,128]{1,0:T(8,128)(2,1)S(1)} %collective-permute-done.4.refs_1_, s16[368,128]{1,0:T(8,128)(2,1)S(1)} %collective-permute-done.5.refs_2_, f32[272,512]{1,0:T(8,128)S(1)} %own.1.refs_3_, ...), custom_call_target="tpu_custom_call" | custom-call | flops 71303168 | bytes 1626112 | tf_op jit(solution)/shard_map/last/pallas_call | solution.py:290
Async XLA Ops:
  2.0 8.2 %collective-permute-start = (s16[368,128]{1,0:T(8,128)(2,1)S(1)}, s16[368,128]{1,0:T(8,128)(2,1)S(1)}, u32[]{:S(2)}, u32[]{:S(2)}) collective-permute-start(s16[368,128]{1,0:T(8,128)(2,1)S(1)} %get-tuple-element.30), channel_id=1, source_target_pairs={{0,24},{1,25},{2,26},{3,27},{4,28},{5,29},{6,30},{7,31},{8,9},{9,1... | collective-permute-start | bytes 282632 | tf_op jit(solution)/shard_map/ppermute | solution.py:320
  3.6 6.6 %collective-permute-start.1 = (s16[368,128]{1,0:T(8,128)(2,1)S(1)}, s16[368,128]{1,0:T(8,128)(2,1)S(1)}, u32[]{:S(2)}, u32[]{:S(2)}) collective-permute-start(s16[368,128]{1,0:T(8,128)(2,1)S(1)} %get-tuple-element.31), channel_id=1, source_target_pairs={{0,16},{1,17},{2,18},{3,19},{4,20},{5,21},{6,22},{7,23},{8,15},{9,... | collective-permute-start | bytes 282632 | tf_op jit(solution)/shard_map/ppermute | solution.py:320
  3.6 6.8 %collective-permute-start.2 = (s16[368,128]{1,0:T(8,128)(2,1)S(1)}, s16[368,128]{1,0:T(8,128)(2,1)S(1)}, u32[]{:S(2)}, u32[]{:S(2)}) collective-permute-start(s16[368,128]{1,0:T(8,128)(2,1)S(1)} %get-tuple-element.32), channel_id=1, source_target_pairs={{0,8},{1,9},{2,10},{3,11},{4,12},{5,13},{6,14},{7,15},{8,0},{9,1},... | collective-permute-start | bytes 282632 | tf_op jit(solution)/shard_map/ppermute | solution.py:320
  12.0 7.6 %collective-permute-start.3 = (s16[368,128]{1,0:T(8,128)(2,1)S(1)}, s16[368,128]{1,0:T(8,128)(2,1)S(1)}, u32[]{:S(2)}, u32[]{:S(2)}) collective-permute-start(s16[368,128]{1,0:T(8,128)(2,1)S(1)} %get-tuple-element.50), channel_id=1, source_target_pairs={{0,24},{1,25},{2,26},{3,27},{4,28},{5,29},{6,30},{7,31},{8,9},{9,1... | collective-permute-start | bytes 282632 | tf_op jit(solution)/shard_map/ppermute | solution.py:320
  12.4 7.2 %collective-permute-start.4 = (s16[368,128]{1,0:T(8,128)(2,1)S(1)}, s16[368,128]{1,0:T(8,128)(2,1)S(1)}, u32[]{:S(2)}, u32[]{:S(2)}) collective-permute-start(s16[368,128]{1,0:T(8,128)(2,1)S(1)} %get-tuple-element.51), channel_id=1, source_target_pairs={{0,16},{1,17},{2,18},{3,19},{4,20},{5,21},{6,22},{7,23},{8,15},{9,... | collective-permute-start | bytes 282632 | tf_op jit(solution)/shard_map/ppermute | solution.py:320
  13.1 6.6 %collective-permute-start.5 = (s16[368,128]{1,0:T(8,128)(2,1)S(1)}, s16[368,128]{1,0:T(8,128)(2,1)S(1)}, u32[]{:S(2)}, u32[]{:S(2)}) collective-permute-start(s16[368,128]{1,0:T(8,128)(2,1)S(1)} %get-tuple-element.52), channel_id=1, source_target_pairs={{0,8},{1,9},{2,10},{3,11},{4,12},{5,13},{6,14},{7,15},{8,0},{9,1},... | collective-permute-start | bytes 282632 | tf_op jit(solution)/shard_map/ppermute | solution.py:320

commit v9 on v6

--- a/solution.py
+++ b/solution.py
@@ -40,12 +40,12 @@
     largest = functools.reduce(
         jnp.maximum, [largest[:, at : at + 128] for at in range(0, values.shape[1], 128)]
     )
-    power = jnp.ceil(jnp.log(jnp.maximum(largest, 1e-30) * (1 / 32000)) * (1 / math.log(2)))
+    power = jnp.ceil(jnp.log(jnp.maximum(largest, 1e-30) * (1 / 32000)) * (8 / math.log(2)))
     return jnp.broadcast_to(power, (8, 128))
 
 
 def coded(values, power):
-    factor = jnp.exp2(-power[:1])
+    factor = jnp.exp2(power[:1] * (-1 / 8))
     return jnp.round(values * jnp.concatenate([factor] * (values.shape[1] // 128), axis=1))
 
 
@@ -59,7 +59,7 @@
 
 def from_message(message, rows, tiles):
     values = message.astype(f32)
-    values = values[: rows * tiles] * jnp.exp2(values[-1:])
+    values = values[: rows * tiles] * jnp.exp2(values[-1:] * (1 / 8))
     return jnp.concatenate([values[at * rows : (at + 1) * rows] for at in range(tiles)], axis=1)
 
 
@@ -133,7 +133,8 @@
     @pl.when(slot != 0)
     def _():
         state = load_rows(held_ref, 0, rows, cells)
-        sent = dot(state.astype(bf16), pick_ref[...])
+        high, low = split(state)
+        sent = dot(high, pick_ref[...]) + dot(low, pick_ref[...])
         power = power_of(sent)
         both = halo_messages(coded(sent, power), power, length)
         send(plan0, slot, messages, {**both, "H": both["U"]})
@@ -159,7 +160,7 @@
 def first_kernel(
     quarter, w_in_t_hbm, w_mid_hbm, w_out_hbm,
     held_ref, near_ref, diff_ref, tran_ref, b_in_ref, b_mid_ref, b_out_ref,
-    matrix_ref, matrix_low_ref, keep_ref, part_ref, w_in_ref, c_in_ref, c_mid_ref, c_out_ref,
+    matrix_ref, matrix_low_ref, halo_matrix_ref, keep_ref, part_ref, w_in_ref, c_in_ref, c_mid_ref, c_out_ref,
     w_mid_ref, w_out_ref, w_in_t_ref, sems,
 ):
     slot = slot_of(quarter)
@@ -190,6 +191,11 @@
             matrix_ref[start : start + piece, :] = high
             if start < cells:
                 matrix_low_ref[start : start + piece, :] = low
+            else:
+                size = matrix_ref.shape[0] - cells
+                for at, half in enumerate((high, high, low)):
+                    place = at * size + start - cells
+                    halo_matrix_ref[place : place + piece, :] = half
         state = load_rows(held_ref, 0, rows, cells)
         high, low = split(state)
         part_ref[...] = (
@@ -208,7 +214,7 @@
 
 
 def middle_kernel(
-    quarter, received, pick_ref, part_ref, matrix_ref,
+    quarter, received, pick_ref, part_ref, halo_matrix_ref,
     w_in_ref, b_in_ref, w_mid_ref, b_mid_ref, w_out_ref, b_out_ref,
     messages, state_ref,
 ):
@@ -218,8 +224,10 @@
         rows, cells = state_ref.shape
         levels, length = w_out_ref.shape[0], messages[0].shape[0]
         heat = from_message(receive(plan0, slot, received, "H"), levels, cells // 128)
-        halos = receive_halos(plan0, slot, received, rows).astype(bf16)
-        state_ref[...] = part_ref[...] + dot(halos, matrix_ref[cells:, :])
+        high, low = split(receive_halos(plan0, slot, received, rows))
+        state_ref[...] = part_ref[...] + dot(
+            jnp.concatenate([high, low, high], axis=1), halo_matrix_ref[...]
+        )
         state_ref[:levels, :] = state_ref[:levels, :] + heat_gain * heat
         state = state_ref[...].astype(bf16)
         sent = dot(state, pick_ref[...])
@@ -349,17 +357,16 @@
         hbm=2 + len(args), scratch=[pltpu.SemaphoreType.DMA((2 + len(args),))],
     )
     received = exchange(plan0, messages, quarter, blocks)
-    matrix, matrix_low, keep, part1, w_in, c_in, c_mid, c_out, w_mid, w_out = call(
+    matrix, matrix_low, halo_matrix, keep, part1, w_in, c_in, c_mid, c_out, w_mid, w_out = call(
         lambda *refs: first_kernel(quarter, *refs), "first",
         [
-            matrix_shape, shape(cells, cells, dtype=bf16), shape(1, cells), full,
+            matrix_shape, shape(cells, cells, dtype=bf16), shape(6 * halo, cells, dtype=bf16),
+            shape(1, cells), full,
             shape(hidden, rows, dtype=bf16), shape(hidden, 128), shape(hidden, 128), shape(levels, 128),
             like(w_mid), like(w_out),
         ],
         w_in.T, w_mid, w_out, flat, near, diff, tran, b_in, b_mid, b_out,
-        hbm=3, scratch=[
-            pltpu.VMEM((features, hidden), bf16), pltpu.SemaphoreType.DMA((3,)),
-        ],
+        hbm=3, scratch=[pltpu.VMEM((features, hidden), bf16), pltpu.SemaphoreType.DMA((3,))],
         flops=2 * cells * hidden * hidden,
     )
     weights = (w_in, c_in, w_mid, c_mid, w_out, c_out)
@@ -368,7 +375,7 @@
             quarter, refs[:count0], *refs[count0 : count0 + 9], refs[count0 + 9 : -1], refs[-1]
         ),
         "middle", [message] * count1 + [full],
-        *received, pick, part1, matrix, *weights, flops=2 * cells * hidden * hidden,
+        *received, pick, part1, halo_matrix, *weights, flops=2 * cells * hidden * hidden,
     )
     received = exchange(plan1, messages, quarter, blocks)
     part2 = call(

time: 20.8 us -> 21.1 us (1.014)
  Pallas kernels: 7.93 us -> 8.22 us
    pallas_call x5, Pallas kernels: 7.93 us -> 8.22 us  [call(): pl.pallas_call(kernel, out_shape=out_shape, in_specs=[HBM] * hbm + [VMEM]...]
where the time goes in v9:
time: 21.1 us; the launch traced here: 20.7 us
  starting transfers between devices  11.2 us (53%)
  Pallas kernels  8.22 us (39%)
  waiting for transfers between devices  1.15 us (5%)
    ppermute x6, starting transfers between devices, exchange(): received.append(lax.ppermute(message, ('grp', 'blk'), pairs))  11.2 us
    pallas_call x5, Pallas kernels, call(): pl.pallas_call(kernel, out_shape=out_shape, in_specs=[HBM] * hbm + [VMEM]...  8.22 us
    ppermute x6, waiting for transfers between devices, exchange(): received.append(lax.ppermute(message, ('grp', 'blk'), pairs))  1.15 us
  transfers between devices with their start and end apart: 6, of which 2 were waited for; matrix products, arithmetic and copies ran while one was open for 0% of the time, Pallas kernels for 17%

profile of v9, /device:TPU:2, one launch (start us, length us, event | category | flops | bytes accessed | tf_op | source)
XLA Modules:
  0.0 20.7 jit_solution(11914241307602459180)
XLA Ops:
  0.0 2.1 %pack.1 = (s16[368,128]{1,0:T(8,128)(2,1)S(1)}, s16[368,128]{1,0:T(8,128)(2,1)S(1)}, s16[368,128]{1,0:T(8,128)(2,1)S(1)}, f32[1088,128]{1,0:T(8,128)S(1)}, s32[2...) custom-call(f32[1080,128]{1,0:T(8,128)} %bitcast.6, ...), custom_call_target="tpu_custom_call" | custom-call | bytes 595304 | tf_op jit(solution)/shard_map/pack/pallas_call | solution.py:297
  2.1 1.6 %collective-permute-start = (s16[368,128]{1,0:T(8,128)(2,1)S(1)}, s16[368,128]{1,0:T(8,128)(2,1)S(1)}, u32[]{:S(2)}, u32[]{:S(2)}) collective-permute-start(s16[368,128]{1,0:T(8,128)(2,1)S(1)} %get-tuple-element.31), channel_id=1, source_target_pairs={{0,24},{1,25},{2,26},{3,27},{4,28},{5,29},{6,30},{7,31},{8,9},{9,1... | collective-permute-start | bytes 282632 | tf_op jit(solution)/shard_map/ppermute | solution.py:327
  3.7 0.0 collective-permute-start.1
  3.7 4.5 %collective-permute-start.2 = (s16[368,128]{1,0:T(8,128)(2,1)S(1)}, s16[368,128]{1,0:T(8,128)(2,1)S(1)}, u32[]{:S(2)}, u32[]{:S(2)}) collective-permute-start(s16[368,128]{1,0:T(8,128)(2,1)S(1)} %get-tuple-element.33), channel_id=1, source_target_pairs={{0,8},{1,9},{2,10},{3,11},{4,12},{5,13},{6,14},{7,15},{8,0},{9,1},... | collective-permute-start | bytes 282632 | tf_op jit(solution)/shard_map/ppermute | solution.py:327
  8.2 2.1 %first.1 = (bf16[768,512]{1,0:T(8,128)(2,1)S(1)}, bf16[512,512]{1,0:T(8,128)(2,1)S(1)}, bf16[768,512]{1,0:T(8,128)(2,1)S(1)}, f32[1,512]{1,0:T(1,128)S(1)}, f32[...) custom-call(bf16[270,512]{1,0:T(8,128)(2,1)} %bitcast.7, ...), custom_call_target="tpu_custom_call" | custom-call | flops 268435456 | bytes 1491304 | tf_op jit(solution)/shard_map/first/pallas_call | solution.py:297
  10.3 0.0 collective-permute-done.refs_0_
  10.3 0.0 collective-permute-done.1.refs_1_
  10.3 0.2 collective-permute-done.2.refs_2_
  10.5 1.5 %middle.1 = (s16[368,128]{1,0:T(8,128)(2,1)S(1)}, s16[368,128]{1,0:T(8,128)(2,1)S(1)}, s16[368,128]{1,0:T(8,128)(2,1)S(1)}, f32[272,512]{1,0:T(8,128)S(1)}) custom-call(s16[368,128]{1,0:T(8,128)(2,1)S(1)} %collective-permute-done.refs_0_, s16[368,128]{1,0:T(8,128)(2,1)S(1)} %collective-permute-done.1.refs_1_, ...), custom_call_target="tpu_custom_call" | custom-call | flops 268435456 | bytes 3353600 | tf_op jit(solution)/shard_map/middle/pallas_call | solution.py:297
  12.0 0.4 %collective-permute-start.3 = (s16[368,128]{1,0:T(8,128)(2,1)S(1)}, s16[368,128]{1,0:T(8,128)(2,1)S(1)}, u32[]{:S(2)}, u32[]{:S(2)}) collective-permute-start(s16[368,128]{1,0:T(8,128)(2,1)S(1)} %get-tuple-element.50), channel_id=1, source_target_pairs={{0,24},{1,25},{2,26},{3,27},{4,28},{5,29},{6,30},{7,31},{8,9},{9,1... | collective-permute-start | bytes 282632 | tf_op jit(solution)/shard_map/ppermute | solution.py:327
  12.5 0.5 %collective-permute-start.4 = (s16[368,128]{1,0:T(8,128)(2,1)S(1)}, s16[368,128]{1,0:T(8,128)(2,1)S(1)}, u32[]{:S(2)}, u32[]{:S(2)}) collective-permute-start(s16[368,128]{1,0:T(8,128)(2,1)S(1)} %get-tuple-element.51), channel_id=1, source_target_pairs={{0,16},{1,17},{2,18},{3,19},{4,20},{5,21},{6,22},{7,23},{8,15},{9,... | collective-permute-start | bytes 282632 | tf_op jit(solution)/shard_map/ppermute | solution.py:327
  13.0 4.2 %collective-permute-start.5 = (s16[368,128]{1,0:T(8,128)(2,1)S(1)}, s16[368,128]{1,0:T(8,128)(2,1)S(1)}, u32[]{:S(2)}, u32[]{:S(2)}) collective-permute-start(s16[368,128]{1,0:T(8,128)(2,1)S(1)} %get-tuple-element.52), channel_id=1, source_target_pairs={{0,8},{1,9},{2,10},{3,11},{4,12},{5,13},{6,14},{7,15},{8,0},{9,1},... | collective-permute-start | bytes 282632 | tf_op jit(solution)/shard_map/ppermute | solution.py:327
  17.2 1.4 %own.1.refs_3_ = f32[272,512]{1,0:T(8,128)S(1)} custom-call(f32[1088,128]{1,0:T(8,128)S(1)} %get-tuple-element.35.refs_3_.refs_0_, f32[272,512]{1,0:T(8,128)S(1)} %get-tuple-element.53.refs_1_, bf16[768,512]{1,0:T(8,128)(2,1)S(1)} %get-tuple-element.54.refs_2_.refs_4_, bf16[512,512]{1,0:T(8,128)(2,1)S(1)} %get-tuple-element.55.refs_3_, ...), custom_call_target="tpu_custom_call" | custom-call | flops 268435456 | bytes 3892224 | tf_op jit(solution)/shard_map/own/pallas_call | solution.py:297
  18.6 1.0 %collective-permute-done.3.refs_0_ = s16[368,128]{1,0:T(8,128)(2,1)S(1)} collective-permute-done((s16[368,128]{1,0:T(8,128)(2,1)S(1)}, s16[368,128]{1,0:T(8,128)(2,1)S(1)}, u32[]{:S(2)}, u32[]{:S(2)}) %collective-permute-start.3) | collective-permute-done | bytes 94240 | tf_op jit(solution)/shard_map/ppermute | solution.py:327
  19.6 0.0 collective-permute-done.4.refs_1_
  19.6 0.0 collective-permute-done.5.refs_2_
  19.6 1.0 %last.1 = f32[1080,128]{1,0:T(8,128)} custom-call(s16[368,128]{1,0:T(8,128)(2,1)S(1)} %collective-permute-done.3.refs_0_, s16[368,128]{1,0:T(8,128)(2,1)S(1)} %collective-permute-done.4.refs_1_, s16[368,128]{1,0:T(8,128)(2,1)S(1)} %collective-permute-done.5.refs_2_, f32[272,512]{1,0:T(8,128)S(1)} %own.1.refs_3_, ...), custom_call_target="tpu_custom_call" | custom-call | flops 71303168 | bytes 1626112 | tf_op jit(solution)/shard_map/last/pallas_call | solution.py:297
Async XLA Ops:
  2.1 8.2 %collective-permute-start = (s16[368,128]{1,0:T(8,128)(2,1)S(1)}, s16[368,128]{1,0:T(8,128)(2,1)S(1)}, u32[]{:S(2)}, u32[]{:S(2)}) collective-permute-start(s16[368,128]{1,0:T(8,128)(2,1)S(1)} %get-tuple-element.31), channel_id=1, source_target_pairs={{0,24},{1,25},{2,26},{3,27},{4,28},{5,29},{6,30},{7,31},{8,9},{9,1... | collective-permute-start | bytes 282632 | tf_op jit(solution)/shard_map/ppermute | solution.py:327
  3.7 6.6 %collective-permute-start.1 = (s16[368,128]{1,0:T(8,128)(2,1)S(1)}, s16[368,128]{1,0:T(8,128)(2,1)S(1)}, u32[]{:S(2)}, u32[]{:S(2)}) collective-permute-start(s16[368,128]{1,0:T(8,128)(2,1)S(1)} %get-tuple-element.32), channel_id=1, source_target_pairs={{0,16},{1,17},{2,18},{3,19},{4,20},{5,21},{6,22},{7,23},{8,15},{9,... | collective-permute-start | bytes 282632 | tf_op jit(solution)/shard_map/ppermute | solution.py:327
  3.7 6.8 %collective-permute-start.2 = (s16[368,128]{1,0:T(8,128)(2,1)S(1)}, s16[368,128]{1,0:T(8,128)(2,1)S(1)}, u32[]{:S(2)}, u32[]{:S(2)}) collective-permute-start(s16[368,128]{1,0:T(8,128)(2,1)S(1)} %get-tuple-element.33), channel_id=1, source_target_pairs={{0,8},{1,9},{2,10},{3,11},{4,12},{5,13},{6,14},{7,15},{8,0},{9,1},... | collective-permute-start | bytes 282632 | tf_op jit(solution)/shard_map/ppermute | solution.py:327
  12.0 7.6 %collective-permute-start.3 = (s16[368,128]{1,0:T(8,128)(2,1)S(1)}, s16[368,128]{1,0:T(8,128)(2,1)S(1)}, u32[]{:S(2)}, u32[]{:S(2)}) collective-permute-start(s16[368,128]{1,0:T(8,128)(2,1)S(1)} %get-tuple-element.50), channel_id=1, source_target_pairs={{0,24},{1,25},{2,26},{3,27},{4,28},{5,29},{6,30},{7,31},{8,9},{9,1... | collective-permute-start | bytes 282632 | tf_op jit(solution)/shard_map/ppermute | solution.py:327
  12.5 7.1 %collective-permute-start.4 = (s16[368,128]{1,0:T(8,128)(2,1)S(1)}, s16[368,128]{1,0:T(8,128)(2,1)S(1)}, u32[]{:S(2)}, u32[]{:S(2)}) collective-permute-start(s16[368,128]{1,0:T(8,128)(2,1)S(1)} %get-tuple-element.51), channel_id=1, source_target_pairs={{0,16},{1,17},{2,18},{3,19},{4,20},{5,21},{6,22},{7,23},{8,15},{9,... | collective-permute-start | bytes 282632 | tf_op jit(solution)/shard_map/ppermute | solution.py:327
  13.0 6.6 %collective-permute-start.5 = (s16[368,128]{1,0:T(8,128)(2,1)S(1)}, s16[368,128]{1,0:T(8,128)(2,1)S(1)}, u32[]{:S(2)}, u32[]{:S(2)}) collective-permute-start(s16[368,128]{1,0:T(8,128)(2,1)S(1)} %get-tuple-element.52), channel_id=1, source_target_pairs={{0,8},{1,9},{2,10},{3,11},{4,12},{5,13},{6,14},{7,15},{8,0},{9,1},... | collective-permute-start | bytes 282632 | tf_op jit(solution)/shard_map/ppermute | solution.py:327

commit v10 on v7

--- a/solution.py
+++ b/solution.py
@@ -143,8 +143,7 @@
         copy.wait()
 
 
-def silu(v):
-    half = 0.5 * v
+def silu(half):
     return half + half * jnp.tanh(half)
 
 
@@ -200,9 +199,12 @@
             copy.wait()
         features = w_in_t_ref.shape[0]
         w_in_ref[...] = jnp.zeros_like(w_in_ref)
-        w_in_ref[:, :features] = w_in_t_ref[...].T
-        for row_ref, column_ref in ((b_in_ref, c_in_ref), (b_mid_ref, c_mid_ref), (b_out_ref, c_out_ref)):
-            column_ref[...] = jnp.broadcast_to(row_ref[...], (128, row_ref.shape[1])).T
+        w_in_ref[:, :features] = (w_in_t_ref[...] * 0.5).T
+        w_mid_ref[...] = w_mid_ref[...] * 0.5
+        for row_ref, column_ref, part in (
+            (b_in_ref, c_in_ref, 0.5), (b_mid_ref, c_mid_ref, 0.5), (b_out_ref, c_out_ref, 1.0),
+        ):
+            column_ref[...] = jnp.broadcast_to(row_ref[...] * part, (128, row_ref.shape[1])).T
 
 
 def middle_kernel(

time: 21.1 us -> 21 us (level)
  Pallas kernels: 8.07 us -> 8.32 us
    ppermute x6, starting transfers between devices: 11.2 us -> 11 us  [exchange(): received.append(lax.ppermute(message, ('grp', 'blk'), pairs))]
    pallas_call x5, Pallas kernels: 8.07 us -> 8.32 us  [call(): pl.pallas_call(kernel, out_shape=out_shape, in_specs=[HBM] * hbm + [VMEM]...]
  transfers between devices with their start and end apart: 6 -> 6, of which waited for: 2 -> 1; matrix products, arithmetic and copies ran while one was open for 0% -> 0% of each run, Pallas kernels for 16% -> 18%
where the time goes in v10:
time: 21 us; the launch traced here: 20.6 us
  starting transfers between devices  11 us (52%)
  Pallas kernels  8.32 us (40%)
  waiting for transfers between devices  1.29 us (6%)
    ppermute x6, starting transfers between devices, exchange(): received.append(lax.ppermute(message, ('grp', 'blk'), pairs))  11 us
    pallas_call x5, Pallas kernels, call(): pl.pallas_call(kernel, out_shape=out_shape, in_specs=[HBM] * hbm + [VMEM]...  8.32 us
    ppermute x6, waiting for transfers between devices, exchange(): received.append(lax.ppermute(message, ('grp', 'blk'), pairs))  1.29 us
  transfers between devices with their start and end apart: 6, of which 1 were waited for; matrix products, arithmetic and copies ran while one was open for 0% of the time, Pallas kernels for 18%

profile of v10, /device:TPU:2, one launch (start us, length us, event | category | flops | bytes accessed | tf_op | source)
XLA Modules:
  0.0 20.6 jit_solution(10163094521820845089)
XLA Ops:
  0.0 2.1 %pack.1 = (s16[368,128]{1,0:T(8,128)(2,1)S(1)}, s16[368,128]{1,0:T(8,128)(2,1)S(1)}, s16[368,128]{1,0:T(8,128)(2,1)S(1)}, f32[1088,128]{1,0:T(8,128)S(1)}, s32[2...) custom-call(f32[1080,128]{1,0:T(8,128)} %bitcast.6, ...), custom_call_target="tpu_custom_call" | custom-call | bytes 595304 | tf_op jit(solution)/shard_map/pack/pallas_call | solution.py:291
  2.1 1.6 %collective-permute-start = (s16[368,128]{1,0:T(8,128)(2,1)S(1)}, s16[368,128]{1,0:T(8,128)(2,1)S(1)}, u32[]{:S(2)}, u32[]{:S(2)}) collective-permute-start(s16[368,128]{1,0:T(8,128)(2,1)S(1)} %get-tuple-element.30), channel_id=1, source_target_pairs={{0,24},{1,25},{2,26},{3,27},{4,28},{5,29},{6,30},{7,31},{8,9},{9,1... | collective-permute-start | bytes 282632 | tf_op jit(solution)/shard_map/ppermute | solution.py:321
  3.7 0.0 collective-permute-start.1
  3.7 4.5 %collective-permute-start.2 = (s16[368,128]{1,0:T(8,128)(2,1)S(1)}, s16[368,128]{1,0:T(8,128)(2,1)S(1)}, u32[]{:S(2)}, u32[]{:S(2)}) collective-permute-start(s16[368,128]{1,0:T(8,128)(2,1)S(1)} %get-tuple-element.32), channel_id=1, source_target_pairs={{0,8},{1,9},{2,10},{3,11},{4,12},{5,13},{6,14},{7,15},{8,0},{9,1},... | collective-permute-start | bytes 282632 | tf_op jit(solution)/shard_map/ppermute | solution.py:321
  8.2 2.5 %first.1 = (bf16[768,512]{1,0:T(8,128)(2,1)S(1)}, bf16[768,512]{1,0:T(8,128)(2,1)S(1)}, f32[1,512]{1,0:T(1,128)S(1)}, f32[272,512]{1,0:T(8,128)S(1)}, bf16[512,2...) custom-call(bf16[270,512]{1,0:T(8,128)(2,1)} %bitcast.7, ...), custom_call_target="tpu_custom_call" | custom-call | flops 268435456 | bytes 1491304 | tf_op jit(solution)/shard_map/first/pallas_call | solution.py:291
  10.7 0.0 collective-permute-done.refs_0_
  10.7 0.0 collective-permute-done.1.refs_1_
  10.7 0.0 collective-permute-done.2.refs_2_
  10.7 1.5 %middle.1 = (s16[368,128]{1,0:T(8,128)(2,1)S(1)}, s16[368,128]{1,0:T(8,128)(2,1)S(1)}, s16[368,128]{1,0:T(8,128)(2,1)S(1)}, f32[272,512]{1,0:T(8,128)S(1)}) custom-call(s16[368,128]{1,0:T(8,128)(2,1)S(1)} %collective-permute-done.refs_0_, s16[368,128]{1,0:T(8,128)(2,1)S(1)} %collective-permute-done.1.refs_1_, ...), custom_call_target="tpu_custom_call" | custom-call | flops 268435456 | bytes 4140032 | tf_op jit(solution)/shard_map/middle/pallas_call | solution.py:291
  12.2 0.2 collective-permute-start.3
  12.4 0.5 %collective-permute-start.4 = (s16[368,128]{1,0:T(8,128)(2,1)S(1)}, s16[368,128]{1,0:T(8,128)(2,1)S(1)}, u32[]{:S(2)}, u32[]{:S(2)}) collective-permute-start(s16[368,128]{1,0:T(8,128)(2,1)S(1)} %get-tuple-element.51), channel_id=1, source_target_pairs={{0,16},{1,17},{2,18},{3,19},{4,20},{5,21},{6,22},{7,23},{8,15},{9,... | collective-permute-start | bytes 282632 | tf_op jit(solution)/shard_map/ppermute | solution.py:321
  13.0 4.2 %collective-permute-start.5 = (s16[368,128]{1,0:T(8,128)(2,1)S(1)}, s16[368,128]{1,0:T(8,128)(2,1)S(1)}, u32[]{:S(2)}, u32[]{:S(2)}) collective-permute-start(s16[368,128]{1,0:T(8,128)(2,1)S(1)} %get-tuple-element.52), channel_id=1, source_target_pairs={{0,8},{1,9},{2,10},{3,11},{4,12},{5,13},{6,14},{7,15},{8,0},{9,1},... | collective-permute-start | bytes 282632 | tf_op jit(solution)/shard_map/ppermute | solution.py:321
  17.1 1.2 %own.1.refs_3_ = f32[272,512]{1,0:T(8,128)S(1)} custom-call(f32[1088,128]{1,0:T(8,128)S(1)} %get-tuple-element.34.refs_3_.refs_0_, f32[272,512]{1,0:T(8,128)S(1)} %get-tuple-element.53.refs_1_, bf16[768,512]{1,0:T(8,128)(2,1)S(1)} %get-tuple-element.42.refs_5_.refs_2_.refs_4_, f32[1,512]{1,0:T(1,128)S(1)} %get-tuple-element.54.refs_3_, ...), custom_call_target="tpu_custom_call" | custom-call | flops 268435456 | bytes 3367936 | tf_op jit(solution)/shard_map/own/pallas_call | solution.py:291
  18.3 1.3 %collective-permute-done.3.refs_0_ = s16[368,128]{1,0:T(8,128)(2,1)S(1)} collective-permute-done((s16[368,128]{1,0:T(8,128)(2,1)S(1)}, s16[368,128]{1,0:T(8,128)(2,1)S(1)}, u32[]{:S(2)}, u32[]{:S(2)}) %collective-permute-start.3) | collective-permute-done | bytes 94240 | tf_op jit(solution)/shard_map/ppermute | solution.py:321
  19.6 0.0 collective-permute-done.4.refs_1_
  19.6 0.0 collective-permute-done.5.refs_2_
  19.6 1.0 %last.1 = f32[1080,128]{1,0:T(8,128)} custom-call(s16[368,128]{1,0:T(8,128)(2,1)S(1)} %collective-permute-done.3.refs_0_, s16[368,128]{1,0:T(8,128)(2,1)S(1)} %collective-permute-done.4.refs_1_, s16[368,128]{1,0:T(8,128)(2,1)S(1)} %collective-permute-done.5.refs_2_, f32[272,512]{1,0:T(8,128)S(1)} %own.1.refs_3_, ...), custom_call_target="tpu_custom_call" | custom-call | flops 71303168 | bytes 1626112 | tf_op jit(solution)/shard_map/last/pallas_call | solution.py:291
Async XLA Ops:
  2.1 8.6 %collective-permute-start = (s16[368,128]{1,0:T(8,128)(2,1)S(1)}, s16[368,128]{1,0:T(8,128)(2,1)S(1)}, u32[]{:S(2)}, u32[]{:S(2)}) collective-permute-start(s16[368,128]{1,0:T(8,128)(2,1)S(1)} %get-tuple-element.30), channel_id=1, source_target_pairs={{0,24},{1,25},{2,26},{3,27},{4,28},{5,29},{6,30},{7,31},{8,9},{9,1... | collective-permute-start | bytes 282632 | tf_op jit(solution)/shard_map/ppermute | solution.py:321
  3.7 7.0 %collective-permute-start.1 = (s16[368,128]{1,0:T(8,128)(2,1)S(1)}, s16[368,128]{1,0:T(8,128)(2,1)S(1)}, u32[]{:S(2)}, u32[]{:S(2)}) collective-permute-start(s16[368,128]{1,0:T(8,128)(2,1)S(1)} %get-tuple-element.31), channel_id=1, source_target_pairs={{0,16},{1,17},{2,18},{3,19},{4,20},{5,21},{6,22},{7,23},{8,15},{9,... | collective-permute-start | bytes 282632 | tf_op jit(solution)/shard_map/ppermute | solution.py:321
  3.7 7.0 %collective-permute-start.2 = (s16[368,128]{1,0:T(8,128)(2,1)S(1)}, s16[368,128]{1,0:T(8,128)(2,1)S(1)}, u32[]{:S(2)}, u32[]{:S(2)}) collective-permute-start(s16[368,128]{1,0:T(8,128)(2,1)S(1)} %get-tuple-element.32), channel_id=1, source_target_pairs={{0,8},{1,9},{2,10},{3,11},{4,12},{5,13},{6,14},{7,15},{8,0},{9,1},... | collective-permute-start | bytes 282632 | tf_op jit(solution)/shard_map/ppermute | solution.py:321
  12.2 7.3 %collective-permute-start.3 = (s16[368,128]{1,0:T(8,128)(2,1)S(1)}, s16[368,128]{1,0:T(8,128)(2,1)S(1)}, u32[]{:S(2)}, u32[]{:S(2)}) collective-permute-start(s16[368,128]{1,0:T(8,128)(2,1)S(1)} %get-tuple-element.50), channel_id=1, source_target_pairs={{0,24},{1,25},{2,26},{3,27},{4,28},{5,29},{6,30},{7,31},{8,9},{9,1... | collective-permute-start | bytes 282632 | tf_op jit(solution)/shard_map/ppermute | solution.py:321
  12.4 7.2 %collective-permute-start.4 = (s16[368,128]{1,0:T(8,128)(2,1)S(1)}, s16[368,128]{1,0:T(8,128)(2,1)S(1)}, u32[]{:S(2)}, u32[]{:S(2)}) collective-permute-start(s16[368,128]{1,0:T(8,128)(2,1)S(1)} %get-tuple-element.51), channel_id=1, source_target_pairs={{0,16},{1,17},{2,18},{3,19},{4,20},{5,21},{6,22},{7,23},{8,15},{9,... | collective-permute-start | bytes 282632 | tf_op jit(solution)/shard_map/ppermute | solution.py:321
  13.0 6.6 %collective-permute-start.5 = (s16[368,128]{1,0:T(8,128)(2,1)S(1)}, s16[368,128]{1,0:T(8,128)(2,1)S(1)}, u32[]{:S(2)}, u32[]{:S(2)}) collective-permute-start(s16[368,128]{1,0:T(8,128)(2,1)S(1)} %get-tuple-element.52), channel_id=1, source_target_pairs={{0,8},{1,9},{2,10},{3,11},{4,12},{5,13},{6,14},{7,15},{8,0},{9,1},... | collective-permute-start | bytes 282632 | tf_op jit(solution)/shard_map/ppermute | solution.py:321

commit v11 on v7

--- a/solution.py
+++ b/solution.py
@@ -11,7 +11,7 @@
 heat_gain = 0.5
 bf16, f32, i16 = jnp.bfloat16, jnp.float32, jnp.int16
 
-plan0 = ("UDH", "UHD", "HUD")
+plan0 = ("HUD", "UHD", "UDH")
 plan1 = ("UDH", "UHD", "HUD")
 
 

time: 21.1 us -> 21.4 us (1.014); the launches traced: 20.6 us -> 21.2 us
  waiting for transfers between devices: 1.29 us -> 3.37 us
  starting transfers between devices: 11.2 us -> 9.75 us
    ppermute x6, waiting for transfers between devices: 1.29 us -> 3.37 us  [exchange(): received.append(lax.ppermute(message, ('grp', 'blk'), pairs))]
    ppermute x6, starting transfers between devices: 11.2 us -> 9.75 us  [exchange(): received.append(lax.ppermute(message, ('grp', 'blk'), pairs))]
  transfers between devices with their start and end apart: 6 -> 6, of which waited for: 2 -> 4; matrix products, arithmetic and copies ran while one was open for 0% -> 0% of each run, Pallas kernels for 16% -> 16%
where the time goes in v11:
time: 21.4 us; the launch traced here: 21.2 us
  starting transfers between devices  9.75 us (46%)
  Pallas kernels  8.07 us (38%)
  waiting for transfers between devices  3.37 us (16%)
    ppermute x6, starting transfers between devices, exchange(): received.append(lax.ppermute(message, ('grp', 'blk'), pairs))  9.75 us
    pallas_call x5, Pallas kernels, call(): pl.pallas_call(kernel, out_shape=out_shape, in_specs=[HBM] * hbm + [VMEM]...  8.07 us
    ppermute x6, waiting for transfers between devices, exchange(): received.append(lax.ppermute(message, ('grp', 'blk'), pairs))  3.37 us
  transfers between devices with their start and end apart: 6, of which 4 were waited for; matrix products, arithmetic and copies ran while one was open for 0% of the time, Pallas kernels for 16%

profile of v11, /device:TPU:2, one launch (start us, length us, event | category | flops | bytes accessed | tf_op | source)
XLA Modules:
  0.0 21.2 jit_solution(14484689001239187176)
XLA Ops:
  0.0 2.1 %pack.1 = (s16[368,128]{1,0:T(8,128)(2,1)S(1)}, s16[368,128]{1,0:T(8,128)(2,1)S(1)}, s16[368,128]{1,0:T(8,128)(2,1)S(1)}, f32[1088,128]{1,0:T(8,128)S(1)}, s32[2...) custom-call(f32[1080,128]{1,0:T(8,128)} %bitcast.6, ...), custom_call_target="tpu_custom_call" | custom-call | bytes 595304 | tf_op jit(solution)/shard_map/pack/pallas_call | solution.py:289
  2.1 1.6 %collective-permute-start = (s16[368,128]{1,0:T(8,128)(2,1)S(1)}, s16[368,128]{1,0:T(8,128)(2,1)S(1)}, u32[]{:S(2)}, u32[]{:S(2)}) collective-permute-start(s16[368,128]{1,0:T(8,128)(2,1)S(1)} %get-tuple-element.30), channel_id=1, source_target_pairs={{0,8},{1,9},{2,10},{3,11},{4,12},{5,13},{6,14},{7,15},{8,0},{9,1},... | collective-permute-start | bytes 282632 | tf_op jit(solution)/shard_map/ppermute | solution.py:319
  3.7 0.0 collective-permute-start.1
  3.7 3.4 %collective-permute-start.2 = (s16[368,128]{1,0:T(8,128)(2,1)S(1)}, s16[368,128]{1,0:T(8,128)(2,1)S(1)}, u32[]{:S(2)}, u32[]{:S(2)}) collective-permute-start(s16[368,128]{1,0:T(8,128)(2,1)S(1)} %get-tuple-element.32), channel_id=1, source_target_pairs={{0,24},{1,25},{2,26},{3,27},{4,28},{5,29},{6,30},{7,31},{8,15},{9,... | collective-permute-start | bytes 282632 | tf_op jit(solution)/shard_map/ppermute | solution.py:319
  7.1 2.1 %first.1 = (bf16[768,512]{1,0:T(8,128)(2,1)S(1)}, bf16[768,512]{1,0:T(8,128)(2,1)S(1)}, f32[1,512]{1,0:T(1,128)S(1)}, f32[272,512]{1,0:T(8,128)S(1)}, bf16[512,2...) custom-call(bf16[270,512]{1,0:T(8,128)(2,1)} %bitcast.7, ...), custom_call_target="tpu_custom_call" | custom-call | flops 268435456 | bytes 1491304 | tf_op jit(solution)/shard_map/first/pallas_call | solution.py:289
  9.2 0.3 %collective-permute-done.refs_0_ = s16[368,128]{1,0:T(8,128)(2,1)S(1)} collective-permute-done((s16[368,128]{1,0:T(8,128)(2,1)S(1)}, s16[368,128]{1,0:T(8,128)(2,1)S(1)}, u32[]{:S(2)}, u32[]{:S(2)}) %collective-permute-start) | collective-permute-done | bytes 94240 | tf_op jit(solution)/shard_map/ppermute | solution.py:319
  9.5 0.0 collective-permute-done.1.refs_1_
  9.5 0.7 %collective-permute-done.2.refs_2_ = s16[368,128]{1,0:T(8,128)(2,1)S(1)} collective-permute-done((s16[368,128]{1,0:T(8,128)(2,1)S(1)}, s16[368,128]{1,0:T(8,128)(2,1)S(1)}, u32[]{:S(2)}, u32[]{:S(2)}) %collective-permute-start.2) | collective-permute-done | bytes 94240 | tf_op jit(solution)/shard_map/ppermute | solution.py:319
  10.3 1.5 %middle.1 = (s16[368,128]{1,0:T(8,128)(2,1)S(1)}, s16[368,128]{1,0:T(8,128)(2,1)S(1)}, s16[368,128]{1,0:T(8,128)(2,1)S(1)}, f32[272,512]{1,0:T(8,128)S(1)}) custom-call(s16[368,128]{1,0:T(8,128)(2,1)S(1)} %collective-permute-done.refs_0_, s16[368,128]{1,0:T(8,128)(2,1)S(1)} %collective-permute-done.1.refs_1_, ...), custom_call_target="tpu_custom_call" | custom-call | flops 268435456 | bytes 4140032 | tf_op jit(solution)/shard_map/middle/pallas_call | solution.py:289
  11.8 0.4 %collective-permute-start.3 = (s16[368,128]{1,0:T(8,128)(2,1)S(1)}, s16[368,128]{1,0:T(8,128)(2,1)S(1)}, u32[]{:S(2)}, u32[]{:S(2)}) collective-permute-start(s16[368,128]{1,0:T(8,128)(2,1)S(1)} %get-tuple-element.50), channel_id=1, source_target_pairs={{0,24},{1,25},{2,26},{3,27},{4,28},{5,29},{6,30},{7,31},{8,9},{9,1... | collective-permute-start | bytes 282632 | tf_op jit(solution)/shard_map/ppermute | solution.py:319
  12.3 1.3 %collective-permute-start.4 = (s16[368,128]{1,0:T(8,128)(2,1)S(1)}, s16[368,128]{1,0:T(8,128)(2,1)S(1)}, u32[]{:S(2)}, u32[]{:S(2)}) collective-permute-start(s16[368,128]{1,0:T(8,128)(2,1)S(1)} %get-tuple-element.51), channel_id=1, source_target_pairs={{0,16},{1,17},{2,18},{3,19},{4,20},{5,21},{6,22},{7,23},{8,15},{9,... | collective-permute-start | bytes 282632 | tf_op jit(solution)/shard_map/ppermute | solution.py:319
  13.6 3.0 %collective-permute-start.5 = (s16[368,128]{1,0:T(8,128)(2,1)S(1)}, s16[368,128]{1,0:T(8,128)(2,1)S(1)}, u32[]{:S(2)}, u32[]{:S(2)}) collective-permute-start(s16[368,128]{1,0:T(8,128)(2,1)S(1)} %get-tuple-element.52), channel_id=1, source_target_pairs={{0,8},{1,9},{2,10},{3,11},{4,12},{5,13},{6,14},{7,15},{8,0},{9,1},... | collective-permute-start | bytes 282632 | tf_op jit(solution)/shard_map/ppermute | solution.py:319
  16.6 1.3 %own.1.refs_3_ = f32[272,512]{1,0:T(8,128)S(1)} custom-call(f32[1088,128]{1,0:T(8,128)S(1)} %get-tuple-element.34.refs_3_.refs_0_, f32[272,512]{1,0:T(8,128)S(1)} %get-tuple-element.53.refs_1_, bf16[768,512]{1,0:T(8,128)(2,1)S(1)} %get-tuple-element.42.refs_5_.refs_2_.refs_4_, f32[1,512]{1,0:T(1,128)S(1)} %get-tuple-element.54.refs_3_, ...), custom_call_target="tpu_custom_call" | custom-call | flops 268435456 | bytes 3367936 | tf_op jit(solution)/shard_map/own/pallas_call | solution.py:289
  17.9 1.5 %collective-permute-done.3.refs_0_ = s16[368,128]{1,0:T(8,128)(2,1)S(1)} collective-permute-done((s16[368,128]{1,0:T(8,128)(2,1)S(1)}, s16[368,128]{1,0:T(8,128)(2,1)S(1)}, u32[]{:S(2)}, u32[]{:S(2)}) %collective-permute-start.3) | collective-permute-done | bytes 94240 | tf_op jit(solution)/shard_map/ppermute | solution.py:319
  19.5 0.0 collective-permute-done.4.refs_1_
  19.5 0.7 %collective-permute-done.5.refs_2_ = s16[368,128]{1,0:T(8,128)(2,1)S(1)} collective-permute-done((s16[368,128]{1,0:T(8,128)(2,1)S(1)}, s16[368,128]{1,0:T(8,128)(2,1)S(1)}, u32[]{:S(2)}, u32[]{:S(2)}) %collective-permute-start.5) | collective-permute-done | bytes 94240 | tf_op jit(solution)/shard_map/ppermute | solution.py:319
  20.2 1.0 %last.1 = f32[1080,128]{1,0:T(8,128)} custom-call(s16[368,128]{1,0:T(8,128)(2,1)S(1)} %collective-permute-done.3.refs_0_, s16[368,128]{1,0:T(8,128)(2,1)S(1)} %collective-permute-done.4.refs_1_, s16[368,128]{1,0:T(8,128)(2,1)S(1)} %collective-permute-done.5.refs_2_, f32[272,512]{1,0:T(8,128)S(1)} %own.1.refs_3_, ...), custom_call_target="tpu_custom_call" | custom-call | flops 71303168 | bytes 1626112 | tf_op jit(solution)/shard_map/last/pallas_call | solution.py:289
Async XLA Ops:
  2.1 7.4 %collective-permute-start = (s16[368,128]{1,0:T(8,128)(2,1)S(1)}, s16[368,128]{1,0:T(8,128)(2,1)S(1)}, u32[]{:S(2)}, u32[]{:S(2)}) collective-permute-start(s16[368,128]{1,0:T(8,128)(2,1)S(1)} %get-tuple-element.30), channel_id=1, source_target_pairs={{0,8},{1,9},{2,10},{3,11},{4,12},{5,13},{6,14},{7,15},{8,0},{9,1},... | collective-permute-start | bytes 282632 | tf_op jit(solution)/shard_map/ppermute | solution.py:319
  3.7 5.9 %collective-permute-start.1 = (s16[368,128]{1,0:T(8,128)(2,1)S(1)}, s16[368,128]{1,0:T(8,128)(2,1)S(1)}, u32[]{:S(2)}, u32[]{:S(2)}) collective-permute-start(s16[368,128]{1,0:T(8,128)(2,1)S(1)} %get-tuple-element.31), channel_id=1, source_target_pairs={{0,16},{1,17},{2,18},{3,19},{4,20},{5,21},{6,22},{7,23},{8,9},{9,1... | collective-permute-start | bytes 282632 | tf_op jit(solution)/shard_map/ppermute | solution.py:319
  3.7 6.6 %collective-permute-start.2 = (s16[368,128]{1,0:T(8,128)(2,1)S(1)}, s16[368,128]{1,0:T(8,128)(2,1)S(1)}, u32[]{:S(2)}, u32[]{:S(2)}) collective-permute-start(s16[368,128]{1,0:T(8,128)(2,1)S(1)} %get-tuple-element.32), channel_id=1, source_target_pairs={{0,24},{1,25},{2,26},{3,27},{4,28},{5,29},{6,30},{7,31},{8,15},{9,... | collective-permute-start | bytes 282632 | tf_op jit(solution)/shard_map/ppermute | solution.py:319
  11.8 7.6 %collective-permute-start.3 = (s16[368,128]{1,0:T(8,128)(2,1)S(1)}, s16[368,128]{1,0:T(8,128)(2,1)S(1)}, u32[]{:S(2)}, u32[]{:S(2)}) collective-permute-start(s16[368,128]{1,0:T(8,128)(2,1)S(1)} %get-tuple-element.50), channel_id=1, source_target_pairs={{0,24},{1,25},{2,26},{3,27},{4,28},{5,29},{6,30},{7,31},{8,9},{9,1... | collective-permute-start | bytes 282632 | tf_op jit(solution)/shard_map/ppermute | solution.py:319
  12.3 7.2 %collective-permute-start.4 = (s16[368,128]{1,0:T(8,128)(2,1)S(1)}, s16[368,128]{1,0:T(8,128)(2,1)S(1)}, u32[]{:S(2)}, u32[]{:S(2)}) collective-permute-start(s16[368,128]{1,0:T(8,128)(2,1)S(1)} %get-tuple-element.51), channel_id=1, source_target_pairs={{0,16},{1,17},{2,18},{3,19},{4,20},{5,21},{6,22},{7,23},{8,15},{9,... | collective-permute-start | bytes 282632 | tf_op jit(solution)/shard_map/ppermute | solution.py:319
  13.6 6.6 %collective-permute-start.5 = (s16[368,128]{1,0:T(8,128)(2,1)S(1)}, s16[368,128]{1,0:T(8,128)(2,1)S(1)}, u32[]{:S(2)}, u32[]{:S(2)}) collective-permute-start(s16[368,128]{1,0:T(8,128)(2,1)S(1)} %get-tuple-element.52), channel_id=1, source_target_pairs={{0,8},{1,9},{2,10},{3,11},{4,12},{5,13},{6,14},{7,15},{8,0},{9,1},... | collective-permute-start | bytes 282632 | tf_op jit(solution)/shard_map/ppermute | solution.py:319
